TPU v7x, 256 devices: a whole 4x4x8 slice. The times are simulated.
256 devices in a mesh: rot: 4 (over z_hi), tx: 16 (over x, y), ty: 4 (over z_lo, core).
Axes of the slice: x: 4, y: 4, z: 8 (z_hi: 4, z_lo: 2; z = z_hi * 2 + z_lo), core: 2. Of those that a mesh axis runs over, the one named last changes fastest.
Arguments:
- tomogram: float32 [512, 128, 64], P('tx', 'ty'), may hold values from -60 to 60
- templates: float32 [8, 32, 1024], P('rot'), may hold values from -6 to 6
Outputs:
- top_score: float32 [512, 4096], P('tx', 'ty')
- next_score: float32 [512, 4096], P('tx', 'ty')
All inputs are finite; a program needn't handle non-finite values.
Results may differ from a plain program's by a relative error of at most 0.0003.
Values sent between devices are 32-bit elements; how exact they have to be, the bound alone decides.
No kernel may reach another device: no remote copies, remote signals or barrier semaphores. Data moves between devices by JAX's collectives and lax.ppermute only.
A program may use at most 128 MiB of HBM per device.

v0:
```python
import math

import jax
import jax.numpy as jnp
from jax import lax
from jax.sharding import PartitionSpec as P

RADIUS = 15


PRECISE = lax.Precision.HIGHEST
epsilon = 1e-05
ALONG_Z = "abj,kj->abk"
ALONG_Y = "ajc,kj->akc"
ALONG_X = "jbc,kj->kbc"


def extended(x, sides, width):
    for axis, dim in sides:
        count, length = (lax.axis_size(axis), x.shape[dim])
        up = [(i, (i + 1) % count) for i in range(count - 1)]
        down = [(j, i) for i, j in up]
        last = lax.slice_in_dim(x, length - width, length, axis=dim)
        first = lax.slice_in_dim(x, 0, width, axis=dim)
        before = lax.ppermute(last, axis, up)
        after = lax.ppermute(first, axis, down)
        x = jnp.concatenate([before, x, after], axis=dim)
    return x


def joined(x, axis, combine):
    everything = jax.tree.map(lambda part: lax.all_gather(part, axis), x)
    first = jax.tree.map(lambda part: part[0], everything)

    def lap(k, so_far):
        return combine(so_far, jax.tree.map(lambda part: part[k], everything))

    return lax.fori_loop(1, lax.axis_size(axis), lap, first)


def phase_pair(out_pos, in_pos, length, sign_val):
    products = jnp.remainder(out_pos[:, None] * in_pos[None, :], length)
    phases = sign_val * 2.0 * math.pi / length * products.astype(jnp.float32)
    return (jnp.cos(phases), jnp.sin(phases))


def contract(pattern, operand, phase_tab):
    return jnp.einsum(
        pattern, operand, phase_tab, precision=PRECISE, preferred_element_type=jnp.float32
    )


def turn_axis(real_part, imag_part, tables, pattern):
    cos_tab, sin_tab = tables
    if imag_part is None:
        return (contract(pattern, real_part, cos_tab), contract(pattern, real_part, sin_tab))
    new_real = contract(pattern, real_part, cos_tab) - contract(pattern, imag_part, sin_tab)
    new_imag = contract(pattern, imag_part, cos_tab) + contract(pattern, real_part, sin_tab)
    return (new_real, new_imag)


def positions(length):
    return jnp.arange(length, dtype=jnp.int32)


def forward_grid(real_part, imag_part):
    size_x, size_y, size_z = real_part.shape
    real_part, imag_part = turn_axis(
        real_part,
        imag_part,
        phase_pair(positions(size_z), positions(size_z), size_z, -1.0),
        ALONG_Z,
    )
    real_part, imag_part = turn_axis(
        real_part,
        imag_part,
        phase_pair(positions(size_y), positions(size_y), size_y, -1.0),
        ALONG_Y,
    )
    return turn_axis(
        real_part,
        imag_part,
        phase_pair(positions(size_x), positions(size_x), size_x, -1.0),
        ALONG_X,
    )


def forward_placed(real_part, imag_part, grid_shape, half_edge):
    size_x, size_y, size_z = grid_shape
    placed = half_edge - positions(real_part.shape[0])
    real_part, imag_part = turn_axis(
        real_part, imag_part, phase_pair(positions(size_z), placed, size_z, -1.0), ALONG_Z
    )
    real_part, imag_part = turn_axis(
        real_part, imag_part, phase_pair(positions(size_y), placed, size_y, -1.0), ALONG_Y
    )
    return turn_axis(
        real_part, imag_part, phase_pair(positions(size_x), placed, size_x, -1.0), ALONG_X
    )


def inverse_center(real_part, imag_part, out_shape, half_edge):
    size_x, size_y, size_z = real_part.shape
    keep_x, keep_y, keep_z = out_shape
    real_part, imag_part = turn_axis(
        real_part,
        imag_part,
        phase_pair(half_edge + positions(keep_x), positions(size_x), size_x, 1.0),
        ALONG_X,
    )
    real_part, imag_part = turn_axis(
        real_part,
        imag_part,
        phase_pair(half_edge + positions(keep_y), positions(size_y), size_y, 1.0),
        ALONG_Y,
    )
    real_part, imag_part = turn_axis(
        real_part,
        imag_part,
        phase_pair(half_edge + positions(keep_z), positions(size_z), size_z, 1.0),
        ALONG_Z,
    )
    volume = float(size_x * size_y * size_z)
    return (real_part / volume, imag_part / volume)


def complex_times(left_real, left_imag, right_real, right_imag):
    return (
        left_real * right_real - left_imag * right_imag,
        left_real * right_imag + left_imag * right_real,
    )


def reversed_freq(values):
    return jnp.roll(jnp.flip(values, (0, 1, 2)), 1, (0, 1, 2))


def pair_top(one, other):
    return (
        jnp.maximum(one[0], other[0]),
        jnp.maximum(jnp.minimum(one[0], other[0]), jnp.maximum(one[1], other[1])),
    )


def local(tomogram, templates):
    tile_x, tile_y, depth = tomogram.shape
    rot_count, box_edge, _ = templates.shape
    half_edge = box_edge // 2
    depth_out = depth - box_edge
    ext_grid = extended(tomogram, (("tx", 0), ("ty", 1)), half_edge)
    grid_shape = ext_grid.shape
    out_shape = (tile_x, tile_y, depth_out)
    centred = jnp.arange(box_edge, dtype=jnp.float32) - (box_edge - 1) / 2.0
    radius_sq = (
        centred[:, None, None] ** 2 + centred[None, :, None] ** 2 + centred[None, None, :] ** 2
    )
    sphere_mask = (radius_sq <= float(RADIUS * RADIUS)).astype(jnp.float32)
    filled = jnp.sum(sphere_mask)
    shaped = templates.reshape(rot_count, box_edge, box_edge, box_edge)
    masked_mean = jnp.sum(shaped * sphere_mask, axis=(1, 2, 3), keepdims=True) / filled
    spread = (
        jnp.sum(sphere_mask * (shaped - masked_mean) ** 2, axis=(1, 2, 3), keepdims=True) / filled
    )
    normed = sphere_mask * (shaped - masked_mean) / jnp.sqrt(spread + epsilon)
    spec_real, spec_imag = forward_grid(ext_grid, ext_grid * ext_grid)
    mask_real, mask_imag = forward_placed(sphere_mask, None, grid_shape, half_edge)
    prod_real, prod_imag = complex_times(spec_real, spec_imag, mask_real, mask_imag)
    local_sum, local_sq = inverse_center(prod_real, prod_imag, out_shape, half_edge)
    local_std = jnp.sqrt(local_sq / filled - (local_sum / filled) ** 2 + epsilon)
    divisor = jnp.sqrt(filled) * local_std
    tomo_real = 0.5 * (spec_real + reversed_freq(spec_real))
    tomo_imag = 0.5 * (spec_imag - reversed_freq(spec_imag))
    top_score = None
    next_score = None
    kern_real, kern_imag = forward_placed(normed[0], normed[1], grid_shape, half_edge)
    prod_real, prod_imag = complex_times(tomo_real, tomo_imag, kern_real, kern_imag)
    corr_one, corr_two = inverse_center(prod_real, prod_imag, out_shape, half_edge)
    score_one = corr_one / divisor
    score_two = corr_two / divisor
    top_score = jnp.maximum(score_one, score_two)
    next_score = jnp.minimum(score_one, score_two)
    top_score, next_score = joined((top_score, next_score), "rot", pair_top)
    return (
        top_score.reshape(tile_x, tile_y * depth_out),
        next_score.reshape(tile_x, tile_y * depth_out),
    )


def solution(mesh):
    placed = (P("tx", "ty", None), P("rot", None, None))
    return jax.shard_map(
        local, mesh=mesh, in_specs=placed, out_specs=(P("tx", "ty"), P("tx", "ty")), check_vma=False
    )
```

profile of v0, /device:TPU:7, one launch (start us, length us, event | category | flops | bytes accessed | tf_op | source)
XLA Modules:
  0.0 240.9 jit_solution(14632737373381272627)
XLA Ops:
  0.6 1.8 fusion.479
  2.4 3.2 %collective-permute-start = (f32[16,32,64]{2,1,0:T(8,128)}, f32[16,32,64]{2,1,0:T(8,128)S(1)}, u32[]{:S(2)}, u32[]{:S(2)}) collective-permute-start(f32[16,32,64]{2,1,0:T(8,128)} %get-tuple-element.160), channel_id=1, source_target_pairs={{0,4},{4,8},{8,12},{12,16},{16,20},{20,24},{24,28},{28,32},{32,36}... | collective-permute-start | bytes 393224 | tf_op jit(solution)/shard_map/ppermute | solution.py:25
  5.6 4.2 %collective-permute-start.1 = (f32[16,32,64]{2,1,0:T(8,128)S(1)}, f32[16,32,64]{2,1,0:T(8,128)S(1)}, u32[]{:S(2)}, u32[]{:S(2)}) collective-permute-start(f32[16,32,64]{2,1,0:T(8,128)S(1)} %get-tuple-element.159), channel_id=1, source_target_pairs={{4,0},{8,4},{12,8},{16,12},{20,16},{24,20},{28,24},{32,28},{36,32}... | collective-permute-start | bytes 393224 | tf_op jit(solution)/shard_map/ppermute | solution.py:26
  22.2 2.5 %fusion.65 = f32[64,64,64]{2,0,1:T(8,128)S(1)} fusion(f32[32,64,64]{2,1,0:T(8,128)S(1)} %fusion.28, s32[32]{0:T(128)S(1)} %iota_subtract_fusion), kind=kOutput, calls=%fused_computation.99 | convolution fusion | flops 100691968 | bytes 1572992 | tf_op jit(solution)/shard_map/jbc,kj->kbc/dot_general | solution.py:48
  27.0 1.4 fusion.139
  29.6 2.5 %fusion.53 = f32[64,64,64]{2,0,1:T(8,128)S(1)} fusion(f32[32,64,64]{2,1,0:T(8,128)S(1)} %fusion.26, s32[32]{0:T(128)S(1)} %iota_subtract_fusion), kind=kOutput, calls=%fused_computation.87 | convolution fusion | flops 100691968 | bytes 1572992 | tf_op jit(solution)/shard_map/jbc,kj->kbc/dot_general | solution.py:48
  33.3 2.5 %fusion.57 = f32[64,64,64]{2,0,1:T(8,128)S(1)} fusion(f32[32,64,64]{2,1,0:T(8,128)S(1)} %fusion.27, s32[32]{0:T(128)S(1)} %iota_subtract_fusion), kind=kOutput, calls=%fused_computation.91 | convolution fusion | flops 100691968 | bytes 1572992 | tf_op jit(solution)/shard_map/jbc,kj->kbc/dot_general | solution.py:48
  35.8 3.8 %convolution_subtract_fusion = f32[64,64,64]{2,0,1:T(8,128)} fusion(f32[64,64,64]{2,0,1:T(8,128)S(1)} %fusion.53, f32[32,64,64]{2,1,0:T(8,128)S(1)} %fusion.27, s32[32]{0:T(128)S(1)} %iota_subtract_fusion), kind=kOutput, calls=%fused_computation.36 | convolution fusion | flops 100954112 | bytes 2621568 | tf_op jit(solution)/shard_map/jbc,kj->kbc/dot_general | solution.py:48
  39.6 3.8 %convolution_add_fusion = f32[64,64,64]{2,0,1:T(8,128)} fusion(f32[64,64,64]{2,0,1:T(8,128)S(1)} %fusion.57, f32[32,64,64]{2,1,0:T(8,128)S(1)} %fusion.26, s32[32]{0:T(128)S(1)} %iota_subtract_fusion), kind=kOutput, calls=%fused_computation.37 | convolution fusion | flops 100954112 | bytes 2621568 | tf_op jit(solution)/shard_map/jbc,kj->kbc/dot_general | solution.py:48
  43.5 14.2 %convolution_add_fusion.1 = f32[64,64,64]{2,0,1:T(8,128)} fusion(f32[64,64,64]{2,0,1:T(8,128)S(1)} %fusion.65, f32[32,64,64]{2,1,0:T(8,128)S(1)} %fusion.29, s32[32]{0:T(128)S(1)} %iota_subtract_fusion), kind=kOutput, calls=%fused_computation.38 | convolution fusion | flops 100954112 | bytes 2621568 | tf_op jit(solution)/shard_map/jbc,kj->kbc/dot_general | solution.py:48
  58.5 3.1 %collective-permute-start.3 = (f32[64,16,64]{2,1,0:T(8,128)S(1)}, f32[64,16,64]{2,1,0:T(8,128)S(1)}, u32[]{:S(2)}, u32[]{:S(2)}) collective-permute-start(f32[64,16,64]{2,1,0:T(8,128)S(1)} %get-tuple-element.158), channel_id=1, source_target_pairs={{1,0},{2,1},{3,2},{5,4},{6,5},{7,6},{9,8},{10,9},{11,10},{13,12},{... | collective-permute-start | bytes 786440 | tf_op jit(solution)/shard_map/ppermute | solution.py:26
  61.7 3.4 %collective-permute-start.2 = (f32[64,16,64]{2,1,0:T(8,128)S(1)}, f32[64,16,64]{2,1,0:T(8,128)S(1)}, u32[]{:S(2)}, u32[]{:S(2)}) collective-permute-start(f32[64,16,64]{2,1,0:T(8,128)S(1)} %get-tuple-element.157), channel_id=1, source_target_pairs={{0,1},{1,2},{2,3},{4,5},{5,6},{6,7},{8,9},{9,10},{10,11},{12,13},{... | collective-permute-start | bytes 786440 | tf_op jit(solution)/shard_map/ppermute | solution.py:25
  65.1 3.8 %fusion.69 = f32[64,64,64]{2,0,1:T(8,128)} fusion(f32[32,64,64]{2,1,0:T(8,128)S(1)} %fusion.29, s32[32]{0:T(128)S(1)} %iota_subtract_fusion), kind=kOutput, calls=%fused_computation.103 | convolution fusion | flops 100691968 | bytes 1572992 | tf_op jit(solution)/shard_map/jbc,kj->kbc/dot_general | solution.py:48
  71.3 2.0 fusion.82
  73.3 2.0 fusion.17
  75.3 2.1 fusion.95
  77.4 2.0 fusion.15
  79.4 2.4 convolution_subtract_fusion.2
  81.8 2.1 fusion.99
  83.9 2.1 add_bitcast_fusion
  86.1 3.1 %fusion.5 = f32[64,64,64]{2,0,1:T(8,128)S(1)} fusion(f32[64,64,64]{2,1,0:T(8,128)S(1)} %add_bitcast_fusion), kind=kOutput, calls=%fused_computation.21 | convolution fusion | flops 201383936 | bytes 2097152 | tf_op jit(solution)/shard_map/jbc,kj->kbc/dot_general | solution.py:48
  89.2 2.1 subtract_bitcast_fusion
  91.3 3.4 %fusion.23 = f32[64,64,64]{2,0,1:T(8,128)S(1)} fusion(f32[64,64,64]{2,0,1:T(8,128)S(1)} %fusion.5, f32[64,64,64]{2,1,0:T(8,128)S(1)} %subtract_bitcast_fusion), kind=kOutput, calls=%fused_computation.35 | convolution fusion | flops 201646080 | bytes 3145728 | tf_op jit(solution)/shard_map/jbc,kj->kbc/dot_general | solution.py:48
  94.7 1.6 slice.113
  96.4 3.1 %fusion.7 = f32[64,64,64]{2,0,1:T(8,128)S(1)} fusion(f32[64,64,64]{2,1,0:T(8,128)S(1)} %add_bitcast_fusion), kind=kOutput, calls=%fused_computation.23 | convolution fusion | flops 201383936 | bytes 2097152 | tf_op jit(solution)/shard_map/jbc,kj->kbc/dot_general | solution.py:48
  99.5 3.1 %fusion.20 = f32[64,64,64]{2,0,1:T(8,128)S(1)} fusion(f32[64,64,64]{2,0,1:T(8,128)S(1)} %fusion.7, f32[64,64,64]{2,1,0:T(8,128)S(1)} %subtract_bitcast_fusion), kind=kOutput, calls=%fused_computation.34 | convolution fusion | flops 201646080 | bytes 3145728 | tf_op jit(solution)/shard_map/jbc,kj->kbc/dot_general | solution.py:48
  102.6 1.9 slice.107
  104.7 4.4 %slice.95 = f32[63,64,64]{2,0,1:T(8,128)} reverse(f32[63,64,64]{2,0,1:T(8,128)} %slice.113), dimensions={0,1,2} | reverse | bytes 2064384 | tf_op jit(solution)/shard_map/jit(_roll_static)/slice | solution.py:135
  109.4 1.9 fusion.1
  112.7 1.9 slice.114
  114.6 4.4 %slice.85 = f32[63,64,64]{2,0,1:T(8,128)} reverse(f32[63,64,64]{2,0,1:T(8,128)} %slice.107), dimensions={0,1,2} | reverse | bytes 2064384 | tf_op jit(solution)/shard_map/jit(_roll_static)/slice | solution.py:135
  119.3 2.1 fusion.2
  123.8 6.6 %multiply_add_fusion.1 = (f32[64,64,64]{2,0,1:T(8,128)S(1)}, f32[64,64,64]{2,0,1:T(8,128)S(1)}, f32[64,64,64]{2,0,1:T(8,128)S(1)}, f32[64,64,64]{2,0,1:T(8,128)S(1)}) fusion(f32[64,64,64]{2,0,1:T(8,128)} %convolution_add_fusion.1, f32[64,64,64]{2,0,1:T(8,128)S(1)} %fusion.23, f32[64,64,63]{2,0,1:T(8,128)S(1)} %bitcast.199, f32[64,64,1]{2,0,1:T(8,128)} %slice.114, ...), kind=kOutput, calls=%fused_computation.17 | convolution fusion | flops 105672704 | bytes 13107328 | tf_op jit(solution)/shard_map/jbc,kj->kbc/dot_general | solution.py:48
  134.2 1.3 fusion.51
  136.8 1.3 fusion.47
  138.1 1.3 fusion.31
  140.2 1.3 fusion.30
  142.2 1.5 fusion.41
  147.5 1.3 fusion.59
  151.4 1.3 fusion.32
  153.5 1.3 fusion.33
  155.6 1.7 fusion.46
  158.8 40.0 %all-gather = f32[128,32,32]{2,1,0:T(8,128)S(1)} all-gather(f32[32,32,32]{2,1,0:T(8,128)S(1)} %get-tuple-element.156), channel_id=2, replica_groups=mesh['rot'=4,'tx'=16,'ty'=4] {'rot'}, dimensions={0}, use_global_device_ids=true | all-gather | bytes 655360 | tf_op jit(solution)/shard_map/all_gather | solution.py:32
  198.8 34.3 %all-gather.1 = f32[128,32,32]{2,1,0:T(8,128)S(1)} all-gather(f32[32,32,32]{2,1,0:T(8,128)S(1)} %get-tuple-element.155), channel_id=3, replica_groups=mesh['rot'=4,'tx'=16,'ty'=4] {'rot'}, dimensions={0}, use_global_device_ids=true | all-gather | bytes 655360 | tf_op jit(solution)/shard_map/all_gather | solution.py:32
  234.5 4.5 %while.17 = (s32[]{:T(128)}, f32[32,32,32]{2,1,0:T(8,128)S(1)}, f32[32,32,32]{2,1,0:T(8,128)S(1)}, f32[4,32,32,32]{3,2,1,0:T(8,128)S(1)}, f32[4,32,32,32]{3,2,1,0:T(8,128)}, /*index=5*/s32[]{:T(128)}, s32[]{:T(128)}, s32[]{:T(128)}) while((s32[]{:T(128)}, f32[32,32,32]{2,1,0:T(8,128)S(1)}, f32[32,32,32]{2,1,0:T(8,128)S(1)}, ...), condition=%wide.region_4.5_spmd, body=%wide.region_3.4_spmd.sunk | while | flops 131077 | bytes 786563 | solution.py:38
  234.5 1.5 fusion.509
  235.9 1.5 fusion.509
  237.4 1.5 fusion.509
  (80 shorter events, 42.5 us)
Async XLA Ops:
  0.6 12.2 %copy-start.7 = (f32[2,32,1024]{2,1,0:T(8,128)S(1)}, f32[2,32,1024]{2,1,0:T(8,128)}, u32[]{:S(2)}) copy-start(f32[2,32,1024]{2,1,0:T(8,128)} %param.5) | copy-start | bytes 786436
  2.4 55.9 %collective-permute-start = (f32[16,32,64]{2,1,0:T(8,128)}, f32[16,32,64]{2,1,0:T(8,128)S(1)}, u32[]{:S(2)}, u32[]{:S(2)}) collective-permute-start(f32[16,32,64]{2,1,0:T(8,128)} %get-tuple-element.160), channel_id=1, source_target_pairs={{0,4},{4,8},{8,12},{12,16},{16,20},{20,24},{24,28},{28,32},{32,36}... | collective-permute-start | bytes 393224 | tf_op jit(solution)/shard_map/ppermute | solution.py:25
  5.6 52.8 %collective-permute-start.1 = (f32[16,32,64]{2,1,0:T(8,128)S(1)}, f32[16,32,64]{2,1,0:T(8,128)S(1)}, u32[]{:S(2)}, u32[]{:S(2)}) collective-permute-start(f32[16,32,64]{2,1,0:T(8,128)S(1)} %get-tuple-element.159), channel_id=1, source_target_pairs={{4,0},{8,4},{12,8},{16,12},{20,16},{24,20},{28,24},{32,28},{36,32}... | collective-permute-start | bytes 393224 | tf_op jit(solution)/shard_map/ppermute | solution.py:26
  43.5 14.9 %copy-start.8 = (f32[32,32,64]{2,1,0:T(8,128)S(1)}, f32[32,32,64]{2,1,0:T(8,128)}, u32[]{:S(2)}) copy-start(f32[32,32,64]{2,1,0:T(8,128)} %param.4) | copy-start | bytes 786436
  58.5 11.5 %collective-permute-start.3 = (f32[64,16,64]{2,1,0:T(8,128)S(1)}, f32[64,16,64]{2,1,0:T(8,128)S(1)}, u32[]{:S(2)}, u32[]{:S(2)}) collective-permute-start(f32[64,16,64]{2,1,0:T(8,128)S(1)} %get-tuple-element.158), channel_id=1, source_target_pairs={{1,0},{2,1},{3,2},{5,4},{6,5},{7,6},{9,8},{10,9},{11,10},{13,12},{... | collective-permute-start | bytes 786440 | tf_op jit(solution)/shard_map/ppermute | solution.py:26
  61.7 9.6 %collective-permute-start.2 = (f32[64,16,64]{2,1,0:T(8,128)S(1)}, f32[64,16,64]{2,1,0:T(8,128)S(1)}, u32[]{:S(2)}, u32[]{:S(2)}) collective-permute-start(f32[64,16,64]{2,1,0:T(8,128)S(1)} %get-tuple-element.157), channel_id=1, source_target_pairs={{0,1},{1,2},{2,3},{4,5},{5,6},{6,7},{8,9},{9,10},{10,11},{12,13},{... | collective-permute-start | bytes 786440 | tf_op jit(solution)/shard_map/ppermute | solution.py:25
  102.6 2.0 copy-start
  111.3 1.3 copy-start.2
  119.3 2.7 %copy-start.5 = (f32[64,64,64]{2,0,1:T(8,128)S(1)}, f32[64,64,64]{2,0,1:T(8,128)}, u32[]{:S(2)}) copy-start(f32[64,64,64]{2,0,1:T(8,128)} %convolution_subtract_fusion) | copy-start | bytes 3145732
  119.3 2.9 %copy-start.6 = (f32[64,64,64]{2,0,1:T(8,128)S(1)}, f32[64,64,64]{2,0,1:T(8,128)}, u32[]{:S(2)}) copy-start(f32[64,64,64]{2,0,1:T(8,128)} %convolution_add_fusion) | copy-start | bytes 3145732
  121.4 1.8 copy-start.1
  121.4 2.4 copy-start.3
  233.1 1.3 copy-start.4
where the time goes:
time: 245 us; the launch traced here: 241 us
  matrix products  111 us (45%)
  blocking collectives  74.3 us (30%)
  local copies, waits for them, and re-layouts  25.6 us (10%)
  starting transfers between devices  14 us (6%)
  other arithmetic  11.5 us (5%)
    dot_general x58, matrix products, contract(): jnp.einsum(pattern, operand, phase_tab, precision=PRECISE, preferred_elem...  111 us
    all_gather x2, blocking collectives, joined(): everything = jax.tree.map(lambda part: lax.all_gather(part, axis), x)  74.3 us
    slice x10, local copies, waits for them, and re-layouts, reversed_freq(): return jnp.roll(jnp.flip(values, (0, 1, 2)), 1, (0, 1, 2))  15.5 us
    ppermute x2, starting transfers between devices, extended(): after = lax.ppermute(first, axis, down)  7.33 us
    ppermute x2, starting transfers between devices, extended(): before = lax.ppermute(last, axis, up)  6.63 us
  transfers between devices with their start and end apart: 4, of which 2 were waited for; matrix products, arithmetic and copies ran while one was open for 21% of the time, Pallas kernels for 0%

commit v1 on v0

v1 whole, which is shorter than its diff:
```python
import functools

import jax
import jax.numpy as jnp
import ml_dtypes
import numpy as np
from jax import lax
from jax.experimental import pallas as pl
from jax.experimental.pallas import tpu as pltpu
from jax.sharding import PartitionSpec as P

RADIUS = 15
EPSILON = 1e-05
GRID = 64
BOX = 32
HALF = 16
LANES = 128
SETS = 4
F32 = jnp.float32
BF16 = jnp.bfloat16


def halves(table):
    hi = table.astype(ml_dtypes.bfloat16)
    lo = (table - hi.astype(np.float64)).astype(ml_dtypes.bfloat16)
    return hi, lo


def wave(out_pos, in_pos):
    angle = 2.0 * np.pi / GRID * np.outer(out_pos, in_pos)
    return np.cos(angle), np.sin(angle)


def left_table(blocks):
    parts = []
    for block in blocks:
        hi, lo = halves(block)
        parts += [hi, hi, lo]
    return np.concatenate(parts, axis=1)


def sphere_np():
    centred = np.arange(BOX) - (BOX - 1) / 2.0
    sq = centred[:, None, None] ** 2 + centred[None, :, None] ** 2 + centred[None, None, :] ** 2
    return (sq <= float(RADIUS * RADIUS)).astype(np.float64)


@functools.cache
def tables():
    freq = np.arange(GRID)
    cos_f, sin_f = wave(freq, np.arange(GRID))
    forward = left_table([np.concatenate([cos_f, sin_f], axis=0)])
    cos_t, sin_t = wave(freq, np.arange(BOX))
    kernel = left_table([cos_t, sin_t])

    def inverse(shift):
        cos_i, sin_i = wave(np.arange(BOX) + shift, freq)
        return left_table([np.concatenate([cos_i, sin_i], axis=0) / GRID])

    cz, sz = cos_f.T, sin_f.T
    zero = np.zeros((GRID, LANES))
    plain = np.concatenate([cz, -sz], axis=1)
    turned = np.concatenate([sz, cz], axis=1)
    tomo_z = np.block([[plain, zero, plain, zero], [zero, plain, zero, plain], [zero, zero, turned, zero], [zero, zero, zero, turned]])
    ct, st = cos_t.T, sin_t.T
    one = np.concatenate([ct, st], axis=1)
    two = np.concatenate([-st, ct], axis=1)
    kern_z = np.concatenate([np.kron(np.eye(4), one), np.kron(np.eye(4), two)], axis=0)

    def inverse_z(shift):
        cos_i, sin_i = wave(freq, np.arange(BOX) + shift)
        real = np.concatenate([cos_i, -sin_i], axis=0) / GRID
        imag = np.concatenate([sin_i, cos_i], axis=0) / GRID
        return np.concatenate([np.kron(np.eye(4), real), np.kron(np.eye(4), imag)], axis=1)

    centre = (BOX - 1) / 2.0
    sphere = sphere_np()
    cos_m, _ = wave(freq, np.arange(BOX) - centre)
    sin_m = wave(freq, np.arange(BOX) - centre)[1]
    spec = sphere.astype(np.complex128)
    for axis in range(3):
        spec = np.moveaxis(np.tensordot(cos_m + 1j * sin_m, spec, axes=(1, axis)), 0, axis)
    real = np.transpose(spec.real, (1, 0, 2))
    mask_spec = np.concatenate([real, real], axis=2).astype(np.float32)
    mask = sphere.reshape(BOX, BOX * BOX).astype(np.float32)
    return (
        mask,
        mask_spec,
        *halves(tomo_z),
        *halves(kern_z),
        forward,
        kernel,
        inverse(0.0),
        inverse(centre),
        *halves(inverse_z(0.0)),
        *halves(inverse_z(centre)),
    )


def split(x):
    hi = x.astype(BF16)
    return hi, (x - hi.astype(F32)).astype(BF16)


def dot(a, b):
    return jnp.dot(a, b, preferred_element_type=F32)


def swapped(x):
    return pltpu.roll(x, GRID, 1)


def column(x):
    hi, lo = split(x)
    return jnp.concatenate([hi, lo, hi], axis=0)


def right_dot(x, w_hi, w_lo):
    hi, lo = split(x)
    return dot(hi, w_hi) + dot(lo, w_hi) + dot(hi, w_lo)


def body(
    own_ref, before_ref, after_ref, t_own_ref, t_far_ref, t_core_ref,
    mask_ref, mask_spec_ref, tz_hi, tz_lo, kz_hi, kz_lo, fwd_ref, ker_ref, inv_ref, inv_m_ref,
    iz_hi, iz_lo, im_hi, im_lo,
    top_ref, next_ref,
    fz, fy, kz, ky, vx, vy,
):
    filled = float(sphere_np().sum())
    lane = lax.broadcasted_iota(jnp.int32, (1, LANES), 1)
    plus_first = jnp.where(lane < GRID, 1.0, -1.0).astype(F32)
    first = lane < GRID

    mask = mask_ref[...]

    def normed(t):
        mu = jnp.sum(jnp.sum(t * mask, axis=0, keepdims=True), axis=1, keepdims=True) / filled
        d = (t - mu) * mask
        v = jnp.sum(jnp.sum(d * d, axis=0, keepdims=True), axis=1, keepdims=True) / filled
        return d / jnp.sqrt(v + EPSILON)

    pairs = [(t_own_ref[0], t_own_ref[1])] + [(t_far_ref[s], t_core_ref[s]) for s in range(3)]
    for p in range(SETS):
        a, b = normed(pairs[p][0]), normed(pairs[p][1])
        rows = [
            jnp.concatenate([a[:, LANES * g : LANES * (g + 1)], b[:, LANES * g : LANES * (g + 1)]], axis=1)
            for g in range(8)
        ]
        out = right_dot(jnp.concatenate(rows, axis=0), kz_hi[...], kz_lo[...])
        for g in range(8):
            for jj in range(4):
                j = 4 * g + jj
                kz[p, BOX * j : BOX * (j + 1), :] = out[BOX * g : BOX * (g + 1), LANES * jj : LANES * (jj + 1)]

    def two(x):
        return jnp.concatenate([column(x), column(swapped(x) * -plus_first)], axis=0)

    @pl.loop(0, BOX, step=2)
    def _(i):
        for p in range(SETS):
            rhs = [two(kz[p, pl.ds(i + e, BOX, stride=BOX), :]) for e in range(2)]
            out = dot(ker_ref[...], jnp.concatenate(rhs, axis=1))
            for e in range(2):
                ky[p, pl.ds(pl.multiple_of((i + e) * GRID, GRID), GRID), :] = out[:, LANES * e : LANES * (e + 1)]

    @pl.loop(0, BOX, step=4)
    def _(x):
        mid = own_ref[pl.ds(x, 4)].reshape(4 * BOX, LANES)
        low = before_ref[pl.ds(x, 4)].reshape(4 * HALF, LANES)
        high = after_ref[pl.ds(x, 4)].reshape(4 * HALF, LANES)
        rows = jnp.concatenate([mid, low, high], axis=0)
        out = right_dot(jnp.concatenate([rows, rows * rows], axis=1), tz_hi[...], tz_lo[...])
        for c in range(4):
            col = out[:, LANES * c : LANES * (c + 1)]
            for e in range(4):
                base = pl.multiple_of((x + e + BOX * (c % 2)) * GRID, GRID)
                fz[c // 2, pl.ds(base + HALF, BOX), :] = col[BOX * e : BOX * (e + 1)]
                fz[c // 2, pl.ds(base, HALF), :] = col[128 + HALF * e : 128 + HALF * (e + 1)]
                fz[c // 2, pl.ds(base + HALF + BOX, HALF), :] = col[192 + HALF * e : 192 + HALF * (e + 1)]

    def forward(a, b):
        out = dot(fwd_ref[...], jnp.concatenate([column(a), column(b)], axis=1))
        res = []
        for e in range(2):
            o = out[:, LANES * e : LANES * (e + 1)]
            res.append(o[:GRID] + swapped(o[GRID:]) * plus_first)
        return res

    def inverse(a, b, table):
        out = dot(table, jnp.concatenate([column(a), column(b)], axis=1))
        res = []
        for e in range(2):
            o = out[:, LANES * e : LANES * (e + 1)]
            res.append(o[:BOX] - swapped(o[BOX:]) * plus_first)
        return res

    @pl.loop(0, GRID, step=2)
    def _(x):
        for c in range(2):
            at = [pl.ds(pl.multiple_of((x + e) * GRID, GRID), GRID) for e in range(2)]
            res = forward(fz[c, at[0], :], fz[c, at[1], :])
            for e in range(2):
                fy[c, at[e], :] = res[e]

    @pl.loop(0, GRID, step=2)
    def _(k):
        spec = forward(*[fy[0, pl.ds(k + e, GRID, stride=GRID), :] for e in range(2)])
        same, cross = [], []
        for s in spec:
            r = swapped(s)
            same.append(jnp.where(first, s, r))
            cross.append(jnp.where(first, -r, s))
        for p in range(SETS):
            rhs = [two(ky[p, pl.ds(k + e, BOX, stride=GRID), :]) for e in range(2)]
            t = dot(ker_ref[...], jnp.concatenate(rhs, axis=1))
            prod = []
            for e in range(2):
                te = t[:, LANES * e : LANES * (e + 1)]
                prod.append(te * same[e] + swapped(te) * cross[e])
            res = inverse(prod[0], prod[1], inv_ref[...])
            for e in range(2):
                vx[p, pl.ds(pl.multiple_of((k + e) * BOX, BOX), BOX), :] = res[e]
        both = forward(*[fy[1, pl.ds(k + e, GRID, stride=GRID), :] for e in range(2)])
        res = inverse(both[0] * mask_spec_ref[k], both[1] * mask_spec_ref[k + 1], inv_m_ref[...])
        for e in range(2):
            vx[SETS, pl.ds(pl.multiple_of((k + e) * BOX, BOX), BOX), :] = res[e]

    @pl.loop(0, BOX, step=2)
    def _(x):
        for p in range(SETS + 1):
            cols = [vx[p, pl.ds(x + e, GRID, stride=BOX), :] for e in range(2)]
            res = inverse(cols[0], cols[1], inv_ref[...] if p < SETS else inv_m_ref[...])
            for e in range(2):
                vy[p, pl.ds(pl.multiple_of((x + e) * BOX, BOX), BOX), :] = res[e]

    def last(p, w_hi, w_lo):
        rows = []
        for g in range(8):
            rows.append(
                jnp.concatenate([vy[p, pl.ds(4 * g + yy, BOX, stride=BOX), :] for yy in range(4)], axis=1)
            )
        out = right_dot(jnp.concatenate(rows, axis=0), w_hi, w_lo)
        return out[:, :LANES], out[:, LANES:]

    total, square = last(SETS, im_hi[...], im_lo[...])
    mean = total / filled
    var = jnp.maximum(square / filled - mean * mean, 0.0)
    scale = 1.0 / (np.float32(np.sqrt(filled)) * jnp.sqrt(var + EPSILON))
    top, second = None, None
    for p in range(SETS):
        one, other = last(p, iz_hi[...], iz_lo[...])
        one, other = one * scale, other * scale
        high, low = jnp.maximum(one, other), jnp.minimum(one, other)
        if top is None:
            top, second = high, low
        else:
            second = jnp.maximum(jnp.minimum(top, high), jnp.maximum(second, low))
            top = jnp.maximum(top, high)
    for g in range(8):
        top_ref[:, LANES * g : LANES * (g + 1)] = top[BOX * g : BOX * (g + 1)]
        next_ref[:, LANES * g : LANES * (g + 1)] = second[BOX * g : BOX * (g + 1)]


def shifts(count, step):
    return [(i, i + step) for i in range(count) if 0 <= i + step < count]


def local(tomogram, templates):
    tx, ty, rots = lax.axis_size("tx"), lax.axis_size("ty"), lax.axis_size("rot")

    def pack(part):
        return jnp.concatenate([part[:, :HALF], part[:, HALF:]], axis=2)

    def unpack(part):
        return jnp.concatenate([part[:, :, :GRID], part[:, :, GRID:]], axis=1)

    before = lax.ppermute(pack(tomogram[HALF:]), "tx", shifts(tx, 1))
    after = lax.ppermute(pack(tomogram[:HALF]), "tx", shifts(tx, -1))

    core = lax.rem(lax.axis_index("ty"), 2)
    mine = lax.dynamic_slice_in_dim(templates, core, 1, axis=0)
    far = [lax.ppermute(mine, "rot", [(i, (i + s) % rots) for i in range(rots)]) for s in range(1, rots)]
    far = jnp.concatenate(far, axis=0)
    core_far = lax.ppermute(far, "ty", [(i, i + 1 - 2 * (i % 2)) for i in range(ty)])

    grid = jnp.concatenate(
        [
            jnp.concatenate([unpack(before), tomogram[:HALF]], axis=0),
            jnp.concatenate([tomogram[HALF:], unpack(after)], axis=0),
        ],
        axis=2,
    )
    low = lax.ppermute(grid[:, HALF:], "ty", shifts(ty, 1))
    high = lax.ppermute(grid[:, :HALF], "ty", shifts(ty, -1))

    out = jax.ShapeDtypeStruct((BOX, BOX * BOX), F32)
    scratch = [
        pltpu.VMEM((2, GRID * GRID, LANES), F32),
        pltpu.VMEM((2, GRID * GRID, LANES), F32),
        pltpu.VMEM((SETS, BOX * BOX, LANES), F32),
        pltpu.VMEM((SETS, BOX * GRID, LANES), F32),
        pltpu.VMEM((SETS + 1, BOX * GRID, LANES), F32),
        pltpu.VMEM((SETS + 1, BOX * BOX, LANES), F32),
    ]
    return pl.pallas_call(
        body,
        out_shape=(out, out),
        scratch_shapes=scratch,
        compiler_params=pltpu.CompilerParams(vmem_limit_bytes=56 * 1024 * 1024),
        cost_estimate=pl.CostEstimate(flops=10**10, bytes_accessed=10**7, transcendentals=0),
        name="scores",
    )(grid, low, high, templates, far, core_far, *[jnp.asarray(t) for t in tables()])


def solution(mesh):
    placed = (P("tx", "ty", None), P("rot", None, None))
    return jax.shard_map(
        local, mesh=mesh, in_specs=placed, out_specs=(P("tx", "ty"), P("tx", "ty")), check_vma=False
    )
```

time: 245 us -> 94.4 us (0.39); the launches traced: 241 us -> 94.2 us
  matrix products: 111 us -> 0 us
  blocking collectives: 74.3 us -> 0 us
  Pallas kernels: 0 us -> 52.9 us
  local copies, waits for them, and re-layouts: 25.6 us -> 3.83 us
  starting transfers between devices: 14 us -> 25.4 us
  other arithmetic: 11.5 us -> 0.41 us
  waiting for transfers between devices: 2.3 us -> 10.8 us
    dot_general x58 -> x0, matrix products: 111 us -> none  [contract(): jnp.einsum(pattern, operand, phase_tab, precision=PRECISE, preferred_elem...]
    all_gather x2 -> x0, blocking collectives: 74.3 us -> none  [joined(): everything = jax.tree.map(lambda part: lax.all_gather(part, axis), x)]
    pallas_call x0 -> x1, Pallas kernels: none -> 52.9 us  [local(): pl.pallas_call(body, out_shape=(out, out), scratch_shapes=scratch, compil...]
    slice x14 -> x5, local copies, waits for them, and re-layouts: 17.5 us -> 1.39 us  [the longest x1 1.13 us: pack(): return jnp.concatenate([part[:, :HALF], part[:, HALF:]], axis=2)]
    ppermute x4 -> x8, starting transfers between devices: 14 us -> 25.4 us  [the longest x3 10.6 us: local(): lax.ppermute(mine, 'rot', [(i, (i + s) % rots) for i in range(rots)])]
    ppermute x4 -> x8, waiting for transfers between devices: 2.3 us -> 10.8 us  [the longest x1 4.39 us: local(): high = lax.ppermute(grid[:, :HALF], 'ty', shifts(ty, -1))]
    max x3 -> x0, other arithmetic: 4.42 us -> none  [pair_top(): jnp.maximum(jnp.minimum(one[0], other[0]), jnp.maximum(one[1], other[1]))]
    concatenate x2 -> x3, other arithmetic: 4.02 us -> 0.41 us  [the longest x1 0.21 us: local(): jnp.concatenate([jnp.concatenate([unpack(before), tomogram[:HALF]], axis=...]
  transfers between devices with their start and end apart: 4 -> 8, of which waited for: 2 -> 4; matrix products, arithmetic and copies ran while one was open for 21% -> 2% of each run, Pallas kernels for 0% -> 0%
where the time goes in v1:
time: 94.4 us; the launch traced here: 94.2 us
  Pallas kernels  52.9 us (56%)
  starting transfers between devices  25.4 us (27%)
  waiting for transfers between devices  10.8 us (11%)
  local copies, waits for them, and re-layouts  3.83 us (4%)
    pallas_call x1, Pallas kernels, local(): pl.pallas_call(body, out_shape=(out, out), scratch_shapes=scratch, compil...  52.9 us
    ppermute x3, starting transfers between devices, local(): lax.ppermute(mine, 'rot', [(i, (i + s) % rots) for i in range(rots)])  10.6 us
    ppermute x1, starting transfers between devices, local(): low = lax.ppermute(grid[:, HALF:], 'ty', shifts(ty, 1))  5.48 us
    ppermute x1, starting transfers between devices, local(): after = lax.ppermute(pack(tomogram[:HALF]), 'tx', shifts(tx, -1))  4.91 us
    ppermute x1, waiting for transfers between devices, local(): high = lax.ppermute(grid[:, :HALF], 'ty', shifts(ty, -1))  4.39 us
    ppermute x1, waiting for transfers between devices, local(): before = lax.ppermute(pack(tomogram[HALF:]), 'tx', shifts(tx, 1))  2.83 us
    ppermute x3, waiting for transfers between devices, local(): lax.ppermute(mine, 'rot', [(i, (i + s) % rots) for i in range(rots)])  2.25 us
    ppermute x1, starting transfers between devices, local(): before = lax.ppermute(pack(tomogram[HALF:]), 'tx', shifts(tx, 1))  1.92 us
  transfers between devices with their start and end apart: 8, of which 4 were waited for; matrix products, arithmetic and copies ran while one was open for 2% of the time, Pallas kernels for 0%

profile of v1, /device:TPU:7, one launch (start us, length us, event | category | flops | bytes accessed | tf_op | source)
XLA Modules:
  0.0 94.2 jit_solution(3960083711347594889)
XLA Ops:
  0.6 0.0 copy-start.1
  0.6 1.0 %constant_dynamic-slice_fusion = f32[1,32,1024]{2,1,0:T(8,128)S(1)} fusion(f32[2,32,1024]{2,1,0:T(8,128)} %t_own_ref.1, s32[]{:T(128)S(6)} %select_n.3), kind=kLoop, calls=%fused_computation.6 | loop fusion | bytes 262148 | tf_op jit(solution)/shard_map/dynamic_slice | solution.py:282
  1.6 3.1 %collective-permute-start.4 = (f32[1,32,1024]{2,1,0:T(8,128)S(1)}, f32[1,32,1024]{2,1,0:T(8,128)S(1)}, u32[]{:S(2)}, u32[]{:S(2)}) collective-permute-start(f32[1,32,1024]{2,1,0:T(8,128)S(1)} %constant_dynamic-slice_fusion), channel_id=1, source_target_pairs={{0,64},{64,128},{128,192},{192,0},{1,65},{65,129},{129,193},{193,1... | collective-permute-start | bytes 393224 | tf_op jit(solution)/shard_map/ppermute | solution.py:283
  4.7 5.1 %collective-permute-start.5 = (f32[1,32,1024]{2,1,0:T(8,128)S(1)}, f32[1,32,1024]{2,1,0:T(8,128)S(1)}, u32[]{:S(2)}, u32[]{:S(2)}) collective-permute-start(f32[1,32,1024]{2,1,0:T(8,128)S(1)} %constant_dynamic-slice_fusion), channel_id=1, source_target_pairs={{0,128},{64,192},{128,0},{192,64},{1,129},{65,193},{129,1},{193,65... | collective-permute-start | bytes 393224 | tf_op jit(solution)/shard_map/ppermute | solution.py:283
  9.8 2.4 %collective-permute-start.6 = (f32[1,32,1024]{2,1,0:T(8,128)S(1)}, f32[1,32,1024]{2,1,0:T(8,128)S(1)}, u32[]{:S(2)}, u32[]{:S(2)}) collective-permute-start(f32[1,32,1024]{2,1,0:T(8,128)S(1)} %constant_dynamic-slice_fusion), channel_id=1, source_target_pairs={{0,192},{64,0},{128,64},{192,128},{1,193},{65,1},{129,65},{193,129... | collective-permute-start | bytes 393224 | tf_op jit(solution)/shard_map/ppermute | solution.py:283
  12.2 1.1 %fusion.1 = (f32[16,16,64]{2,1,0:T(8,128)S(1)}, f32[16,16,64]{2,1,0:T(8,128)S(1)}, f32[16,16,64]{2,1,0:T(8,128)S(1)}, f32[16,16,64]{2,1,0:T(8,128)S(1)}) fusion(f32[32,32,64]{2,1,0:T(8,128)} %param.16), kind=kLoop, calls=%fused_computation.8 | loop fusion | bytes 524288 | tf_op jit(solution)/shard_map/slice | solution.py:273
  13.3 0.1 pad_maximum_fusion.1
  13.4 4.9 %collective-permute-start.1 = (f32[16,16,128]{2,1,0:T(8,128)S(1)}, f32[16,16,128]{2,1,0:T(8,128)S(1)}, u32[]{:S(2)}, u32[]{:S(2)}) collective-permute-start(f32[16,16,128]{2,1,0:T(8,128)S(1)} %pad_maximum_fusion.1), channel_id=1, source_target_pairs={{4,0},{8,4},{12,8},{16,12},{20,16},{24,20},{28,24},{32,28},{36,32}... | collective-permute-start | bytes 393224 | tf_op jit(solution)/shard_map/ppermute | solution.py:279
  18.3 0.1 pad_maximum_fusion
  18.5 1.9 %collective-permute-start = (f32[16,16,128]{2,1,0:T(8,128)S(1)}, f32[16,16,128]{2,1,0:T(8,128)S(1)}, u32[]{:S(2)}, u32[]{:S(2)}) collective-permute-start(f32[16,16,128]{2,1,0:T(8,128)S(1)} %pad_maximum_fusion), channel_id=1, source_target_pairs={{0,4},{4,8},{8,12},{12,16},{16,20},{20,24},{24,28},{28,32},{32,36}... | collective-permute-start | bytes 393224 | tf_op jit(solution)/shard_map/ppermute | solution.py:278
  20.4 0.0 copy-done.1
  20.4 0.0 collective-permute-done.4
  20.5 0.0 collective-permute-done.5
  20.5 2.2 %collective-permute-done.6 = f32[1,32,1024]{2,1,0:T(8,128)S(1)} collective-permute-done((f32[1,32,1024]{2,1,0:T(8,128)S(1)}, f32[1,32,1024]{2,1,0:T(8,128)S(1)}, u32[]{:S(2)}, u32[]{:S(2)}) %collective-permute-start.6) | collective-permute-done | bytes 131104 | tf_op jit(solution)/shard_map/ppermute | solution.py:283
  22.8 0.0 copy-start.2
  22.8 0.6 collective-permute-start.7
  23.3 0.0 collective-permute-done.1
  23.3 0.1 fusion.4
  23.4 2.8 %collective-permute-done = f32[16,16,128]{2,1,0:T(8,128)S(1)} collective-permute-done((f32[16,16,128]{2,1,0:T(8,128)S(1)}, f32[16,16,128]{2,1,0:T(8,128)S(1)}, u32[]{:S(2)}, u32[]{:S(2)}) %collective-permute-start) | collective-permute-done | bytes 131104 | tf_op jit(solution)/shard_map/ppermute | solution.py:278
  26.3 0.1 fusion.3
  26.4 0.2 maximum_maximum_fusion.own_ref
  26.6 0.0 copy-start
  26.6 5.5 %collective-permute-start.2 = (f32[32,16,128]{2,1,0:T(8,128)S(1)}, f32[32,16,128]{2,1,0:T(8,128)S(1)}, u32[]{:S(2)}, u32[]{:S(2)}) collective-permute-start(f32[32,16,128]{2,1,0:T(8,128)S(1)} %get-tuple-element.3), channel_id=1, source_target_pairs={{0,1},{1,2},{2,3},{4,5},{5,6},{6,7},{8,9},{9,10},{10,11},{12,13},{... | collective-permute-start | bytes 786440 | tf_op jit(solution)/shard_map/ppermute | solution.py:294
  32.1 1.9 %collective-permute-start.3 = (f32[32,16,128]{2,1,0:T(8,128)S(1)}, f32[32,16,128]{2,1,0:T(8,128)S(1)}, u32[]{:S(2)}, u32[]{:S(2)}) collective-permute-start(f32[32,16,128]{2,1,0:T(8,128)S(1)} %get-tuple-element.2), channel_id=1, source_target_pairs={{1,0},{2,1},{3,2},{5,4},{6,5},{7,6},{9,8},{10,9},{11,10},{13,12},{... | collective-permute-start | bytes 786440 | tf_op jit(solution)/shard_map/ppermute | solution.py:295
  34.1 1.4 %collective-permute-done.2.before_ref = f32[32,16,128]{2,1,0:T(8,128)S(1)} collective-permute-done((f32[32,16,128]{2,1,0:T(8,128)S(1)}, f32[32,16,128]{2,1,0:T(8,128)S(1)}, u32[]{:S(2)}, u32[]{:S(2)}) %collective-permute-start.2) | collective-permute-done | bytes 262176 | tf_op jit(solution)/shard_map/ppermute | solution.py:294
  35.4 0.0 copy-start.4
  35.4 4.4 %collective-permute-done.3.after_ref = f32[32,16,128]{2,1,0:T(8,128)S(1)} collective-permute-done((f32[32,16,128]{2,1,0:T(8,128)S(1)}, f32[32,16,128]{2,1,0:T(8,128)S(1)}, u32[]{:S(2)}, u32[]{:S(2)}) %collective-permute-start.3) | collective-permute-done | bytes 262176 | tf_op jit(solution)/shard_map/ppermute | solution.py:295
  39.8 0.0 copy-start.5
  39.8 0.0 collective-permute-done.7.t_core_ref
  39.8 0.0 copy-done.2
  39.8 0.0 copy-done
  39.8 0.0 copy-done.4
  39.8 0.7 copy-done.5
  40.5 0.0 copy-start.3
  40.5 0.8 copy-done.3
  41.3 52.9 %scores.1 = (f32[32,1024]{1,0:T(8,128)}, f32[32,1024]{1,0:T(8,128)}) custom-call(f32[32,32,128]{2,1,0:T(8,128)} %copy-done, f32[32,16,128]{2,1,0:T(8,128)} %copy-done.4, f32[32,16,128]{2,1,0:T(8,128)} %copy-done.5, f32[2,32,1024]{2,1,0:T(8,128)} %t_own_ref.1, f32[3,32,1024]{2,1,0:T(8,128)} %copy-done.2, f32[3,32,1024]{2,1,0:T(8,128)} %copy-done.3, ...), custom_call_target="tpu_custom_call" | custom-call | flops 10000000000 | bytes 10000000 | tf_op jit(solution)/shard_map/scores/pallas_call | solution.py:306
  (5 shorter events, 0.1 us)
Async XLA Ops:
  0.6 19.8 %copy-start.1 = (f32[32,32,64]{2,1,0:T(8,128)S(1)}, f32[32,32,64]{2,1,0:T(8,128)}, u32[]{:S(2)}) copy-start(f32[32,32,64]{2,1,0:T(8,128)} %param.16) | copy-start | bytes 786436
  1.6 18.8 %collective-permute-start.4 = (f32[1,32,1024]{2,1,0:T(8,128)S(1)}, f32[1,32,1024]{2,1,0:T(8,128)S(1)}, u32[]{:S(2)}, u32[]{:S(2)}) collective-permute-start(f32[1,32,1024]{2,1,0:T(8,128)S(1)} %constant_dynamic-slice_fusion), channel_id=1, source_target_pairs={{0,64},{64,128},{128,192},{192,0},{1,65},{65,129},{129,193},{193,1... | collective-permute-start | bytes 393224 | tf_op jit(solution)/shard_map/ppermute | solution.py:283
  4.7 15.8 %collective-permute-start.5 = (f32[1,32,1024]{2,1,0:T(8,128)S(1)}, f32[1,32,1024]{2,1,0:T(8,128)S(1)}, u32[]{:S(2)}, u32[]{:S(2)}) collective-permute-start(f32[1,32,1024]{2,1,0:T(8,128)S(1)} %constant_dynamic-slice_fusion), channel_id=1, source_target_pairs={{0,128},{64,192},{128,0},{192,64},{1,129},{65,193},{129,1},{193,65... | collective-permute-start | bytes 393224 | tf_op jit(solution)/shard_map/ppermute | solution.py:283
  9.8 12.9 %collective-permute-start.6 = (f32[1,32,1024]{2,1,0:T(8,128)S(1)}, f32[1,32,1024]{2,1,0:T(8,128)S(1)}, u32[]{:S(2)}, u32[]{:S(2)}) collective-permute-start(f32[1,32,1024]{2,1,0:T(8,128)S(1)} %constant_dynamic-slice_fusion), channel_id=1, source_target_pairs={{0,192},{64,0},{128,64},{192,128},{1,193},{65,1},{129,65},{193,129... | collective-permute-start | bytes 393224 | tf_op jit(solution)/shard_map/ppermute | solution.py:283
  13.4 9.9 %collective-permute-start.1 = (f32[16,16,128]{2,1,0:T(8,128)S(1)}, f32[16,16,128]{2,1,0:T(8,128)S(1)}, u32[]{:S(2)}, u32[]{:S(2)}) collective-permute-start(f32[16,16,128]{2,1,0:T(8,128)S(1)} %pad_maximum_fusion.1), channel_id=1, source_target_pairs={{4,0},{8,4},{12,8},{16,12},{20,16},{24,20},{28,24},{32,28},{36,32}... | collective-permute-start | bytes 393224 | tf_op jit(solution)/shard_map/ppermute | solution.py:279
  18.5 7.8 %collective-permute-start = (f32[16,16,128]{2,1,0:T(8,128)S(1)}, f32[16,16,128]{2,1,0:T(8,128)S(1)}, u32[]{:S(2)}, u32[]{:S(2)}) collective-permute-start(f32[16,16,128]{2,1,0:T(8,128)S(1)} %pad_maximum_fusion), channel_id=1, source_target_pairs={{0,4},{4,8},{8,12},{12,16},{16,20},{20,24},{24,28},{28,32},{32,36}... | collective-permute-start | bytes 393224 | tf_op jit(solution)/shard_map/ppermute | solution.py:278
  22.8 17.1 %copy-start.2 = (f32[3,32,1024]{2,1,0:T(8,128)}, f32[3,32,1024]{2,1,0:T(8,128)S(1)}, u32[]{:S(2)}) copy-start(f32[3,32,1024]{2,1,0:T(8,128)S(1)} %constant_dynamic-update-slice_fusion.t_far_ref) | copy-start | bytes 1179652
  22.8 17.1 %collective-permute-start.7 = (f32[3,32,1024]{2,1,0:T(8,128)S(1)}, f32[3,32,1024]{2,1,0:T(8,128)S(1)}, u32[]{:S(2)}, u32[]{:S(2)}) collective-permute-start(f32[3,32,1024]{2,1,0:T(8,128)S(1)} %constant_dynamic-update-slice_fusion.t_far_ref), channel_id=1, source_target_pairs={{0,1},{1,0},{2,3},{3,2},{4,5},{5,4},{6,7},{7,6},{8,9},{9,8},{10,11... | collective-permute-start | bytes 1179656 | tf_op jit(solution)/shard_map/ppermute | solution.py:285
  26.6 13.2 %copy-start = (f32[32,32,128]{2,1,0:T(8,128)}, f32[32,32,128]{2,1,0:T(8,128)S(1)}, u32[]{:S(2)}) copy-start(f32[32,32,128]{2,1,0:T(8,128)S(1)} %maximum_maximum_fusion.own_ref) | copy-start | bytes 1572868
  26.6 8.8 %collective-permute-start.2 = (f32[32,16,128]{2,1,0:T(8,128)S(1)}, f32[32,16,128]{2,1,0:T(8,128)S(1)}, u32[]{:S(2)}, u32[]{:S(2)}) collective-permute-start(f32[32,16,128]{2,1,0:T(8,128)S(1)} %get-tuple-element.3), channel_id=1, source_target_pairs={{0,1},{1,2},{2,3},{4,5},{5,6},{6,7},{8,9},{9,10},{10,11},{12,13},{... | collective-permute-start | bytes 786440 | tf_op jit(solution)/shard_map/ppermute | solution.py:294
  32.1 7.7 %collective-permute-start.3 = (f32[32,16,128]{2,1,0:T(8,128)S(1)}, f32[32,16,128]{2,1,0:T(8,128)S(1)}, u32[]{:S(2)}, u32[]{:S(2)}) collective-permute-start(f32[32,16,128]{2,1,0:T(8,128)S(1)} %get-tuple-element.2), channel_id=1, source_target_pairs={{1,0},{2,1},{3,2},{5,4},{6,5},{7,6},{9,8},{10,9},{11,10},{13,12},{... | collective-permute-start | bytes 786440 | tf_op jit(solution)/shard_map/ppermute | solution.py:295
  35.4 4.4 %copy-start.4 = (f32[32,16,128]{2,1,0:T(8,128)}, f32[32,16,128]{2,1,0:T(8,128)S(1)}, u32[]{:S(2)}) copy-start(f32[32,16,128]{2,1,0:T(8,128)S(1)} %collective-permute-done.2.before_ref) | copy-start | bytes 786436
  39.8 0.7 copy-start.5
  40.5 0.8 copy-start.3

commit v2 on v1

--- a/solution.py
+++ b/solution.py
@@ -156,7 +156,7 @@
     def two(x):
         return jnp.concatenate([column(x), column(swapped(x) * -plus_first)], axis=0)
 
-    @pl.loop(0, BOX, step=2)
+    @pl.loop(0, BOX, step=2, unroll=8)
     def _(i):
         for p in range(SETS):
             rhs = [two(kz[p, pl.ds(i + e, BOX, stride=BOX), :]) for e in range(2)]
@@ -195,7 +195,7 @@
             res.append(o[:BOX] - swapped(o[BOX:]) * plus_first)
         return res
 
-    @pl.loop(0, GRID, step=2)
+    @pl.loop(0, GRID, step=2, unroll=8)
     def _(x):
         for c in range(2):
             at = [pl.ds(pl.multiple_of((x + e) * GRID, GRID), GRID) for e in range(2)]
@@ -203,7 +203,7 @@
             for e in range(2):
                 fy[c, at[e], :] = res[e]
 
-    @pl.loop(0, GRID, step=2)
+    @pl.loop(0, GRID, step=2, unroll=8)
     def _(k):
         spec = forward(*[fy[0, pl.ds(k + e, GRID, stride=GRID), :] for e in range(2)])
         same, cross = [], []
@@ -226,7 +226,7 @@
         for e in range(2):
             vx[SETS, pl.ds(pl.multiple_of((k + e) * BOX, BOX), BOX), :] = res[e]
 
-    @pl.loop(0, BOX, step=2)
+    @pl.loop(0, BOX, step=2, unroll=8)
     def _(x):
         for p in range(SETS + 1):
             cols = [vx[p, pl.ds(x + e, GRID, stride=BOX), :] for e in range(2)]
@@ -294,6 +294,10 @@
     low = lax.ppermute(grid[:, HALF:], "ty", shifts(ty, 1))
     high = lax.ppermute(grid[:, :HALF], "ty", shifts(ty, -1))
 
+    return kernel_call(grid, low, high, templates, far, core_far)
+
+
+def kernel_call(grid, low, high, templates, far, core_far):
     out = jax.ShapeDtypeStruct((BOX, BOX * BOX), F32)
     scratch = [
         pltpu.VMEM((2, GRID * GRID, LANES), F32),

time: 94.4 us -> 74.7 us (0.79)
  Pallas kernels: 52.9 us -> 33.2 us
    pallas_call x1, Pallas kernels: 52.9 us -> 33.2 us  [kernel_call(): pl.pallas_call(body, out_shape=(out, out), scratch_shapes=scratch, compil...]
where the time goes in v2:
time: 74.7 us; the launch traced here: 74.5 us
  Pallas kernels  33.2 us (44%)
  starting transfers between devices  25.5 us (34%)
  waiting for transfers between devices  10.7 us (14%)
  local copies, waits for them, and re-layouts  3.83 us (5%)
  between operations  0.82 us (1%)
    pallas_call x1, Pallas kernels, kernel_call(): pl.pallas_call(body, out_shape=(out, out), scratch_shapes=scratch, compil...  33.2 us
    ppermute x3, starting transfers between devices, local(): lax.ppermute(mine, 'rot', [(i, (i + s) % rots) for i in range(rots)])  10.6 us
    ppermute x1, starting transfers between devices, local(): low = lax.ppermute(grid[:, HALF:], 'ty', shifts(ty, 1))  5.48 us
    ppermute x1, starting transfers between devices, local(): after = lax.ppermute(pack(tomogram[:HALF]), 'tx', shifts(tx, -1))  4.91 us
    ppermute x1, waiting for transfers between devices, local(): high = lax.ppermute(grid[:, :HALF], 'ty', shifts(ty, -1))  4.39 us
    ppermute x1, waiting for transfers between devices, local(): before = lax.ppermute(pack(tomogram[HALF:]), 'tx', shifts(tx, 1))  2.83 us
    ppermute x3, waiting for transfers between devices, local(): lax.ppermute(mine, 'rot', [(i, (i + s) % rots) for i in range(rots)])  2.25 us
    ppermute x1, starting transfers between devices, local(): high = lax.ppermute(grid[:, :HALF], 'ty', shifts(ty, -1))  2.1 us
  transfers between devices with their start and end apart: 8, of which 4 were waited for; matrix products, arithmetic and copies ran while one was open for 2% of the time, Pallas kernels for 0%

profile of v2, /device:TPU:7, one launch (start us, length us, event | category | flops | bytes accessed | tf_op | source)
XLA Modules:
  0.0 74.5 jit_solution(7531736320474432502)
XLA Ops:
  0.6 0.0 copy-start.1
  0.6 1.0 %constant_dynamic-slice_fusion = f32[1,32,1024]{2,1,0:T(8,128)S(1)} fusion(f32[2,32,1024]{2,1,0:T(8,128)} %t_own_ref.1, s32[]{:T(128)S(6)} %select_n.3), kind=kLoop, calls=%fused_computation.6 | loop fusion | bytes 262148 | tf_op jit(solution)/shard_map/dynamic_slice | solution.py:282
  1.6 3.1 %collective-permute-start.4 = (f32[1,32,1024]{2,1,0:T(8,128)S(1)}, f32[1,32,1024]{2,1,0:T(8,128)S(1)}, u32[]{:S(2)}, u32[]{:S(2)}) collective-permute-start(f32[1,32,1024]{2,1,0:T(8,128)S(1)} %constant_dynamic-slice_fusion), channel_id=1, source_target_pairs={{0,64},{64,128},{128,192},{192,0},{1,65},{65,129},{129,193},{193,1... | collective-permute-start | bytes 393224 | tf_op jit(solution)/shard_map/ppermute | solution.py:283
  4.7 5.1 %collective-permute-start.5 = (f32[1,32,1024]{2,1,0:T(8,128)S(1)}, f32[1,32,1024]{2,1,0:T(8,128)S(1)}, u32[]{:S(2)}, u32[]{:S(2)}) collective-permute-start(f32[1,32,1024]{2,1,0:T(8,128)S(1)} %constant_dynamic-slice_fusion), channel_id=1, source_target_pairs={{0,128},{64,192},{128,0},{192,64},{1,129},{65,193},{129,1},{193,65... | collective-permute-start | bytes 393224 | tf_op jit(solution)/shard_map/ppermute | solution.py:283
  9.8 2.4 %collective-permute-start.6 = (f32[1,32,1024]{2,1,0:T(8,128)S(1)}, f32[1,32,1024]{2,1,0:T(8,128)S(1)}, u32[]{:S(2)}, u32[]{:S(2)}) collective-permute-start(f32[1,32,1024]{2,1,0:T(8,128)S(1)} %constant_dynamic-slice_fusion), channel_id=1, source_target_pairs={{0,192},{64,0},{128,64},{192,128},{1,193},{65,1},{129,65},{193,129... | collective-permute-start | bytes 393224 | tf_op jit(solution)/shard_map/ppermute | solution.py:283
  12.2 1.1 %fusion.1 = (f32[16,16,64]{2,1,0:T(8,128)S(1)}, f32[16,16,64]{2,1,0:T(8,128)S(1)}, f32[16,16,64]{2,1,0:T(8,128)S(1)}, f32[16,16,64]{2,1,0:T(8,128)S(1)}) fusion(f32[32,32,64]{2,1,0:T(8,128)} %param.16), kind=kLoop, calls=%fused_computation.8 | loop fusion | bytes 524288 | tf_op jit(solution)/shard_map/slice | solution.py:273
  13.3 0.1 pad_maximum_fusion.1
  13.4 4.9 %collective-permute-start.1 = (f32[16,16,128]{2,1,0:T(8,128)S(1)}, f32[16,16,128]{2,1,0:T(8,128)S(1)}, u32[]{:S(2)}, u32[]{:S(2)}) collective-permute-start(f32[16,16,128]{2,1,0:T(8,128)S(1)} %pad_maximum_fusion.1), channel_id=1, source_target_pairs={{4,0},{8,4},{12,8},{16,12},{20,16},{24,20},{28,24},{32,28},{36,32}... | collective-permute-start | bytes 393224 | tf_op jit(solution)/shard_map/ppermute | solution.py:279
  18.3 0.1 pad_maximum_fusion
  18.5 1.9 %collective-permute-start = (f32[16,16,128]{2,1,0:T(8,128)S(1)}, f32[16,16,128]{2,1,0:T(8,128)S(1)}, u32[]{:S(2)}, u32[]{:S(2)}) collective-permute-start(f32[16,16,128]{2,1,0:T(8,128)S(1)} %pad_maximum_fusion), channel_id=1, source_target_pairs={{0,4},{4,8},{8,12},{12,16},{16,20},{20,24},{24,28},{28,32},{32,36}... | collective-permute-start | bytes 393224 | tf_op jit(solution)/shard_map/ppermute | solution.py:278
  20.4 0.0 copy-done.1
  20.4 0.0 collective-permute-done.4
  20.5 0.0 collective-permute-done.5
  20.5 2.2 %collective-permute-done.6 = f32[1,32,1024]{2,1,0:T(8,128)S(1)} collective-permute-done((f32[1,32,1024]{2,1,0:T(8,128)S(1)}, f32[1,32,1024]{2,1,0:T(8,128)S(1)}, u32[]{:S(2)}, u32[]{:S(2)}) %collective-permute-start.6) | collective-permute-done | bytes 131104 | tf_op jit(solution)/shard_map/ppermute | solution.py:283
  22.8 0.0 copy-start.2
  22.8 0.6 collective-permute-start.7
  23.3 0.0 collective-permute-done.1
  23.3 0.1 fusion.4
  23.4 2.8 %collective-permute-done = f32[16,16,128]{2,1,0:T(8,128)S(1)} collective-permute-done((f32[16,16,128]{2,1,0:T(8,128)S(1)}, f32[16,16,128]{2,1,0:T(8,128)S(1)}, u32[]{:S(2)}, u32[]{:S(2)}) %collective-permute-start) | collective-permute-done | bytes 131104 | tf_op jit(solution)/shard_map/ppermute | solution.py:278
  26.3 0.1 fusion.3
  26.4 0.2 maximum_maximum_fusion.own_ref
  26.6 0.0 copy-start
  26.6 5.5 %collective-permute-start.2 = (f32[32,16,128]{2,1,0:T(8,128)S(1)}, f32[32,16,128]{2,1,0:T(8,128)S(1)}, u32[]{:S(2)}, u32[]{:S(2)}) collective-permute-start(f32[32,16,128]{2,1,0:T(8,128)S(1)} %get-tuple-element.3), channel_id=1, source_target_pairs={{0,1},{1,2},{2,3},{4,5},{5,6},{6,7},{8,9},{9,10},{10,11},{12,13},{... | collective-permute-start | bytes 786440 | tf_op jit(solution)/shard_map/ppermute | solution.py:294
  32.1 2.1 %collective-permute-start.3 = (f32[32,16,128]{2,1,0:T(8,128)S(1)}, f32[32,16,128]{2,1,0:T(8,128)S(1)}, u32[]{:S(2)}, u32[]{:S(2)}) collective-permute-start(f32[32,16,128]{2,1,0:T(8,128)S(1)} %get-tuple-element.2), channel_id=1, source_target_pairs={{1,0},{2,1},{3,2},{5,4},{6,5},{7,6},{9,8},{10,9},{11,10},{13,12},{... | collective-permute-start | bytes 786440 | tf_op jit(solution)/shard_map/ppermute | solution.py:295
  34.2 1.2 %collective-permute-done.2.before_ref = f32[32,16,128]{2,1,0:T(8,128)S(1)} collective-permute-done((f32[32,16,128]{2,1,0:T(8,128)S(1)}, f32[32,16,128]{2,1,0:T(8,128)S(1)}, u32[]{:S(2)}, u32[]{:S(2)}) %collective-permute-start.2) | collective-permute-done | bytes 262176 | tf_op jit(solution)/shard_map/ppermute | solution.py:294
  35.4 0.0 copy-start.4
  35.4 4.4 %collective-permute-done.3.after_ref = f32[32,16,128]{2,1,0:T(8,128)S(1)} collective-permute-done((f32[32,16,128]{2,1,0:T(8,128)S(1)}, f32[32,16,128]{2,1,0:T(8,128)S(1)}, u32[]{:S(2)}, u32[]{:S(2)}) %collective-permute-start.3) | collective-permute-done | bytes 262176 | tf_op jit(solution)/shard_map/ppermute | solution.py:295
  39.8 0.0 copy-start.5
  39.8 0.0 collective-permute-done.7.t_core_ref
  39.8 0.0 copy-done.2
  39.8 0.0 copy-done
  39.8 0.0 copy-done.4
  39.8 0.7 copy-done.5
  40.5 0.0 copy-start.3
  40.5 0.8 %copy-done.3 = f32[3,32,1024]{2,1,0:T(8,128)} copy-done((f32[3,32,1024]{2,1,0:T(8,128)}, f32[3,32,1024]{2,1,0:T(8,128)S(1)}, u32[]{:S(2)}) %copy-start.3) | copy-done | bytes 393240
  41.3 33.2 %scores.1 = (f32[32,1024]{1,0:T(8,128)}, f32[32,1024]{1,0:T(8,128)}) custom-call(f32[32,32,128]{2,1,0:T(8,128)} %copy-done, f32[32,16,128]{2,1,0:T(8,128)} %copy-done.4, f32[32,16,128]{2,1,0:T(8,128)} %copy-done.5, f32[2,32,1024]{2,1,0:T(8,128)} %t_own_ref.1, f32[3,32,1024]{2,1,0:T(8,128)} %copy-done.2, f32[3,32,1024]{2,1,0:T(8,128)} %copy-done.3, ...), custom_call_target="tpu_custom_call" | custom-call | flops 10000000000 | bytes 10000000 | tf_op jit(solution)/shard_map/scores/pallas_call | solution.py:310
  (5 shorter events, 0.1 us)
Async XLA Ops:
  0.6 19.8 %copy-start.1 = (f32[32,32,64]{2,1,0:T(8,128)S(1)}, f32[32,32,64]{2,1,0:T(8,128)}, u32[]{:S(2)}) copy-start(f32[32,32,64]{2,1,0:T(8,128)} %param.16) | copy-start | bytes 786436
  1.6 18.8 %collective-permute-start.4 = (f32[1,32,1024]{2,1,0:T(8,128)S(1)}, f32[1,32,1024]{2,1,0:T(8,128)S(1)}, u32[]{:S(2)}, u32[]{:S(2)}) collective-permute-start(f32[1,32,1024]{2,1,0:T(8,128)S(1)} %constant_dynamic-slice_fusion), channel_id=1, source_target_pairs={{0,64},{64,128},{128,192},{192,0},{1,65},{65,129},{129,193},{193,1... | collective-permute-start | bytes 393224 | tf_op jit(solution)/shard_map/ppermute | solution.py:283
  4.7 15.8 %collective-permute-start.5 = (f32[1,32,1024]{2,1,0:T(8,128)S(1)}, f32[1,32,1024]{2,1,0:T(8,128)S(1)}, u32[]{:S(2)}, u32[]{:S(2)}) collective-permute-start(f32[1,32,1024]{2,1,0:T(8,128)S(1)} %constant_dynamic-slice_fusion), channel_id=1, source_target_pairs={{0,128},{64,192},{128,0},{192,64},{1,129},{65,193},{129,1},{193,65... | collective-permute-start | bytes 393224 | tf_op jit(solution)/shard_map/ppermute | solution.py:283
  9.8 12.9 %collective-permute-start.6 = (f32[1,32,1024]{2,1,0:T(8,128)S(1)}, f32[1,32,1024]{2,1,0:T(8,128)S(1)}, u32[]{:S(2)}, u32[]{:S(2)}) collective-permute-start(f32[1,32,1024]{2,1,0:T(8,128)S(1)} %constant_dynamic-slice_fusion), channel_id=1, source_target_pairs={{0,192},{64,0},{128,64},{192,128},{1,193},{65,1},{129,65},{193,129... | collective-permute-start | bytes 393224 | tf_op jit(solution)/shard_map/ppermute | solution.py:283
  13.4 9.9 %collective-permute-start.1 = (f32[16,16,128]{2,1,0:T(8,128)S(1)}, f32[16,16,128]{2,1,0:T(8,128)S(1)}, u32[]{:S(2)}, u32[]{:S(2)}) collective-permute-start(f32[16,16,128]{2,1,0:T(8,128)S(1)} %pad_maximum_fusion.1), channel_id=1, source_target_pairs={{4,0},{8,4},{12,8},{16,12},{20,16},{24,20},{28,24},{32,28},{36,32}... | collective-permute-start | bytes 393224 | tf_op jit(solution)/shard_map/ppermute | solution.py:279
  18.5 7.8 %collective-permute-start = (f32[16,16,128]{2,1,0:T(8,128)S(1)}, f32[16,16,128]{2,1,0:T(8,128)S(1)}, u32[]{:S(2)}, u32[]{:S(2)}) collective-permute-start(f32[16,16,128]{2,1,0:T(8,128)S(1)} %pad_maximum_fusion), channel_id=1, source_target_pairs={{0,4},{4,8},{8,12},{12,16},{16,20},{20,24},{24,28},{28,32},{32,36}... | collective-permute-start | bytes 393224 | tf_op jit(solution)/shard_map/ppermute | solution.py:278
  22.8 17.1 %copy-start.2 = (f32[3,32,1024]{2,1,0:T(8,128)}, f32[3,32,1024]{2,1,0:T(8,128)S(1)}, u32[]{:S(2)}) copy-start(f32[3,32,1024]{2,1,0:T(8,128)S(1)} %constant_dynamic-update-slice_fusion.t_far_ref) | copy-start | bytes 1179652
  22.8 17.1 %collective-permute-start.7 = (f32[3,32,1024]{2,1,0:T(8,128)S(1)}, f32[3,32,1024]{2,1,0:T(8,128)S(1)}, u32[]{:S(2)}, u32[]{:S(2)}) collective-permute-start(f32[3,32,1024]{2,1,0:T(8,128)S(1)} %constant_dynamic-update-slice_fusion.t_far_ref), channel_id=1, source_target_pairs={{0,1},{1,0},{2,3},{3,2},{4,5},{5,4},{6,7},{7,6},{8,9},{9,8},{10,11... | collective-permute-start | bytes 1179656 | tf_op jit(solution)/shard_map/ppermute | solution.py:285
  26.6 13.2 %copy-start = (f32[32,32,128]{2,1,0:T(8,128)}, f32[32,32,128]{2,1,0:T(8,128)S(1)}, u32[]{:S(2)}) copy-start(f32[32,32,128]{2,1,0:T(8,128)S(1)} %maximum_maximum_fusion.own_ref) | copy-start | bytes 1572868
  26.6 8.8 %collective-permute-start.2 = (f32[32,16,128]{2,1,0:T(8,128)S(1)}, f32[32,16,128]{2,1,0:T(8,128)S(1)}, u32[]{:S(2)}, u32[]{:S(2)}) collective-permute-start(f32[32,16,128]{2,1,0:T(8,128)S(1)} %get-tuple-element.3), channel_id=1, source_target_pairs={{0,1},{1,2},{2,3},{4,5},{5,6},{6,7},{8,9},{9,10},{10,11},{12,13},{... | collective-permute-start | bytes 786440 | tf_op jit(solution)/shard_map/ppermute | solution.py:294
  32.1 7.7 %collective-permute-start.3 = (f32[32,16,128]{2,1,0:T(8,128)S(1)}, f32[32,16,128]{2,1,0:T(8,128)S(1)}, u32[]{:S(2)}, u32[]{:S(2)}) collective-permute-start(f32[32,16,128]{2,1,0:T(8,128)S(1)} %get-tuple-element.2), channel_id=1, source_target_pairs={{1,0},{2,1},{3,2},{5,4},{6,5},{7,6},{9,8},{10,9},{11,10},{13,12},{... | collective-permute-start | bytes 786440 | tf_op jit(solution)/shard_map/ppermute | solution.py:295
  35.4 4.4 %copy-start.4 = (f32[32,16,128]{2,1,0:T(8,128)}, f32[32,16,128]{2,1,0:T(8,128)S(1)}, u32[]{:S(2)}) copy-start(f32[32,16,128]{2,1,0:T(8,128)S(1)} %collective-permute-done.2.before_ref) | copy-start | bytes 786436
  39.8 0.7 copy-start.5
  40.5 0.8 %copy-start.3 = (f32[3,32,1024]{2,1,0:T(8,128)}, f32[3,32,1024]{2,1,0:T(8,128)S(1)}, u32[]{:S(2)}) copy-start(f32[3,32,1024]{2,1,0:T(8,128)S(1)} %collective-permute-done.7.t_core_ref) | copy-start | bytes 1179652

commit v3 on v1

v3 whole, which is shorter than its diff:
```python
import functools
import math

import jax
import jax.numpy as jnp
import ml_dtypes
import numpy as np
from jax import lax
from jax.experimental import pallas as pl
from jax.experimental.pallas import tpu as pltpu
from jax.sharding import PartitionSpec as P

RADIUS = 15
EPSILON = 1e-05
GRID = 64
BOX = 32
HALF = 16
LANES = 128
F32 = jnp.float32
BF16 = jnp.bfloat16


def halves(table):
    hi = table.astype(ml_dtypes.bfloat16)
    lo = (table - hi.astype(np.float64)).astype(ml_dtypes.bfloat16)
    return hi, lo


def wave(out_pos, in_pos):
    angle = 2.0 * np.pi / GRID * np.outer(out_pos, in_pos)
    return np.cos(angle), np.sin(angle)


def left_table(out_pos, in_pos, scale):
    cos, sin = wave(out_pos, in_pos)
    hi, lo = halves(np.concatenate([cos, sin], axis=0) * scale)
    return np.concatenate([hi, hi, lo], axis=1)


def sphere_np():
    centred = np.arange(BOX) - (BOX - 1) / 2.0
    sq = centred[:, None, None] ** 2 + centred[None, :, None] ** 2 + centred[None, None, :] ** 2
    return (sq <= float(RADIUS * RADIUS)).astype(np.float64)


def block(rows, cols, parts):
    some = next(iter(parts.values()))
    full = np.zeros((rows, cols) + some.shape)
    for at, part in parts.items():
        full[at] = part
    return full.transpose(0, 2, 1, 3).reshape(rows * some.shape[0], cols * some.shape[1])


@functools.cache
def tables():
    freq = np.arange(GRID)
    odd = np.arange(BOX) + 0.5
    centre = (BOX - 1) / 2.0
    cz, sz = wave(np.arange(GRID), odd)
    tomo = {}
    for kind in range(2):
        for side in range(2):
            for dup in range(2):
                tomo[2 * kind + side, 8 * side + 2 * dup + kind] = cz
                tomo[2 * kind + side, 8 * side + 4 + 2 * dup + kind] = -sz
    tomo_z = block(4, 16, tomo)
    ct, st = wave(np.arange(BOX), odd)
    kern = {}
    for rot in range(4):
        for jj in range(2):
            kern[2 * rot + jj, 8 * jj + rot] = ct
            kern[2 * rot + jj, 8 * jj + 4 + rot] = st
    kern_z = block(8, 16, kern)
    ci, si = wave(odd, np.arange(BOX))
    cm, sm = wave(odd, np.arange(BOX) + centre)
    back, back_mask = {}, {}
    for vol in range(4):
        back[vol, vol] = ci / BOX
        back[4 + vol, vol] = -si / BOX
    for vol in range(2):
        for copy in range(4):
            back_mask[vol, 4 * vol + copy] = cm / BOX
            back_mask[4 + vol, 4 * vol + copy] = -sm / BOX
    back_hi, back_lo = halves(block(8, 4, back))
    back_mask_z = block(8, 8, back_mask)
    sphere = sphere_np()
    shifted = np.arange(BOX) - centre
    cx, sx = wave(freq, shifted)
    cy, sy = wave(freq, np.arange(BOX))
    co, so = wave(odd, shifted)
    spec = np.einsum("ai,bj,ck,ijk->bac", cx + 1j * sx, cy + 1j * sy, co + 1j * so, sphere, optimize=True)
    mask_re = np.tile(spec.real, (1, 1, 4)).astype(np.float32)
    mask_im = np.tile(spec.imag, (1, 1, 4)).astype(np.float32)
    mask = sphere.reshape(BOX, BOX * BOX).astype(np.float32)
    scale = 1.0 / (GRID * GRID)
    return (
        mask,
        mask_re,
        mask_im,
        *halves(tomo_z),
        *halves(kern_z),
        left_table(freq, np.arange(GRID), 1.0),
        left_table(freq, np.arange(BOX), 1.0),
        left_table(np.arange(BOX), freq, scale),
        left_table(np.arange(BOX) + centre, freq, scale),
        np.concatenate([back_hi, back_lo], axis=1),
        back_hi,
        *halves(back_mask_z),
    )


def split(x):
    hi = x.astype(BF16)
    return hi, (x - hi.astype(F32)).astype(BF16)


def dot(a, b):
    return jnp.dot(a, b, preferred_element_type=F32)


def right_dot(x, w_hi, w_lo):
    hi, lo = split(x)
    return dot(hi, w_hi) + dot(lo, w_hi) + dot(hi, w_lo)


def left_dot(table, x, sign):
    hi, lo = split(x)
    out = dot(table, jnp.concatenate([hi, lo, hi], axis=0))
    n = out.shape[0] // 2
    tr, ti, br, bi = out[:n, :LANES], out[:n, LANES:], out[n:, :LANES], out[n:, LANES:]
    if sign > 0:
        return tr - bi, ti + br
    return tr + bi, ti - br


def add(a, b):
    return a[0] + b[0], a[1] + b[1]


def sub(a, b):
    return a[0] - b[0], a[1] - b[1]


def turn(a, sign):
    return (-a[1], a[0]) if sign > 0 else (a[1], -a[0])


def add_turned(a, b, sign):
    return (a[0] - b[1], a[1] + b[0]) if sign > 0 else (a[0] + b[1], a[1] - b[0])


def twiddle(a, num, den):
    num = num % den
    if num == 0:
        return a
    c, s = math.cos(2 * math.pi * num / den), math.sin(2 * math.pi * num / den)
    if 4 * num % den == 0:
        quarter = 4 * num // den
        return [a, turn(a, 1), (-a[0], -a[1]), turn(a, -1)][quarter]
    if 8 * num % den == 0:
        h = math.sqrt(0.5)
        odd = 8 * num // den
        if odd == 1:
            return (a[0] - a[1]) * h, (a[0] + a[1]) * h
        if odd == 3:
            return (a[0] + a[1]) * -h, (a[0] - a[1]) * h
        if odd == 5:
            return (a[1] - a[0]) * h, (a[0] + a[1]) * -h
        return (a[0] + a[1]) * h, (a[1] - a[0]) * h
    return a[0] * c - a[1] * s, a[0] * s + a[1] * c


def four(x, sign):
    a, b, c, d = add(x[0], x[2]), sub(x[0], x[2]), add(x[1], x[3]), sub(x[1], x[3])
    return [add(a, c), add_turned(b, d, sign), sub(a, c), add_turned(b, d, -sign)]


def eight(x, sign, keep=8):
    even, odd = four(x[0::2], sign), four(x[1::2], sign)
    odd = [odd[0], twiddle(odd[1], sign, 8), odd[2], twiddle(odd[3], 3 * sign, 8)]
    low = [add(even[0], odd[0]), add(even[1], odd[1]), add_turned(even[2], odd[2], sign), add(even[3], odd[3])]
    if keep == 4:
        return low
    return low + [sub(even[0], odd[0]), sub(even[1], odd[1]), add_turned(even[2], odd[2], -sign), sub(even[3], odd[3])]


def eight_of_four(x, sign):
    even = four(x, sign)
    odd = four([twiddle(x[m], sign * m, 8) for m in range(4)], sign)
    return [part for pair in zip(even, odd) for part in pair]


def prep(*refs):
    rotations, (mask_ref, kz_hi, kz_lo, ker_ref, out_ref) = refs[:4], refs[4:]
    filled = float(sphere_np().sum())
    low_half = lax.broadcasted_iota(jnp.int32, (1, LANES), 1) < GRID
    mask = mask_ref[...]
    normed = []
    for ref in rotations:
        t = ref[...]
        mu = jnp.sum(jnp.sum(t * mask, axis=0, keepdims=True), axis=1, keepdims=True) / filled
        d = (t - mu) * mask
        v = jnp.sum(jnp.sum(d * d, axis=0, keepdims=True), axis=1, keepdims=True) / filled
        normed.append(d * (1.0 / jnp.sqrt(v + EPSILON)))
    rows = []
    for jg in range(8):
        tile = [t[:, LANES * jg : LANES * (jg + 1)] for t in normed]
        far = [pltpu.roll(t, GRID, 1) for t in tile]
        rows += [
            jnp.concatenate([jnp.where(low_half, tile[r], far[r + 1]) for r in (0, 2)], axis=1),
            jnp.concatenate([jnp.where(low_half, far[r], tile[r + 1]) for r in (0, 2)], axis=1),
        ]
    out = right_dot(jnp.concatenate(rows, axis=0), kz_hi[...], kz_lo[...])
    for j in range(BOX):
        x = out[BOX * (j // 2) : BOX * (j // 2 + 1), 256 * (j % 2) : 256 * (j % 2 + 1)]
        re, im = left_dot(ker_ref[...], x, 1)
        out_ref[0, j] = re
        out_ref[1, j] = im


def get(ref, *index):
    return ref[(0,) + index], ref[(1,) + index]


def put(ref, value, *index):
    ref[(0,) + index] = value[0]
    ref[(1,) + index] = value[1]


def body(
    own_ref, before_ref, after_ref, kern_a, kern_b,
    mask_re, mask_im, tz_hi, tz_lo, fwd_ref, inv_ref, inv_m_ref, bz_two, bz_hi, bm_hi, bm_lo,
    top_ref, next_ref,
    spec, kspec, fspec, work, back, u_hi, u_lo,
):
    filled = float(sphere_np().sum())
    lane = lax.broadcasted_iota(jnp.int32, (1, LANES), 1)
    odd_quarter = lane % GRID >= BOX

    def tile(step):
        return pl.ds(pl.multiple_of(step * 8, 8), 8)

    def kernels_along_y(step):
        at = tile(step)
        for g, kern in enumerate((kern_a, kern_b)):
            for n2 in range(8):
                x = eight_of_four([get(kern, n2 + 8 * m, at) for m in range(4)], 1)
                for k1 in range(8):
                    put(work.at[g], twiddle(x[k1], n2 * k1, GRID), k1, n2)
            for k1 in range(8):
                x = eight([get(work.at[g], k1, n2) for n2 in range(8)], 1)
                for k2 in range(8):
                    put(kspec.at[g], x[k2], k1 + 8 * k2, at)

    for ref, first, count in ((before_ref, 0, HALF), (own_ref, HALF, BOX), (after_ref, HALF + BOX, HALF)):

        @pl.loop(0, count // 8)
        def _(step, ref=ref, first=first):
            y = step * 8
            rows = ref[pl.ds(y, 8)].reshape(8 * BOX, LANES)
            out = right_dot(jnp.concatenate([rows, rows * rows], axis=1), tz_hi[...], tz_lo[...])
            for e in range(8):
                some = out[BOX * e : BOX * (e + 1)]
                re, im = left_dot(fwd_ref[...], jnp.concatenate([some[:, :256], some[:, 256:]], axis=0), -1)
                spec[0, first + y + e] = re
                spec[1, first + y + e] = im
            kernels_along_y(step + first // 8)

    def finish(place, at, slot):
        for n2 in range(8):
            x = eight([get(work.at[slot], n2, k1) for k1 in range(8)], 1, keep=4)
            for n1 in range(4):
                put(back.at[place], x[n1], n2 + 8 * n1, at)

    @pl.loop(0, 8)
    def _(step):
        at = tile(step)
        for n2 in range(8):
            x = eight([get(spec, n2 + 8 * m, at) for m in range(8)], -1)
            for k1 in range(8):
                put(work.at[0], twiddle(x[k1], -n2 * k1, GRID), k1, n2)
        for k1 in range(8):
            x = eight([get(work.at[0], k1, n2) for n2 in range(8)], -1)
            prod = []
            for k2 in range(8):
                k = k1 + 8 * k2
                re, im = x[k2]
                put(fspec, [jnp.where(odd_quarter, pltpu.roll(v, BOX, 1), v) for v in (re, im)], k, at)
                a, b = mask_re[k, at], mask_im[k, at]
                prod.append((re * a - im * b, re * b + im * a))
            prod = eight(prod, 1)
            for n2 in range(8):
                put(work.at[1], twiddle(prod[n2], k1 * n2, GRID), n2, k1)
        finish(2, at, 1)

    def product_along_y(step, g):
        at = tile(step)
        for k1 in range(8):
            prod = []
            for k2 in range(8):
                k = k1 + 8 * k2
                a, b = get(fspec, k, at)
                re, im = get(kspec.at[g], k, at)
                prod.append((re * a - im * b, re * b + im * a))
            prod = eight(prod, 1)
            for n2 in range(8):
                put(work.at[g], twiddle(prod[n2], k1 * n2, GRID), n2, k1)
        finish(g, at, g)

    def along_x(step, s):
        for yy in range(4):
            y = 4 * step + yy
            x = jnp.concatenate([back[s, 0, y], back[s, 1, y]], axis=1)
            hi, lo = split(jnp.concatenate(left_dot(inv_ref[...] if s < 2 else inv_m_ref[...], x, 1), axis=1))
            rows = pl.ds(pl.multiple_of(y * BOX, BOX), BOX)
            u_hi[s, rows, :] = hi
            u_lo[s, rows, :] = lo

    @pl.loop(0, 8)
    def _(step):
        product_along_y(step, 0)
        along_x(step, 2)

    @pl.loop(0, 8)
    def _(step):
        product_along_y(step, 1)
        along_x(step, 0)

    for step in range(8):
        along_x(step, 1)

    def merged(one, other):
        return jnp.maximum(one[0], other[0]), jnp.maximum(jnp.minimum(one[0], other[0]), jnp.maximum(one[1], other[1]))

    quarter = lane // BOX
    for part in range(2):
        rows = pl.ds(512 * part, 512)
        hi, lo = u_hi[2, rows, :], u_lo[2, rows, :]
        sums = dot(hi, bm_hi[...]) + dot(lo, bm_hi[...]) + dot(hi, bm_lo[...])
        mean = sums[:, :LANES] / filled
        var = jnp.maximum(sums[:, LANES:] / filled - mean * mean, 0.0)
        scale = 1.0 / (np.float32(np.sqrt(filled)) * jnp.sqrt(var + EPSILON))
        corr = []
        for g in range(2):
            both = dot(u_hi[g, rows, :], bz_two[...])
            corr.append((both[:, :LANES] + both[:, LANES:] + dot(u_lo[g, rows, :], bz_hi[...])) * scale)
        best = jnp.maximum(corr[0], corr[1]), jnp.minimum(corr[0], corr[1])
        best = merged(best, [pltpu.roll(v, GRID, 1) for v in best])
        best = merged(best, [pltpu.roll(v, BOX, 1) for v in best])
        for ref, v in zip((top_ref, next_ref), best):
            for e in range(4):
                y = [v[BOX * (4 * e + q) : BOX * (4 * e + q + 1)] for q in range(4)]
                o = jnp.where(quarter < 2, jnp.where(quarter == 0, y[0], y[1]), jnp.where(quarter == 2, y[2], y[3]))
                ref[:, LANES * (4 * part + e) : LANES * (4 * part + e + 1)] = o


def shifts(count, step):
    return [(i, i + step) for i in range(count) if 0 <= i + step < count]


def local(tomogram, templates):
    tx, ty, rots = lax.axis_size("tx"), lax.axis_size("ty"), lax.axis_size("rot")
    tile = jnp.swapaxes(tomogram, 0, 1)

    def pack(part):
        return jnp.concatenate([part[:HALF], part[HALF:]], axis=2)

    def unpack(part):
        return jnp.concatenate([part[:, :, :GRID], part[:, :, GRID:]], axis=0)

    before = lax.ppermute(pack(tile[:, HALF:]), "tx", shifts(tx, 1))
    after = lax.ppermute(pack(tile[:, :HALF]), "tx", shifts(tx, -1))

    core = lax.rem(lax.axis_index("ty"), 2)
    mine = lax.dynamic_slice_in_dim(templates, core, 1, axis=0)
    far = [lax.ppermute(mine, "rot", [(i, (i + s) % rots) for i in range(rots)]) for s in range(1, rots)]
    far = jnp.concatenate(far, axis=0)
    core_far = lax.ppermute(far, "ty", [(i, i + 1 - 2 * (i % 2)) for i in range(ty)])

    grid = jnp.concatenate(
        [
            jnp.concatenate([unpack(before), tile[:, :HALF]], axis=1),
            jnp.concatenate([tile[:, HALF:], unpack(after)], axis=1),
        ],
        axis=2,
    )
    low = lax.ppermute(grid[HALF:], "ty", shifts(ty, 1))
    high = lax.ppermute(grid[:HALF], "ty", shifts(ty, -1))
    first = prep_call(templates[0], templates[1], far[0], far[1])
    second = prep_call(far[2], core_far[0], core_far[1], core_far[2])
    return kernel_call(grid, low, high, first, second)


def prep_call(*four_templates):
    mask, _, _, _, _, kz_hi, kz_lo, _, ker = tables()[:9]
    return pl.pallas_call(
        prep,
        out_shape=jax.ShapeDtypeStruct((2, BOX, GRID, LANES), F32),
        compiler_params=pltpu.CompilerParams(vmem_limit_bytes=16 * 1024 * 1024),
        cost_estimate=pl.CostEstimate(flops=2 * 10**9, bytes_accessed=4 * 10**6, transcendentals=0),
        name="prep",
    )(*four_templates, *[jnp.asarray(t) for t in (mask, kz_hi, kz_lo, ker)])


def kernel_call(grid, low, high, first, second):
    out = jax.ShapeDtypeStruct((BOX, BOX * BOX), F32)
    scratch = [
        pltpu.VMEM((2, GRID, GRID, LANES), F32),
        pltpu.VMEM((2, 2, GRID, GRID, LANES), F32),
        pltpu.VMEM((2, GRID, GRID, LANES), F32),
        pltpu.VMEM((2, 2, 8, 8, 8, LANES), F32),
        pltpu.VMEM((3, 2, BOX, GRID, LANES), F32),
        pltpu.VMEM((3, BOX * BOX, 2 * LANES), BF16),
        pltpu.VMEM((3, BOX * BOX, 2 * LANES), BF16),
    ]
    _, mask_re, mask_im, tz_hi, tz_lo, _, _, fwd, _, inv, inv_m, *back = tables()
    return pl.pallas_call(
        body,
        out_shape=(out, out),
        scratch_shapes=scratch,
        compiler_params=pltpu.CompilerParams(vmem_limit_bytes=40 * 1024 * 1024),
        cost_estimate=pl.CostEstimate(flops=10**10, bytes_accessed=10**7, transcendentals=0),
        name="scores",
    )(grid, low, high, first, second, *[jnp.asarray(t) for t in (mask_re, mask_im, tz_hi, tz_lo, fwd, inv, inv_m, *back)])


def solution(mesh):
    placed = (P("tx", "ty", None), P("rot", None, None))
    return jax.shard_map(
        local, mesh=mesh, in_specs=placed, out_specs=(P("tx", "ty"), P("tx", "ty")), check_vma=False
    )
```

time: 94.4 us -> 59.1 us (0.63)
  Pallas kernels: 52.9 us -> 24.7 us
  waiting for transfers between devices: 10.8 us -> 3.4 us
    pallas_call x1 -> x3, Pallas kernels: 52.9 us -> 24.7 us  [the longest x1 21.7 us: kernel_call(): pl.pallas_call(body, out_shape=(out, out), scratch_shapes=scratch, compil...]
    ppermute x4, waiting for transfers between devices: 8.59 us -> 3.39 us  [the longest x1 3.32 us: local(): before = lax.ppermute(pack(tile[:, HALF:]), 'tx', shifts(tx, 1))]
    ppermute x3, waiting for transfers between devices: 2.25 us -> 0.01 us  [local(): lax.ppermute(mine, 'rot', [(i, (i + s) % rots) for i in range(rots)])]
    ppermute x1, starting transfers between devices: 0.58 us -> 2.31 us  [local(): lax.ppermute(far, 'ty', [(i, i + 1 - 2 * (i % 2)) for i in range(ty)])]
    ppermute x3, starting transfers between devices: 10.6 us -> 9.35 us  [local(): lax.ppermute(mine, 'rot', [(i, (i + s) % rots) for i in range(rots)])]
    slice x5, local copies, waits for them, and re-layouts: 1.39 us -> 0.29 us  [the longest x2 0.18 us: unpack(): return jnp.concatenate([part[:, :, :GRID], part[:, :, GRID:]], axis=0)]
    unnamed x14 -> x31, local copies, waits for them, and re-layouts: 1.46 us -> 2.13 us
  transfers between devices with their start and end apart: 8 -> 8, of which waited for: 4 -> 2; matrix products, arithmetic and copies ran while one was open for 2% -> 4% of each run, Pallas kernels for 0% -> 5%
where the time goes in v3:
time: 59.1 us; the launch traced here: 58.9 us
  starting transfers between devices  25.9 us (44%)
  Pallas kernels  24.7 us (42%)
  local copies, waits for them, and re-layouts  3.51 us (6%)
  waiting for transfers between devices  3.4 us (6%)
  between operations  0.97 us (2%)
    pallas_call x1, Pallas kernels, kernel_call(): pl.pallas_call(body, out_shape=(out, out), scratch_shapes=scratch, compil...  21.7 us
    ppermute x3, starting transfers between devices, local(): lax.ppermute(mine, 'rot', [(i, (i + s) % rots) for i in range(rots)])  9.35 us
    ppermute x1, starting transfers between devices, local(): after = lax.ppermute(pack(tile[:, :HALF]), 'tx', shifts(tx, -1))  4.91 us
    ppermute x1, starting transfers between devices, local(): high = lax.ppermute(grid[:HALF], 'ty', shifts(ty, -1))  4.85 us
    ppermute x1, waiting for transfers between devices, local(): before = lax.ppermute(pack(tile[:, HALF:]), 'tx', shifts(tx, 1))  3.32 us
    pallas_call x2, Pallas kernels, prep_call(): pl.pallas_call(prep, out_shape=jax.ShapeDtypeStruct((2, BOX, GRID, LANES)...  2.98 us
    ppermute x1, starting transfers between devices, local(): low = lax.ppermute(grid[HALF:], 'ty', shifts(ty, 1))  2.54 us
    ppermute x1, starting transfers between devices, local(): lax.ppermute(far, 'ty', [(i, i + 1 - 2 * (i % 2)) for i in range(ty)])  2.31 us
  transfers between devices with their start and end apart: 8, of which 2 were waited for; matrix products, arithmetic and copies ran while one was open for 4% of the time, Pallas kernels for 5%

profile of v3, /device:TPU:7, one launch (start us, length us, event | category | flops | bytes accessed | tf_op | source)
XLA Modules:
  0.0 58.9 jit_solution(14423320294410480053)
XLA Ops:
  0.6 1.1 %constant_dynamic-slice_fusion = (f32[1,32,1024]{2,1,0:T(8,128)S(1)}, f32[32,1024]{1,0:T(8,128)S(1)}, f32[32,1024]{1,0:T(8,128)S(1)}) fusion(f32[2,32,1024]{2,1,0:T(8,128)} %param.18, s32[]{:T(128)S(6)} %select_n.3), kind=kLoop, calls=%fused_computation.10 | loop fusion | bytes 786436 | tf_op jit(solution)/shard_map/dynamic_slice | solution.py:375
  1.7 6.1 %collective-permute-start.6 = (f32[1,32,1024]{2,1,0:T(8,128)S(1)}, f32[1,32,1024]{2,1,0:T(8,128)S(1)}, u32[]{:S(2)}, u32[]{:S(2)}) collective-permute-start(f32[1,32,1024]{2,1,0:T(8,128)S(1)} %get-tuple-element.13), channel_id=1, source_target_pairs={{0,192},{64,0},{128,64},{192,128},{1,193},{65,1},{129,65},{193,129... | collective-permute-start | bytes 393224 | tf_op jit(solution)/shard_map/ppermute | solution.py:376
  7.8 1.0 %collective-permute-start.5 = (f32[1,32,1024]{2,1,0:T(8,128)S(1)}, f32[1,32,1024]{2,1,0:T(8,128)S(1)}, u32[]{:S(2)}, u32[]{:S(2)}) collective-permute-start(f32[1,32,1024]{2,1,0:T(8,128)S(1)} %get-tuple-element.13), channel_id=1, source_target_pairs={{0,128},{64,192},{128,0},{192,64},{1,129},{65,193},{129,1},{193,65... | collective-permute-start | bytes 393224 | tf_op jit(solution)/shard_map/ppermute | solution.py:376
  8.8 2.3 %collective-permute-start.4 = (f32[1,32,1024]{2,1,0:T(8,128)S(1)}, f32[1,32,1024]{2,1,0:T(8,128)S(1)}, u32[]{:S(2)}, u32[]{:S(2)}) collective-permute-start(f32[1,32,1024]{2,1,0:T(8,128)S(1)} %get-tuple-element.13), channel_id=1, source_target_pairs={{0,64},{64,128},{128,192},{192,0},{1,65},{65,129},{129,193},{193,1... | collective-permute-start | bytes 393224 | tf_op jit(solution)/shard_map/ppermute | solution.py:376
  11.1 1.3 %copy.21 = f32[32,32,64]{2,0,1:T(8,128)S(1)} copy(f32[32,32,64]{2,1,0:T(8,128)} %param.17) | data formatting | bytes 524288 | tf_op args[0]
  12.5 0.1 pad_maximum_fusion.2
  12.6 4.9 %collective-permute-start.1 = (f32[16,16,128]{2,1,0:T(8,128)S(1)}, f32[16,16,128]{2,1,0:T(8,128)S(1)}, u32[]{:S(2)}, u32[]{:S(2)}) collective-permute-start(f32[16,16,128]{2,1,0:T(8,128)S(1)} %pad_maximum_fusion.2), channel_id=1, source_target_pairs={{4,0},{8,4},{12,8},{16,12},{20,16},{24,20},{28,24},{32,28},{36,32}... | collective-permute-start | bytes 393224 | tf_op jit(solution)/shard_map/ppermute | solution.py:372
  17.5 0.1 pad_maximum_fusion.1
  17.6 1.9 %collective-permute-start = (f32[16,16,128]{2,1,0:T(8,128)S(1)}, f32[16,16,128]{2,1,0:T(8,128)S(1)}, u32[]{:S(2)}, u32[]{:S(2)}) collective-permute-start(f32[16,16,128]{2,1,0:T(8,128)S(1)} %pad_maximum_fusion.1), channel_id=1, source_target_pairs={{0,4},{4,8},{8,12},{12,16},{16,20},{20,24},{24,28},{28,32},{32,36}... | collective-permute-start | bytes 393224 | tf_op jit(solution)/shard_map/ppermute | solution.py:371
  19.6 0.0 copy-start.4
  19.6 0.0 copy-start.5
  19.6 0.0 copy-start.9
  19.6 0.0 copy-start.14
  19.6 0.0 collective-permute-done.6
  19.6 0.0 collective-permute-done.5
  19.6 0.0 collective-permute-done.4
  19.7 2.3 %collective-permute-start.7 = (f32[3,32,1024]{2,1,0:T(8,128)S(1)}, f32[3,32,1024]{2,1,0:T(8,128)S(1)}, u32[]{:S(2)}, u32[]{:S(2)}) collective-permute-start(f32[3,32,1024]{2,1,0:T(8,128)S(1)} %pad_maximum_fusion), channel_id=1, source_target_pairs={{0,1},{1,0},{2,3},{3,2},{4,5},{5,4},{6,7},{7,6},{8,9},{9,8},{10,11... | collective-permute-start | bytes 1179656 | tf_op jit(solution)/shard_map/ppermute | solution.py:378
  22.0 0.0 collective-permute-done.1
  22.0 0.1 fusion.4
  22.1 3.3 %collective-permute-done = f32[16,16,128]{2,1,0:T(8,128)S(1)} collective-permute-done((f32[16,16,128]{2,1,0:T(8,128)S(1)}, f32[16,16,128]{2,1,0:T(8,128)S(1)}, u32[]{:S(2)}, u32[]{:S(2)}) %collective-permute-start) | collective-permute-done | bytes 131104 | tf_op jit(solution)/shard_map/ppermute | solution.py:371
  25.4 0.1 fusion.3
  25.5 0.2 maximum_maximum_fusion.own_ref
  25.8 4.9 %collective-permute-start.3 = (f32[16,32,128]{2,1,0:T(8,128)S(1)}, f32[16,32,128]{2,1,0:T(8,128)S(1)}, u32[]{:S(2)}, u32[]{:S(2)}) collective-permute-start(f32[16,32,128]{2,1,0:T(8,128)S(1)} %get-tuple-element.2), channel_id=1, source_target_pairs={{1,0},{2,1},{3,2},{5,4},{6,5},{7,6},{9,8},{10,9},{11,10},{13,12},{... | collective-permute-start | bytes 786440 | tf_op jit(solution)/shard_map/ppermute | solution.py:388
  30.6 2.5 %collective-permute-start.2 = (f32[16,32,128]{2,1,0:T(8,128)S(1)}, f32[16,32,128]{2,1,0:T(8,128)S(1)}, u32[]{:S(2)}, u32[]{:S(2)}) collective-permute-start(f32[16,32,128]{2,1,0:T(8,128)S(1)} %get-tuple-element.3), channel_id=1, source_target_pairs={{0,1},{1,2},{2,3},{4,5},{5,6},{6,7},{8,9},{9,10},{10,11},{12,13},{... | collective-permute-start | bytes 786440 | tf_op jit(solution)/shard_map/ppermute | solution.py:387
  33.2 0.0 copy-done.4
  33.2 1.5 %prep.2.kern_a = f32[2,32,64,128]{3,2,1,0:T(8,128)S(1)} custom-call(f32[32,1024]{1,0:T(8,128)S(1)} %get-tuple-element.14.refs_0_, f32[32,1024]{1,0:T(8,128)S(1)} %get-tuple-element.15.refs_1_, f32[32,1024]{1,0:T(8,128)S(1)} %bitcast.18, f32[32,1024]{1,0:T(8,128)S(1)} %bitcast.17, f32[32,1024]{1,0:T(8,128)S(1)} %copy-done.9, bf16[256,512]{1,0:T(8,128)(2,1)S(1)} %copy-done.5, ...), custom_call_target="tpu_custom_call" | custom-call | flops 2000000000 | bytes 4000000 | tf_op jit(solution)/shard_map/prep/pallas_call | solution.py:396
  34.7 0.0 collective-permute-done.7
  34.8 0.0 copy-start
  34.8 0.0 copy-start.1
  34.8 0.0 copy-start.2
  34.8 0.0 copy-start.3
  34.8 0.0 copy-start.6
  34.8 0.0 copy-start.7
  34.8 0.0 copy-start.8
  34.8 0.0 copy-start.10
  34.9 0.0 copy-start.11
  34.9 0.0 copy-start.12
  34.9 0.0 copy-start.13
  34.9 1.5 %prep.3.kern_b = f32[2,32,64,128]{3,2,1,0:T(8,128)S(1)} custom-call(f32[32,1024]{1,0:T(8,128)S(1)} %bitcast.16, f32[32,1024]{1,0:T(8,128)S(1)} %get-tuple-element.12.refs_1_, f32[32,1024]{1,0:T(8,128)S(1)} %get-tuple-element.11.refs_2_, f32[32,1024]{1,0:T(8,128)S(1)} %get-tuple-element.10.refs_3_, f32[32,1024]{1,0:T(8,128)S(1)} %copy-done.9, ...), custom_call_target="tpu_custom_call" | custom-call | flops 2000000000 | bytes 4000000 | tf_op jit(solution)/shard_map/prep/pallas_call | solution.py:396
  36.4 0.0 collective-permute-done.3.after_ref
  36.4 0.1 collective-permute-done.2.before_ref
  36.5 0.5 copy-done.1
  37.0 0.1 copy-done.3
  37.1 0.0 copy-done.6
  37.1 0.0 copy-done.7
  37.1 0.0 copy-done.8
  37.2 0.0 copy-done.11
  37.2 21.7 %scores.1 = (f32[32,1024]{1,0:T(8,128)}, f32[32,1024]{1,0:T(8,128)}) custom-call(f32[32,32,128]{2,1,0:T(8,128)S(1)} %maximum_maximum_fusion.own_ref, f32[16,32,128]{2,1,0:T(8,128)S(1)} %collective-permute-done.2.before_ref, f32[16,32,128]{2,1,0:T(8,128)S(1)} %collective-permute-done.3.after_ref, f32[2,32,64,128]{3,2,1,0:T(8,128)S(1)} %prep.2.kern_a, ...), custom_call_target="tpu_custom_call" | custom-call | flops 10000000000 | bytes 10000000 | tf_op jit(solution)/shard_map/scores/pallas_call | solution.py:417
  (13 shorter events, 0.2 us)
Async XLA Ops:
  1.7 17.9 %collective-permute-start.6 = (f32[1,32,1024]{2,1,0:T(8,128)S(1)}, f32[1,32,1024]{2,1,0:T(8,128)S(1)}, u32[]{:S(2)}, u32[]{:S(2)}) collective-permute-start(f32[1,32,1024]{2,1,0:T(8,128)S(1)} %get-tuple-element.13), channel_id=1, source_target_pairs={{0,192},{64,0},{128,64},{192,128},{1,193},{65,1},{129,65},{193,129... | collective-permute-start | bytes 393224 | tf_op jit(solution)/shard_map/ppermute | solution.py:376
  7.8 11.8 %collective-permute-start.5 = (f32[1,32,1024]{2,1,0:T(8,128)S(1)}, f32[1,32,1024]{2,1,0:T(8,128)S(1)}, u32[]{:S(2)}, u32[]{:S(2)}) collective-permute-start(f32[1,32,1024]{2,1,0:T(8,128)S(1)} %get-tuple-element.13), channel_id=1, source_target_pairs={{0,128},{64,192},{128,0},{192,64},{1,129},{65,193},{129,1},{193,65... | collective-permute-start | bytes 393224 | tf_op jit(solution)/shard_map/ppermute | solution.py:376
  8.8 10.8 %collective-permute-start.4 = (f32[1,32,1024]{2,1,0:T(8,128)S(1)}, f32[1,32,1024]{2,1,0:T(8,128)S(1)}, u32[]{:S(2)}, u32[]{:S(2)}) collective-permute-start(f32[1,32,1024]{2,1,0:T(8,128)S(1)} %get-tuple-element.13), channel_id=1, source_target_pairs={{0,64},{64,128},{128,192},{192,0},{1,65},{65,129},{129,193},{193,1... | collective-permute-start | bytes 393224 | tf_op jit(solution)/shard_map/ppermute | solution.py:376
  12.6 9.4 %collective-permute-start.1 = (f32[16,16,128]{2,1,0:T(8,128)S(1)}, f32[16,16,128]{2,1,0:T(8,128)S(1)}, u32[]{:S(2)}, u32[]{:S(2)}) collective-permute-start(f32[16,16,128]{2,1,0:T(8,128)S(1)} %pad_maximum_fusion.2), channel_id=1, source_target_pairs={{4,0},{8,4},{12,8},{16,12},{20,16},{24,20},{28,24},{32,28},{36,32}... | collective-permute-start | bytes 393224 | tf_op jit(solution)/shard_map/ppermute | solution.py:372
  17.6 7.8 %collective-permute-start = (f32[16,16,128]{2,1,0:T(8,128)S(1)}, f32[16,16,128]{2,1,0:T(8,128)S(1)}, u32[]{:S(2)}, u32[]{:S(2)}) collective-permute-start(f32[16,16,128]{2,1,0:T(8,128)S(1)} %pad_maximum_fusion.1), channel_id=1, source_target_pairs={{0,4},{4,8},{8,12},{12,16},{16,20},{20,24},{24,28},{28,32},{32,36}... | collective-permute-start | bytes 393224 | tf_op jit(solution)/shard_map/ppermute | solution.py:371
  19.6 13.6 %copy-start.4 = (bf16[256,512]{1,0:T(8,128)(2,1)S(1)}, bf16[256,512]{1,0:T(8,128)(2,1)}, u32[]{:S(2)}) copy-start(bf16[256,512]{1,0:T(8,128)(2,1)} %constant.43.clone.refs_6_) | copy-start | bytes 786436
  19.6 13.6 %copy-start.5 = (bf16[256,512]{1,0:T(8,128)(2,1)S(1)}, bf16[256,512]{1,0:T(8,128)(2,1)}, u32[]{:S(2)}) copy-start(bf16[256,512]{1,0:T(8,128)(2,1)} %constant.42.clone.refs_5_) | copy-start | bytes 786436
  19.6 13.6 %copy-start.9 = (f32[32,1024]{1,0:T(8,128)S(1)}, f32[32,1024]{1,0:T(8,128)}, u32[]{:S(2)}) copy-start(f32[32,1024]{1,0:T(8,128)} %constant.41.clone.refs_4_) | copy-start | bytes 393220
  19.6 13.6 %copy-start.14 = (bf16[128,96]{1,0:T(8,128)(2,1)S(1)}, bf16[128,96]{1,0:T(8,128)(2,1)}, u32[]{:S(2)}) copy-start(bf16[128,96]{1,0:T(8,128)(2,1)} %constant.44.clone.refs_7_) | copy-start | bytes 73732
  19.7 15.0 %collective-permute-start.7 = (f32[3,32,1024]{2,1,0:T(8,128)S(1)}, f32[3,32,1024]{2,1,0:T(8,128)S(1)}, u32[]{:S(2)}, u32[]{:S(2)}) collective-permute-start(f32[3,32,1024]{2,1,0:T(8,128)S(1)} %pad_maximum_fusion), channel_id=1, source_target_pairs={{0,1},{1,0},{2,3},{3,2},{4,5},{5,4},{6,7},{7,6},{8,9},{9,8},{10,11... | collective-permute-start | bytes 1179656 | tf_op jit(solution)/shard_map/ppermute | solution.py:378
  25.8 10.6 %collective-permute-start.3 = (f32[16,32,128]{2,1,0:T(8,128)S(1)}, f32[16,32,128]{2,1,0:T(8,128)S(1)}, u32[]{:S(2)}, u32[]{:S(2)}) collective-permute-start(f32[16,32,128]{2,1,0:T(8,128)S(1)} %get-tuple-element.2), channel_id=1, source_target_pairs={{1,0},{2,1},{3,2},{5,4},{6,5},{7,6},{9,8},{10,9},{11,10},{13,12},{... | collective-permute-start | bytes 786440 | tf_op jit(solution)/shard_map/ppermute | solution.py:388
  30.6 5.8 %collective-permute-start.2 = (f32[16,32,128]{2,1,0:T(8,128)S(1)}, f32[16,32,128]{2,1,0:T(8,128)S(1)}, u32[]{:S(2)}, u32[]{:S(2)}) collective-permute-start(f32[16,32,128]{2,1,0:T(8,128)S(1)} %get-tuple-element.3), channel_id=1, source_target_pairs={{0,1},{1,2},{2,3},{4,5},{5,6},{6,7},{8,9},{9,10},{10,11},{12,13},{... | collective-permute-start | bytes 786440 | tf_op jit(solution)/shard_map/ppermute | solution.py:387
  34.8 1.7 %copy-start = (f32[64,64,128]{2,1,0:T(8,128)S(1)}, f32[64,64,128]{2,1,0:T(8,128)}, u32[]{:S(2)}) copy-start(f32[64,64,128]{2,1,0:T(8,128)} %constant.46.clone.mask_im) | copy-start | bytes 6291460
  34.8 2.2 %copy-start.1 = (f32[64,64,128]{2,1,0:T(8,128)S(1)}, f32[64,64,128]{2,1,0:T(8,128)}, u32[]{:S(2)}) copy-start(f32[64,64,128]{2,1,0:T(8,128)} %constant.45.clone.mask_re) | copy-start | bytes 6291460
  34.8 2.2 %copy-start.2 = (bf16[256,512]{1,0:T(8,128)(2,1)S(1)}, bf16[256,512]{1,0:T(8,128)(2,1)}, u32[]{:S(2)}) copy-start(bf16[256,512]{1,0:T(8,128)(2,1)} %constant.48.clone.tz_lo) | copy-start | bytes 786436
  34.8 2.3 %copy-start.3 = (bf16[256,512]{1,0:T(8,128)(2,1)S(1)}, bf16[256,512]{1,0:T(8,128)(2,1)}, u32[]{:S(2)}) copy-start(bf16[256,512]{1,0:T(8,128)(2,1)} %constant.47.clone.tz_hi) | copy-start | bytes 786436
  34.8 2.3 %copy-start.6 = (bf16[256,256]{1,0:T(8,128)(2,1)S(1)}, bf16[256,256]{1,0:T(8,128)(2,1)}, u32[]{:S(2)}) copy-start(bf16[256,256]{1,0:T(8,128)(2,1)} %constant.55.clone.bm_lo) | copy-start | bytes 393220
  34.8 2.3 %copy-start.7 = (bf16[256,256]{1,0:T(8,128)(2,1)S(1)}, bf16[256,256]{1,0:T(8,128)(2,1)}, u32[]{:S(2)}) copy-start(bf16[256,256]{1,0:T(8,128)(2,1)} %constant.54.clone.bm_hi) | copy-start | bytes 393220
  34.8 2.3 %copy-start.8 = (bf16[256,256]{1,0:T(8,128)(2,1)S(1)}, bf16[256,256]{1,0:T(8,128)(2,1)}, u32[]{:S(2)}) copy-start(bf16[256,256]{1,0:T(8,128)(2,1)} %constant.52.clone.bz_two) | copy-start | bytes 393220
  34.8 2.3 %copy-start.10 = (bf16[256,128]{1,0:T(8,128)(2,1)S(1)}, bf16[256,128]{1,0:T(8,128)(2,1)}, u32[]{:S(2)}) copy-start(bf16[256,128]{1,0:T(8,128)(2,1)} %constant.53.clone.bz_hi) | copy-start | bytes 196612
  34.9 2.3 %copy-start.11 = (bf16[128,192]{1,0:T(8,128)(2,1)S(1)}, bf16[128,192]{1,0:T(8,128)(2,1)}, u32[]{:S(2)}) copy-start(bf16[128,192]{1,0:T(8,128)(2,1)} %constant.49.clone.fwd_ref) | copy-start | bytes 147460
  34.9 2.3 %copy-start.12 = (bf16[64,192]{1,0:T(8,128)(2,1)S(1)}, bf16[64,192]{1,0:T(8,128)(2,1)}, u32[]{:S(2)}) copy-start(bf16[64,192]{1,0:T(8,128)(2,1)} %constant.51.clone.inv_m_ref) | copy-start | bytes 73732
  34.9 2.3 %copy-start.13 = (bf16[64,192]{1,0:T(8,128)(2,1)S(1)}, bf16[64,192]{1,0:T(8,128)(2,1)}, u32[]{:S(2)}) copy-start(bf16[64,192]{1,0:T(8,128)(2,1)} %constant.50.clone.inv_ref) | copy-start | bytes 73732

commit v4 on v3

--- a/solution.py
+++ b/solution.py
@@ -59,11 +59,10 @@
     cz, sz = wave(np.arange(GRID), odd)
     tomo = {}
     for kind in range(2):
-        for side in range(2):
-            for dup in range(2):
-                tomo[2 * kind + side, 8 * side + 2 * dup + kind] = cz
-                tomo[2 * kind + side, 8 * side + 4 + 2 * dup + kind] = -sz
-    tomo_z = block(4, 16, tomo)
+        for dup in range(2):
+            tomo[kind, 2 * dup + kind] = cz
+            tomo[kind, 4 + 2 * dup + kind] = -sz
+    tomo_hi, tomo_lo = halves(block(2, 8, tomo))
     ct, st = wave(np.arange(BOX), odd)
     kern = {}
     for rot in range(4):
@@ -77,35 +76,39 @@
     for vol in range(4):
         back[vol, vol] = ci / BOX
         back[4 + vol, vol] = -si / BOX
-    for vol in range(2):
+    for row in range(4):
         for copy in range(4):
-            back_mask[vol, 4 * vol + copy] = cm / BOX
-            back_mask[4 + vol, 4 * vol + copy] = -sm / BOX
+            back_mask[row, 4 * (row % 2) + copy] = cm / BOX
+            back_mask[4 + row, 4 * (row % 2) + copy] = -sm / BOX
     back_hi, back_lo = halves(block(8, 4, back))
     back_mask_z = block(8, 8, back_mask)
+    one = np.eye(BOX)
+    copies = block(8, 8, {(row, col): one for half in (0, 4) for row, first in ((half, 0), (half + 2, 4)) for col in range(first, first + 4)})
     sphere = sphere_np()
     shifted = np.arange(BOX) - centre
     cx, sx = wave(freq, shifted)
     cy, sy = wave(freq, np.arange(BOX))
     co, so = wave(odd, shifted)
     spec = np.einsum("ai,bj,ck,ijk->bac", cx + 1j * sx, cy + 1j * sy, co + 1j * so, sphere, optimize=True)
-    mask_re = np.tile(spec.real, (1, 1, 4)).astype(np.float32)
-    mask_im = np.tile(spec.imag, (1, 1, 4)).astype(np.float32)
+    spec = np.concatenate([spec[:, :BOX], spec[:, :BOX], spec[:, BOX:], spec[:, BOX:]], axis=2)
+    mask_re, mask_im = spec.real.astype(np.float32), spec.imag.astype(np.float32)
     mask = sphere.reshape(BOX, BOX * BOX).astype(np.float32)
     scale = 1.0 / (GRID * GRID)
     return (
         mask,
         mask_re,
         mask_im,
-        *halves(tomo_z),
+        np.concatenate([tomo_hi, tomo_hi], axis=0),
+        tomo_lo,
         *halves(kern_z),
-        left_table(freq, np.arange(GRID), 1.0),
+        left_table(freq[:BOX], np.arange(GRID), 1.0),
         left_table(freq, np.arange(BOX), 1.0),
         left_table(np.arange(BOX), freq, scale),
-        left_table(np.arange(BOX) + centre, freq, scale),
+        np.concatenate([left_table(np.arange(BOX) + centre, f, scale) for f in (freq[:BOX], freq[BOX:])], axis=0),
         np.concatenate([back_hi, back_lo], axis=1),
         back_hi,
         *halves(back_mask_z),
+        copies.astype(ml_dtypes.bfloat16),
     )
 
 
@@ -125,7 +128,10 @@
 
 def left_dot(table, x, sign):
     hi, lo = split(x)
-    out = dot(table, jnp.concatenate([hi, lo, hi], axis=0))
+    return joined_parts(dot(table, jnp.concatenate([hi, lo, hi], axis=0)), sign)
+
+
+def joined_parts(out, sign):
     n = out.shape[0] // 2
     tr, ti, br, bi = out[:n, :LANES], out[:n, LANES:], out[n:, :LANES], out[n:, LANES:]
     if sign > 0:
@@ -229,9 +235,9 @@
 
 def body(
     own_ref, before_ref, after_ref, kern_a, kern_b,
-    mask_re, mask_im, tz_hi, tz_lo, fwd_ref, inv_ref, inv_m_ref, bz_two, bz_hi, bm_hi, bm_lo,
+    mask_re, mask_im, tz_two, tz_lo, fwd_ref, inv_ref, inv_m_ref, bz_two, bz_hi, bm_hi, bm_lo, copies_ref,
     top_ref, next_ref,
-    spec, kspec, fspec, work, back, u_hi, u_lo,
+    spec, kspec, fspec, work, slab, back, back_m, plain, u_hi, u_lo,
 ):
     filled = float(sphere_np().sum())
     lane = lax.broadcasted_iota(jnp.int32, (1, LANES), 1)
@@ -240,39 +246,52 @@
     def tile(step):
         return pl.ds(pl.multiple_of(step * 8, 8), 8)
 
-    def kernels_along_y(step):
-        at = tile(step)
+    def kernels_first(at, n2, slot):
         for g, kern in enumerate((kern_a, kern_b)):
-            for n2 in range(8):
-                x = eight_of_four([get(kern, n2 + 8 * m, at) for m in range(4)], 1)
-                for k1 in range(8):
-                    put(work.at[g], twiddle(x[k1], n2 * k1, GRID), k1, n2)
+            x = eight_of_four([get(kern, n2 + 8 * m, at) for m in range(4)], 1)
             for k1 in range(8):
-                x = eight([get(work.at[g], k1, n2) for n2 in range(8)], 1)
-                for k2 in range(8):
-                    put(kspec.at[g], x[k2], k1 + 8 * k2, at)
-
-    for ref, first, count in ((before_ref, 0, HALF), (own_ref, HALF, BOX), (after_ref, HALF + BOX, HALF)):
-
-        @pl.loop(0, count // 8)
-        def _(step, ref=ref, first=first):
-            y = step * 8
-            rows = ref[pl.ds(y, 8)].reshape(8 * BOX, LANES)
-            out = right_dot(jnp.concatenate([rows, rows * rows], axis=1), tz_hi[...], tz_lo[...])
-            for e in range(8):
-                some = out[BOX * e : BOX * (e + 1)]
-                re, im = left_dot(fwd_ref[...], jnp.concatenate([some[:, :256], some[:, 256:]], axis=0), -1)
-                spec[0, first + y + e] = re
-                spec[1, first + y + e] = im
-            kernels_along_y(step + first // 8)
+                put(work.at[2 * slot + g], twiddle(x[k1], n2 * k1, GRID), k1, n2)
+
+    def kernels_second(at, k1, slot):
+        for g in range(2):
+            x = eight([get(work.at[2 * slot + g], k1, n2) for n2 in range(8)], 1)
+            for k2 in range(8):
+                put(kspec.at[g], x[k2], k1 + 8 * k2, at)
+
+    low_half = lane < GRID
+    row_odd = lax.broadcasted_iota(jnp.int32, (GRID, 2 * LANES), 0) % 2 == 1
+    col_upper = lax.broadcasted_iota(jnp.int32, (GRID, 2 * LANES), 1) % LANES >= GRID
+    parity = jnp.where(jnp.logical_and(row_odd, col_upper), -1.0, 1.0).astype(F32)
+    def along_z(step):
+        ref, start = ((before_ref, 0), (own_ref, 2), (after_ref, 6))[(step >= 2) + (step >= 6)]
+        one = ref[8 * (step - start) : 8 * (step - start) + 8].reshape(8 * BOX, LANES)
+        two = one * one
+        lower = jnp.where(low_half, one, pltpu.roll(two, GRID, 1))
+        upper = jnp.where(low_half, pltpu.roll(one, GRID, 1), two)
+        rows = [v[BOX * e : BOX * (e + 1)] for e in range(8) for v in (lower, upper)]
+        hi, lo = split(jnp.concatenate(rows, axis=0))
+        slab[step % 2] = dot(jnp.concatenate([hi, lo], axis=1), tz_two[...]) + dot(hi, tz_lo[...])
+
+    along_z(0)
+    for step in range(8):
+        at = slice(8 * step, 8 * step + 8)
+        if step < 7:
+            along_z(step + 1)
+        for e in range(8):
+            kernels_first(at, e, step % 2)
+        for e in range(8):
+            re, im = left_dot(fwd_ref[...], slab[step % 2, GRID * e : GRID * (e + 1)] * parity, -1)
+            spec[0, 8 * step + e] = re
+            spec[1, 8 * step + e] = im
+            kernels_second(at, e, step % 2)
 
     def finish(place, at, slot):
         for n2 in range(8):
             x = eight([get(work.at[slot], n2, k1) for k1 in range(8)], 1, keep=4)
             for n1 in range(4):
-                put(back.at[place], x[n1], n2 + 8 * n1, at)
-
-    @pl.loop(0, 8)
+                put(place, x[n1], n2 + 8 * n1, at)
+
+    @pl.loop(0, 4)
     def _(step):
         at = tile(step)
         for n2 in range(8):
@@ -285,49 +304,55 @@
             for k2 in range(8):
                 k = k1 + 8 * k2
                 re, im = x[k2]
-                put(fspec, [jnp.where(odd_quarter, pltpu.roll(v, BOX, 1), v) for v in (re, im)], k, at)
+                put(plain, (re, im), k)
                 a, b = mask_re[k, at], mask_im[k, at]
                 prod.append((re * a - im * b, re * b + im * a))
             prod = eight(prod, 1)
             for n2 in range(8):
                 put(work.at[1], twiddle(prod[n2], k1 * n2, GRID), n2, k1)
-        finish(2, at, 1)
-
-    def product_along_y(step, g):
-        at = tile(step)
-        for k1 in range(8):
-            prod = []
-            for k2 in range(8):
-                k = k1 + 8 * k2
-                a, b = get(fspec, k, at)
-                re, im = get(kspec.at[g], k, at)
-                prod.append((re * a - im * b, re * b + im * a))
-            prod = eight(prod, 1)
-            for n2 in range(8):
-                put(work.at[g], twiddle(prod[n2], k1 * n2, GRID), n2, k1)
-        finish(g, at, g)
-
-    def along_x(step, s):
-        for yy in range(4):
-            y = 4 * step + yy
-            x = jnp.concatenate([back[s, 0, y], back[s, 1, y]], axis=1)
-            hi, lo = split(jnp.concatenate(left_dot(inv_ref[...] if s < 2 else inv_m_ref[...], x, 1), axis=1))
-            rows = pl.ds(pl.multiple_of(y * BOX, BOX), BOX)
-            u_hi[s, rows, :] = hi
-            u_lo[s, rows, :] = lo
-
-    @pl.loop(0, 8)
-    def _(step):
-        product_along_y(step, 0)
-        along_x(step, 2)
-
-    @pl.loop(0, 8)
-    def _(step):
-        product_along_y(step, 1)
-        along_x(step, 0)
-
-    for step in range(8):
-        along_x(step, 1)
+        for c in range(2):
+            out = dot(jnp.concatenate(split(plain[c].reshape(GRID * 8, LANES)), axis=1), copies_ref[...])
+            fspec[c, :, at] = out[:, :LANES].reshape(GRID, 8, LANES)
+            fspec[c, :, tile(step + 4)] = out[:, LANES:].reshape(GRID, 8, LANES)
+        finish(back_m, at, 1)
+
+    def product_along_y(at, g, k1):
+        prod = []
+        for k2 in range(8):
+            k = k1 + 8 * k2
+            a, b = get(fspec, k, at)
+            re, im = get(kspec.at[g], k, at)
+            prod.append((re * a - im * b, re * b + im * a))
+        prod = eight(prod, 1)
+        for n2 in range(8):
+            put(work.at[g], twiddle(prod[n2], k1 * n2, GRID), n2, k1)
+
+    def along_x(y, s):
+        if s == 2:
+            hi, lo = split(jnp.concatenate([back_m[0, y], back_m[1, y]], axis=1))
+            out = dot(inv_m_ref[...], jnp.concatenate([hi, lo, hi], axis=0))
+            first, other = joined_parts(out[: 2 * BOX], 1), joined_parts(out[2 * BOX :], 1)
+            res = [jnp.where(low_half, a, b) for a, b in zip(first, other)]
+        else:
+            res = left_dot(inv_ref[...], jnp.concatenate([back[s, 0, y], back[s, 1, y]], axis=1), 1)
+        hi, lo = split(jnp.concatenate(res, axis=1))
+        rows = pl.ds(pl.multiple_of(y * BOX, BOX), BOX)
+        u_hi[s, rows, :] = hi
+        u_lo[s, rows, :] = lo
+
+    for g, s in ((0, 2), (1, 0)):
+
+        @pl.loop(0, 8, unroll=4)
+        def _(step, g=g, s=s):
+            at = tile(step)
+            for k1 in range(8):
+                product_along_y(at, g, k1)
+                if k1 % 2:
+                    along_x(4 * step + k1 // 2, s)
+            finish(back.at[g], at, g)
+
+    for y in range(BOX):
+        along_x(y, 1)
 
     def merged(one, other):
         return jnp.maximum(one[0], other[0]), jnp.maximum(jnp.minimum(one[0], other[0]), jnp.maximum(one[1], other[1]))
@@ -405,11 +430,14 @@
 def kernel_call(grid, low, high, first, second):
     out = jax.ShapeDtypeStruct((BOX, BOX * BOX), F32)
     scratch = [
-        pltpu.VMEM((2, GRID, GRID, LANES), F32),
+        pltpu.VMEM((2, GRID, BOX, LANES), F32),
         pltpu.VMEM((2, 2, GRID, GRID, LANES), F32),
         pltpu.VMEM((2, GRID, GRID, LANES), F32),
-        pltpu.VMEM((2, 2, 8, 8, 8, LANES), F32),
-        pltpu.VMEM((3, 2, BOX, GRID, LANES), F32),
+        pltpu.VMEM((4, 2, 8, 8, 8, LANES), F32),
+        pltpu.VMEM((2, 8 * GRID, 2 * LANES), F32),
+        pltpu.VMEM((2, 2, BOX, GRID, LANES), F32),
+        pltpu.VMEM((2, BOX, BOX, LANES), F32),
+        pltpu.VMEM((2, GRID, 8, LANES), F32),
         pltpu.VMEM((3, BOX * BOX, 2 * LANES), BF16),
         pltpu.VMEM((3, BOX * BOX, 2 * LANES), BF16),
     ]

time: 59.1 us -> 52.7 us (0.89)
  Pallas kernels: 24.7 us -> 18.6 us
  local copies, waits for them, and re-layouts: 3.51 us -> 2.84 us
    pallas_call x1, Pallas kernels: 21.7 us -> 15.6 us  [kernel_call(): pl.pallas_call(body, out_shape=(out, out), scratch_shapes=scratch, compil...]
    unnamed x31 -> x33, local copies, waits for them, and re-layouts: 2.13 us -> 1.46 us
  transfers between devices with their start and end apart: 8 -> 8, of which waited for: 2 -> 1; matrix products, arithmetic and copies ran while one was open for 4% -> 4% of each run, Pallas kernels for 5% -> 6%
where the time goes in v4:
time: 52.7 us; the launch traced here: 52.3 us
  starting transfers between devices  26.1 us (50%)
  Pallas kernels  18.6 us (35%)
  waiting for transfers between devices  3.34 us (6%)
  local copies, waits for them, and re-layouts  2.84 us (5%)
  between operations  1.07 us (2%)
    pallas_call x1, Pallas kernels, kernel_call(): pl.pallas_call(body, out_shape=(out, out), scratch_shapes=scratch, compil...  15.6 us
    ppermute x3, starting transfers between devices, local(): lax.ppermute(mine, 'rot', [(i, (i + s) % rots) for i in range(rots)])  9.35 us
    ppermute x1, starting transfers between devices, local(): after = lax.ppermute(pack(tile[:, :HALF]), 'tx', shifts(tx, -1))  4.91 us
    ppermute x1, starting transfers between devices, local(): high = lax.ppermute(grid[:HALF], 'ty', shifts(ty, -1))  4.85 us
    ppermute x1, waiting for transfers between devices, local(): before = lax.ppermute(pack(tile[:, HALF:]), 'tx', shifts(tx, 1))  3.32 us
    pallas_call x2, Pallas kernels, prep_call(): pl.pallas_call(prep, out_shape=jax.ShapeDtypeStruct((2, BOX, GRID, LANES)...  2.99 us
    ppermute x1, starting transfers between devices, local(): low = lax.ppermute(grid[HALF:], 'ty', shifts(ty, 1))  2.72 us
    ppermute x1, starting transfers between devices, local(): lax.ppermute(far, 'ty', [(i, i + 1 - 2 * (i % 2)) for i in range(ty)])  2.31 us
  transfers between devices with their start and end apart: 8, of which 1 were waited for; matrix products, arithmetic and copies ran while one was open for 4% of the time, Pallas kernels for 6%

profile of v4, /device:TPU:7, one launch (start us, length us, event | category | flops | bytes accessed | tf_op | source)
XLA Modules:
  0.0 52.3 jit_solution(10278456704941794885)
XLA Ops:
  0.6 1.1 %constant_dynamic-slice_fusion = (f32[1,32,1024]{2,1,0:T(8,128)S(1)}, f32[32,1024]{1,0:T(8,128)S(1)}, f32[32,1024]{1,0:T(8,128)S(1)}) fusion(f32[2,32,1024]{2,1,0:T(8,128)} %param.19, s32[]{:T(128)S(6)} %select_n.3), kind=kLoop, calls=%fused_computation.10 | loop fusion | bytes 786436 | tf_op jit(solution)/shard_map/dynamic_slice | solution.py:400
  1.7 6.1 %collective-permute-start.6 = (f32[1,32,1024]{2,1,0:T(8,128)S(1)}, f32[1,32,1024]{2,1,0:T(8,128)S(1)}, u32[]{:S(2)}, u32[]{:S(2)}) collective-permute-start(f32[1,32,1024]{2,1,0:T(8,128)S(1)} %get-tuple-element.13), channel_id=1, source_target_pairs={{0,192},{64,0},{128,64},{192,128},{1,193},{65,1},{129,65},{193,129... | collective-permute-start | bytes 393224 | tf_op jit(solution)/shard_map/ppermute | solution.py:401
  7.8 1.0 %collective-permute-start.5 = (f32[1,32,1024]{2,1,0:T(8,128)S(1)}, f32[1,32,1024]{2,1,0:T(8,128)S(1)}, u32[]{:S(2)}, u32[]{:S(2)}) collective-permute-start(f32[1,32,1024]{2,1,0:T(8,128)S(1)} %get-tuple-element.13), channel_id=1, source_target_pairs={{0,128},{64,192},{128,0},{192,64},{1,129},{65,193},{129,1},{193,65... | collective-permute-start | bytes 393224 | tf_op jit(solution)/shard_map/ppermute | solution.py:401
  8.8 2.3 %collective-permute-start.4 = (f32[1,32,1024]{2,1,0:T(8,128)S(1)}, f32[1,32,1024]{2,1,0:T(8,128)S(1)}, u32[]{:S(2)}, u32[]{:S(2)}) collective-permute-start(f32[1,32,1024]{2,1,0:T(8,128)S(1)} %get-tuple-element.13), channel_id=1, source_target_pairs={{0,64},{64,128},{128,192},{192,0},{1,65},{65,129},{129,193},{193,1... | collective-permute-start | bytes 393224 | tf_op jit(solution)/shard_map/ppermute | solution.py:401
  11.1 1.3 %copy.22 = f32[32,32,64]{2,0,1:T(8,128)S(1)} copy(f32[32,32,64]{2,1,0:T(8,128)} %param.18) | data formatting | bytes 524288 | tf_op args[0]
  12.5 0.1 pad_maximum_fusion.2
  12.6 4.9 %collective-permute-start.1 = (f32[16,16,128]{2,1,0:T(8,128)S(1)}, f32[16,16,128]{2,1,0:T(8,128)S(1)}, u32[]{:S(2)}, u32[]{:S(2)}) collective-permute-start(f32[16,16,128]{2,1,0:T(8,128)S(1)} %pad_maximum_fusion.2), channel_id=1, source_target_pairs={{4,0},{8,4},{12,8},{16,12},{20,16},{24,20},{28,24},{32,28},{36,32}... | collective-permute-start | bytes 393224 | tf_op jit(solution)/shard_map/ppermute | solution.py:397
  17.5 0.1 pad_maximum_fusion.1
  17.6 1.9 %collective-permute-start = (f32[16,16,128]{2,1,0:T(8,128)S(1)}, f32[16,16,128]{2,1,0:T(8,128)S(1)}, u32[]{:S(2)}, u32[]{:S(2)}) collective-permute-start(f32[16,16,128]{2,1,0:T(8,128)S(1)} %pad_maximum_fusion.1), channel_id=1, source_target_pairs={{0,4},{4,8},{8,12},{12,16},{16,20},{20,24},{24,28},{28,32},{32,36}... | collective-permute-start | bytes 393224 | tf_op jit(solution)/shard_map/ppermute | solution.py:396
  19.6 0.0 copy-start.2
  19.6 0.0 copy-start.3
  19.6 0.0 copy-start.9
  19.6 0.0 copy-start.15
  19.6 0.0 collective-permute-done.6
  19.6 0.0 collective-permute-done.5
  19.6 0.0 collective-permute-done.4
  19.7 2.3 %collective-permute-start.7 = (f32[3,32,1024]{2,1,0:T(8,128)S(1)}, f32[3,32,1024]{2,1,0:T(8,128)S(1)}, u32[]{:S(2)}, u32[]{:S(2)}) collective-permute-start(f32[3,32,1024]{2,1,0:T(8,128)S(1)} %pad_maximum_fusion), channel_id=1, source_target_pairs={{0,1},{1,0},{2,3},{3,2},{4,5},{5,4},{6,7},{7,6},{8,9},{9,8},{10,11... | collective-permute-start | bytes 1179656 | tf_op jit(solution)/shard_map/ppermute | solution.py:403
  22.0 0.0 collective-permute-done.1
  22.0 0.1 fusion.4
  22.1 3.3 %collective-permute-done = f32[16,16,128]{2,1,0:T(8,128)S(1)} collective-permute-done((f32[16,16,128]{2,1,0:T(8,128)S(1)}, f32[16,16,128]{2,1,0:T(8,128)S(1)}, u32[]{:S(2)}, u32[]{:S(2)}) %collective-permute-start) | collective-permute-done | bytes 131104 | tf_op jit(solution)/shard_map/ppermute | solution.py:396
  25.4 0.1 fusion.3
  25.5 0.2 maximum_maximum_fusion.own_ref
  25.8 4.9 %collective-permute-start.3 = (f32[16,32,128]{2,1,0:T(8,128)S(1)}, f32[16,32,128]{2,1,0:T(8,128)S(1)}, u32[]{:S(2)}, u32[]{:S(2)}) collective-permute-start(f32[16,32,128]{2,1,0:T(8,128)S(1)} %get-tuple-element.2), channel_id=1, source_target_pairs={{1,0},{2,1},{3,2},{5,4},{6,5},{7,6},{9,8},{10,9},{11,10},{13,12},{... | collective-permute-start | bytes 786440 | tf_op jit(solution)/shard_map/ppermute | solution.py:413
  30.6 2.7 %collective-permute-start.2 = (f32[16,32,128]{2,1,0:T(8,128)S(1)}, f32[16,32,128]{2,1,0:T(8,128)S(1)}, u32[]{:S(2)}, u32[]{:S(2)}) collective-permute-start(f32[16,32,128]{2,1,0:T(8,128)S(1)} %get-tuple-element.3), channel_id=1, source_target_pairs={{0,1},{1,2},{2,3},{4,5},{5,6},{6,7},{8,9},{9,10},{10,11},{12,13},{... | collective-permute-start | bytes 786440 | tf_op jit(solution)/shard_map/ppermute | solution.py:412
  33.4 0.0 copy-done.2
  33.4 0.0 copy-done.3
  33.4 0.0 copy-done.9
  33.4 0.0 copy-done.15
  33.4 1.5 %prep.2.kern_a = f32[2,32,64,128]{3,2,1,0:T(8,128)S(1)} custom-call(f32[32,1024]{1,0:T(8,128)S(1)} %get-tuple-element.14.refs_0_, f32[32,1024]{1,0:T(8,128)S(1)} %get-tuple-element.15.refs_1_, f32[32,1024]{1,0:T(8,128)S(1)} %bitcast.18, f32[32,1024]{1,0:T(8,128)S(1)} %bitcast.17, f32[32,1024]{1,0:T(8,128)S(1)} %copy-done.9, bf16[256,512]{1,0:T(8,128)(2,1)S(1)} %copy-done.3, ...), custom_call_target="tpu_custom_call" | custom-call | flops 2000000000 | bytes 4000000 | tf_op jit(solution)/shard_map/prep/pallas_call | solution.py:421
  34.9 0.0 collective-permute-done.7
  34.9 0.0 copy-start
  35.0 0.0 copy-start.1
  35.0 0.0 copy-start.4
  35.0 0.0 copy-start.5
  35.0 0.0 copy-start.6
  35.0 0.0 copy-start.7
  35.0 0.0 copy-start.8
  35.0 0.0 copy-start.10
  35.0 0.0 copy-start.11
  35.1 0.0 copy-start.12
  35.1 0.0 copy-start.13
  35.1 0.0 copy-start.14
  35.1 1.5 %prep.3.kern_b = f32[2,32,64,128]{3,2,1,0:T(8,128)S(1)} custom-call(f32[32,1024]{1,0:T(8,128)S(1)} %bitcast.16, f32[32,1024]{1,0:T(8,128)S(1)} %get-tuple-element.12.refs_1_, f32[32,1024]{1,0:T(8,128)S(1)} %get-tuple-element.11.refs_2_, f32[32,1024]{1,0:T(8,128)S(1)} %get-tuple-element.10.refs_3_, f32[32,1024]{1,0:T(8,128)S(1)} %copy-done.9, ...), custom_call_target="tpu_custom_call" | custom-call | flops 2000000000 | bytes 4000000 | tf_op jit(solution)/shard_map/prep/pallas_call | solution.py:421
  36.6 0.0 collective-permute-done.3.after_ref
  36.6 0.0 collective-permute-done.2.before_ref
  36.6 0.0 copy-done
  36.6 0.0 copy-done.1
  36.7 15.6 %scores.1 = (f32[32,1024]{1,0:T(8,128)}, f32[32,1024]{1,0:T(8,128)}) custom-call(f32[32,32,128]{2,1,0:T(8,128)S(1)} %maximum_maximum_fusion.own_ref, f32[16,32,128]{2,1,0:T(8,128)S(1)} %collective-permute-done.2.before_ref, f32[16,32,128]{2,1,0:T(8,128)S(1)} %collective-permute-done.3.after_ref, f32[2,32,64,128]{3,2,1,0:T(8,128)S(1)} %prep.2.kern_a, ...), custom_call_target="tpu_custom_call" | custom-call | flops 10000000000 | bytes 10000000 | tf_op jit(solution)/shard_map/scores/pallas_call | solution.py:445
  (15 shorter events, 0.2 us)
Async XLA Ops:
  1.7 17.9 %collective-permute-start.6 = (f32[1,32,1024]{2,1,0:T(8,128)S(1)}, f32[1,32,1024]{2,1,0:T(8,128)S(1)}, u32[]{:S(2)}, u32[]{:S(2)}) collective-permute-start(f32[1,32,1024]{2,1,0:T(8,128)S(1)} %get-tuple-element.13), channel_id=1, source_target_pairs={{0,192},{64,0},{128,64},{192,128},{1,193},{65,1},{129,65},{193,129... | collective-permute-start | bytes 393224 | tf_op jit(solution)/shard_map/ppermute | solution.py:401
  7.8 11.8 %collective-permute-start.5 = (f32[1,32,1024]{2,1,0:T(8,128)S(1)}, f32[1,32,1024]{2,1,0:T(8,128)S(1)}, u32[]{:S(2)}, u32[]{:S(2)}) collective-permute-start(f32[1,32,1024]{2,1,0:T(8,128)S(1)} %get-tuple-element.13), channel_id=1, source_target_pairs={{0,128},{64,192},{128,0},{192,64},{1,129},{65,193},{129,1},{193,65... | collective-permute-start | bytes 393224 | tf_op jit(solution)/shard_map/ppermute | solution.py:401
  8.8 10.8 %collective-permute-start.4 = (f32[1,32,1024]{2,1,0:T(8,128)S(1)}, f32[1,32,1024]{2,1,0:T(8,128)S(1)}, u32[]{:S(2)}, u32[]{:S(2)}) collective-permute-start(f32[1,32,1024]{2,1,0:T(8,128)S(1)} %get-tuple-element.13), channel_id=1, source_target_pairs={{0,64},{64,128},{128,192},{192,0},{1,65},{65,129},{129,193},{193,1... | collective-permute-start | bytes 393224 | tf_op jit(solution)/shard_map/ppermute | solution.py:401
  12.6 9.4 %collective-permute-start.1 = (f32[16,16,128]{2,1,0:T(8,128)S(1)}, f32[16,16,128]{2,1,0:T(8,128)S(1)}, u32[]{:S(2)}, u32[]{:S(2)}) collective-permute-start(f32[16,16,128]{2,1,0:T(8,128)S(1)} %pad_maximum_fusion.2), channel_id=1, source_target_pairs={{4,0},{8,4},{12,8},{16,12},{20,16},{24,20},{28,24},{32,28},{36,32}... | collective-permute-start | bytes 393224 | tf_op jit(solution)/shard_map/ppermute | solution.py:397
  17.6 7.8 %collective-permute-start = (f32[16,16,128]{2,1,0:T(8,128)S(1)}, f32[16,16,128]{2,1,0:T(8,128)S(1)}, u32[]{:S(2)}, u32[]{:S(2)}) collective-permute-start(f32[16,16,128]{2,1,0:T(8,128)S(1)} %pad_maximum_fusion.1), channel_id=1, source_target_pairs={{0,4},{4,8},{8,12},{12,16},{16,20},{20,24},{24,28},{28,32},{32,36}... | collective-permute-start | bytes 393224 | tf_op jit(solution)/shard_map/ppermute | solution.py:396
  19.6 13.8 %copy-start.2 = (bf16[256,512]{1,0:T(8,128)(2,1)S(1)}, bf16[256,512]{1,0:T(8,128)(2,1)}, u32[]{:S(2)}) copy-start(bf16[256,512]{1,0:T(8,128)(2,1)} %constant.45.clone.refs_6_) | copy-start | bytes 786436
  19.6 13.8 %copy-start.3 = (bf16[256,512]{1,0:T(8,128)(2,1)S(1)}, bf16[256,512]{1,0:T(8,128)(2,1)}, u32[]{:S(2)}) copy-start(bf16[256,512]{1,0:T(8,128)(2,1)} %constant.44.clone.refs_5_) | copy-start | bytes 786436
  19.6 13.8 %copy-start.9 = (f32[32,1024]{1,0:T(8,128)S(1)}, f32[32,1024]{1,0:T(8,128)}, u32[]{:S(2)}) copy-start(f32[32,1024]{1,0:T(8,128)} %constant.43.clone.refs_4_) | copy-start | bytes 393220
  19.6 13.8 %copy-start.15 = (bf16[128,96]{1,0:T(8,128)(2,1)S(1)}, bf16[128,96]{1,0:T(8,128)(2,1)}, u32[]{:S(2)}) copy-start(bf16[128,96]{1,0:T(8,128)(2,1)} %constant.46.clone.refs_7_) | copy-start | bytes 73732
  19.7 15.2 %collective-permute-start.7 = (f32[3,32,1024]{2,1,0:T(8,128)S(1)}, f32[3,32,1024]{2,1,0:T(8,128)S(1)}, u32[]{:S(2)}, u32[]{:S(2)}) collective-permute-start(f32[3,32,1024]{2,1,0:T(8,128)S(1)} %pad_maximum_fusion), channel_id=1, source_target_pairs={{0,1},{1,0},{2,3},{3,2},{4,5},{5,4},{6,7},{7,6},{8,9},{9,8},{10,11... | collective-permute-start | bytes 1179656 | tf_op jit(solution)/shard_map/ppermute | solution.py:403
  25.8 10.8 %collective-permute-start.3 = (f32[16,32,128]{2,1,0:T(8,128)S(1)}, f32[16,32,128]{2,1,0:T(8,128)S(1)}, u32[]{:S(2)}, u32[]{:S(2)}) collective-permute-start(f32[16,32,128]{2,1,0:T(8,128)S(1)} %get-tuple-element.2), channel_id=1, source_target_pairs={{1,0},{2,1},{3,2},{5,4},{6,5},{7,6},{9,8},{10,9},{11,10},{13,12},{... | collective-permute-start | bytes 786440 | tf_op jit(solution)/shard_map/ppermute | solution.py:413
  30.6 6.0 %collective-permute-start.2 = (f32[16,32,128]{2,1,0:T(8,128)S(1)}, f32[16,32,128]{2,1,0:T(8,128)S(1)}, u32[]{:S(2)}, u32[]{:S(2)}) collective-permute-start(f32[16,32,128]{2,1,0:T(8,128)S(1)} %get-tuple-element.3), channel_id=1, source_target_pairs={{0,1},{1,2},{2,3},{4,5},{5,6},{6,7},{8,9},{9,10},{10,11},{12,13},{... | collective-permute-start | bytes 786440 | tf_op jit(solution)/shard_map/ppermute | solution.py:412
  34.9 1.7 %copy-start = (f32[64,32,128]{2,1,0:T(8,128)S(1)}, f32[64,32,128]{2,1,0:T(8,128)}, u32[]{:S(2)}) copy-start(f32[64,32,128]{2,1,0:T(8,128)} %constant.48.clone.mask_im) | copy-start | bytes 3145732
  35.0 1.7 %copy-start.1 = (f32[64,32,128]{2,1,0:T(8,128)S(1)}, f32[64,32,128]{2,1,0:T(8,128)}, u32[]{:S(2)}) copy-start(f32[64,32,128]{2,1,0:T(8,128)} %constant.47.clone.mask_re) | copy-start | bytes 3145732
  35.0 1.7 %copy-start.4 = (bf16[256,256]{1,0:T(8,128)(2,1)S(1)}, bf16[256,256]{1,0:T(8,128)(2,1)}, u32[]{:S(2)}) copy-start(bf16[256,256]{1,0:T(8,128)(2,1)} %constant.58.clone.copies_ref) | copy-start | bytes 393220
  35.0 1.7 %copy-start.5 = (bf16[256,256]{1,0:T(8,128)(2,1)S(1)}, bf16[256,256]{1,0:T(8,128)(2,1)}, u32[]{:S(2)}) copy-start(bf16[256,256]{1,0:T(8,128)(2,1)} %constant.57.clone.bm_lo) | copy-start | bytes 393220
  35.0 1.7 %copy-start.6 = (bf16[256,256]{1,0:T(8,128)(2,1)S(1)}, bf16[256,256]{1,0:T(8,128)(2,1)}, u32[]{:S(2)}) copy-start(bf16[256,256]{1,0:T(8,128)(2,1)} %constant.56.clone.bm_hi) | copy-start | bytes 393220
  35.0 1.7 %copy-start.7 = (bf16[256,256]{1,0:T(8,128)(2,1)S(1)}, bf16[256,256]{1,0:T(8,128)(2,1)}, u32[]{:S(2)}) copy-start(bf16[256,256]{1,0:T(8,128)(2,1)} %constant.54.clone.bz_two) | copy-start | bytes 393220
  35.0 1.7 %copy-start.8 = (bf16[256,256]{1,0:T(8,128)(2,1)S(1)}, bf16[256,256]{1,0:T(8,128)(2,1)}, u32[]{:S(2)}) copy-start(bf16[256,256]{1,0:T(8,128)(2,1)} %constant.49.clone.tz_two) | copy-start | bytes 393220
  35.0 1.7 %copy-start.10 = (bf16[256,128]{1,0:T(8,128)(2,1)S(1)}, bf16[256,128]{1,0:T(8,128)(2,1)}, u32[]{:S(2)}) copy-start(bf16[256,128]{1,0:T(8,128)(2,1)} %constant.55.clone.bz_hi) | copy-start | bytes 196612
  35.0 1.7 %copy-start.11 = (bf16[128,256]{1,0:T(8,128)(2,1)S(1)}, bf16[128,256]{1,0:T(8,128)(2,1)}, u32[]{:S(2)}) copy-start(bf16[128,256]{1,0:T(8,128)(2,1)} %constant.50.clone.tz_lo) | copy-start | bytes 196612
  35.1 1.7 %copy-start.12 = (bf16[128,96]{1,0:T(8,128)(2,1)S(1)}, bf16[128,96]{1,0:T(8,128)(2,1)}, u32[]{:S(2)}) copy-start(bf16[128,96]{1,0:T(8,128)(2,1)} %constant.53.clone.inv_m_ref) | copy-start | bytes 73732
  35.1 1.6 %copy-start.13 = (bf16[64,192]{1,0:T(8,128)(2,1)S(1)}, bf16[64,192]{1,0:T(8,128)(2,1)}, u32[]{:S(2)}) copy-start(bf16[64,192]{1,0:T(8,128)(2,1)} %constant.52.clone.inv_ref) | copy-start | bytes 73732
  35.1 1.6 %copy-start.14 = (bf16[64,192]{1,0:T(8,128)(2,1)S(1)}, bf16[64,192]{1,0:T(8,128)(2,1)}, u32[]{:S(2)}) copy-start(bf16[64,192]{1,0:T(8,128)(2,1)} %constant.51.clone.fwd_ref) | copy-start | bytes 73732

commit v5 on v4

--- a/solution.py
+++ b/solution.py
@@ -24,6 +24,11 @@
     hi = table.astype(ml_dtypes.bfloat16)
     lo = (table - hi.astype(np.float64)).astype(ml_dtypes.bfloat16)
     return hi, lo
+
+
+def stacked(table):
+    hi, lo = halves(table)
+    return np.concatenate([hi, hi, lo], axis=0)
 
 
 def wave(out_pos, in_pos):
@@ -98,16 +103,15 @@
         mask,
         mask_re,
         mask_im,
-        np.concatenate([tomo_hi, tomo_hi], axis=0),
-        tomo_lo,
-        *halves(kern_z),
+        np.concatenate([tomo_hi, tomo_hi, tomo_lo], axis=0),
+        stacked(kern_z),
         left_table(freq[:BOX], np.arange(GRID), 1.0),
         left_table(freq, np.arange(BOX), 1.0),
         left_table(np.arange(BOX), freq, scale),
         np.concatenate([left_table(np.arange(BOX) + centre, f, scale) for f in (freq[:BOX], freq[BOX:])], axis=0),
         np.concatenate([back_hi, back_lo], axis=1),
         back_hi,
-        *halves(back_mask_z),
+        stacked(back_mask_z),
         copies.astype(ml_dtypes.bfloat16),
     )
 
@@ -121,9 +125,8 @@
     return jnp.dot(a, b, preferred_element_type=F32)
 
 
-def right_dot(x, w_hi, w_lo):
-    hi, lo = split(x)
-    return dot(hi, w_hi) + dot(lo, w_hi) + dot(hi, w_lo)
+def right_dot(hi, lo, table):
+    return dot(jnp.concatenate([hi, lo, hi], axis=1), table)
 
 
 def left_dot(table, x, sign):
@@ -197,7 +200,7 @@
 
 
 def prep(*refs):
-    rotations, (mask_ref, kz_hi, kz_lo, ker_ref, out_ref) = refs[:4], refs[4:]
+    rotations, (mask_ref, kz_ref, ker_ref, out_ref) = refs[:4], refs[4:]
     filled = float(sphere_np().sum())
     low_half = lax.broadcasted_iota(jnp.int32, (1, LANES), 1) < GRID
     mask = mask_ref[...]
@@ -216,7 +219,7 @@
             jnp.concatenate([jnp.where(low_half, tile[r], far[r + 1]) for r in (0, 2)], axis=1),
             jnp.concatenate([jnp.where(low_half, far[r], tile[r + 1]) for r in (0, 2)], axis=1),
         ]
-    out = right_dot(jnp.concatenate(rows, axis=0), kz_hi[...], kz_lo[...])
+    out = right_dot(*split(jnp.concatenate(rows, axis=0)), kz_ref[...])
     for j in range(BOX):
         x = out[BOX * (j // 2) : BOX * (j // 2 + 1), 256 * (j % 2) : 256 * (j % 2 + 1)]
         re, im = left_dot(ker_ref[...], x, 1)
@@ -235,7 +238,7 @@
 
 def body(
     own_ref, before_ref, after_ref, kern_a, kern_b,
-    mask_re, mask_im, tz_two, tz_lo, fwd_ref, inv_ref, inv_m_ref, bz_two, bz_hi, bm_hi, bm_lo, copies_ref,
+    mask_re, mask_im, tz_ref, fwd_ref, inv_ref, inv_m_ref, bz_two, bz_hi, bm_ref, copies_ref,
     top_ref, next_ref,
     spec, kspec, fspec, work, slab, back, back_m, plain, u_hi, u_lo,
 ):
@@ -270,7 +273,7 @@
         upper = jnp.where(low_half, pltpu.roll(one, GRID, 1), two)
         rows = [v[BOX * e : BOX * (e + 1)] for e in range(8) for v in (lower, upper)]
         hi, lo = split(jnp.concatenate(rows, axis=0))
-        slab[step % 2] = dot(jnp.concatenate([hi, lo], axis=1), tz_two[...]) + dot(hi, tz_lo[...])
+        slab[step % 2] = right_dot(hi, lo, tz_ref[...])
 
     along_z(0)
     for step in range(8):
@@ -360,8 +363,7 @@
     quarter = lane // BOX
     for part in range(2):
         rows = pl.ds(512 * part, 512)
-        hi, lo = u_hi[2, rows, :], u_lo[2, rows, :]
-        sums = dot(hi, bm_hi[...]) + dot(lo, bm_hi[...]) + dot(hi, bm_lo[...])
+        sums = right_dot(u_hi[2, rows, :], u_lo[2, rows, :], bm_ref[...])
         mean = sums[:, :LANES] / filled
         var = jnp.maximum(sums[:, LANES:] / filled - mean * mean, 0.0)
         scale = 1.0 / (np.float32(np.sqrt(filled)) * jnp.sqrt(var + EPSILON))
@@ -393,8 +395,9 @@
     def unpack(part):
         return jnp.concatenate([part[:, :, :GRID], part[:, :, GRID:]], axis=0)
 
-    before = lax.ppermute(pack(tile[:, HALF:]), "tx", shifts(tx, 1))
-    after = lax.ppermute(pack(tile[:, :HALF]), "tx", shifts(tx, -1))
+    up, down, templates = lax.optimization_barrier((pack(tile[:, HALF:]), pack(tile[:, :HALF]), templates))
+    before = lax.ppermute(up, "tx", shifts(tx, 1))
+    after = lax.ppermute(down, "tx", shifts(tx, -1))
 
     core = lax.rem(lax.axis_index("ty"), 2)
     mine = lax.dynamic_slice_in_dim(templates, core, 1, axis=0)
@@ -417,14 +420,14 @@
 
 
 def prep_call(*four_templates):
-    mask, _, _, _, _, kz_hi, kz_lo, _, ker = tables()[:9]
+    mask, _, _, _, kz, _, ker = tables()[:7]
     return pl.pallas_call(
         prep,
         out_shape=jax.ShapeDtypeStruct((2, BOX, GRID, LANES), F32),
         compiler_params=pltpu.CompilerParams(vmem_limit_bytes=16 * 1024 * 1024),
         cost_estimate=pl.CostEstimate(flops=2 * 10**9, bytes_accessed=4 * 10**6, transcendentals=0),
         name="prep",
-    )(*four_templates, *[jnp.asarray(t) for t in (mask, kz_hi, kz_lo, ker)])
+    )(*four_templates, *[jnp.asarray(t) for t in (mask, kz, ker)])
 
 
 def kernel_call(grid, low, high, first, second):
@@ -441,7 +444,7 @@
         pltpu.VMEM((3, BOX * BOX, 2 * LANES), BF16),
         pltpu.VMEM((3, BOX * BOX, 2 * LANES), BF16),
     ]
-    _, mask_re, mask_im, tz_hi, tz_lo, _, _, fwd, _, inv, inv_m, *back = tables()
+    _, mask_re, mask_im, tz, _, fwd, _, inv, inv_m, *back = tables()
     return pl.pallas_call(
         body,
         out_shape=(out, out),
@@ -449,7 +452,7 @@
         compiler_params=pltpu.CompilerParams(vmem_limit_bytes=40 * 1024 * 1024),
         cost_estimate=pl.CostEstimate(flops=10**10, bytes_accessed=10**7, transcendentals=0),
         name="scores",
-    )(grid, low, high, first, second, *[jnp.asarray(t) for t in (mask_re, mask_im, tz_hi, tz_lo, fwd, inv, inv_m, *back)])
+    )(grid, low, high, first, second, *[jnp.asarray(t) for t in (mask_re, mask_im, tz, fwd, inv, inv_m, *back)])
 
 
 def solution(mesh):

time: 52.7 us -> 49.3 us (0.935)
  the two profiles are of different devices: /device:TPU:7 before, /device:TPU:56 now
where the time goes in v5:
time: 49.3 us; the launch traced here: 49.1 us
  starting transfers between devices  19.7 us (40%)
  Pallas kernels  18.4 us (37%)
  waiting for transfers between devices  7.75 us (16%)
  local copies, waits for them, and re-layouts  1.83 us (4%)
  between operations  1.01 us (2%)
    pallas_call x1, Pallas kernels, kernel_call(): pl.pallas_call(body, out_shape=(out, out), scratch_shapes=scratch, compil...  15.4 us
    ppermute x3, starting transfers between devices, local(): lax.ppermute(mine, 'rot', [(i, (i + s) % rots) for i in range(rots)])  9.29 us
    ppermute x3, waiting for transfers between devices, local(): lax.ppermute(mine, 'rot', [(i, (i + s) % rots) for i in range(rots)])  4.09 us
    ppermute x1, starting transfers between devices, local(): before = lax.ppermute(up, 'tx', shifts(tx, 1))  3.05 us
    pallas_call x2, Pallas kernels, prep_call(): pl.pallas_call(prep, out_shape=jax.ShapeDtypeStruct((2, BOX, GRID, LANES)...  2.96 us
    ppermute x1, starting transfers between devices, local(): after = lax.ppermute(down, 'tx', shifts(tx, -1))  2.78 us
    ppermute x1, starting transfers between devices, local(): low = lax.ppermute(grid[HALF:], 'ty', shifts(ty, 1))  2.6 us
    ppermute x1, starting transfers between devices, local(): high = lax.ppermute(grid[:HALF], 'ty', shifts(ty, -1))  1.92 us
  transfers between devices with their start and end apart: 8, of which 4 were waited for; matrix products, arithmetic and copies ran while one was open for 1% of the time, Pallas kernels for 6%

profile of v5, /device:TPU:56, one launch (start us, length us, event | category | flops | bytes accessed | tf_op | source)
XLA Modules:
  0.0 49.1 jit_solution(12119809874675731780)
XLA Ops:
  0.6 0.0 copy-start.13
  0.6 1.4 %copy.19 = f32[32,32,64]{2,0,1:T(8,128)S(1)} copy(f32[32,32,64]{2,1,0:T(8,128)} %param.15) | data formatting | bytes 524288 | tf_op args[0]
  2.1 0.1 pad_maximum_fusion.1
  2.2 0.0 copy-done.13
  2.3 5.5 %collective-permute-start.6 = (f32[1,32,1024]{2,1,0:T(8,128)S(1)}, f32[1,32,1024]{2,1,0:T(8,128)S(1)}, u32[]{:S(2)}, u32[]{:S(2)}) collective-permute-start(f32[1,32,1024]{2,1,0:T(8,128)S(1)} %get-tuple-element.19), channel_id=1, source_target_pairs={{0,192},{64,0},{128,64},{192,128},{1,193},{65,1},{129,65},{193,129... | collective-permute-start | bytes 393224 | tf_op jit(solution)/shard_map/ppermute | solution.py:404
  7.8 1.4 %collective-permute-start.5 = (f32[1,32,1024]{2,1,0:T(8,128)S(1)}, f32[1,32,1024]{2,1,0:T(8,128)S(1)}, u32[]{:S(2)}, u32[]{:S(2)}) collective-permute-start(f32[1,32,1024]{2,1,0:T(8,128)S(1)} %get-tuple-element.19), channel_id=1, source_target_pairs={{0,128},{64,192},{128,0},{192,64},{1,129},{65,193},{129,1},{193,65... | collective-permute-start | bytes 393224 | tf_op jit(solution)/shard_map/ppermute | solution.py:404
  9.2 2.4 %collective-permute-start.4 = (f32[1,32,1024]{2,1,0:T(8,128)S(1)}, f32[1,32,1024]{2,1,0:T(8,128)S(1)}, u32[]{:S(2)}, u32[]{:S(2)}) collective-permute-start(f32[1,32,1024]{2,1,0:T(8,128)S(1)} %get-tuple-element.19), channel_id=1, source_target_pairs={{0,64},{64,128},{128,192},{192,0},{1,65},{65,129},{129,193},{193,1... | collective-permute-start | bytes 393224 | tf_op jit(solution)/shard_map/ppermute | solution.py:404
  11.6 3.0 %collective-permute-start = (f32[16,16,128]{2,1,0:T(8,128)S(1)}, f32[16,16,128]{2,1,0:T(8,128)S(1)}, u32[]{:S(2)}, u32[]{:S(2)}) collective-permute-start(f32[16,16,128]{2,1,0:T(8,128)S(1)} %get-tuple-element.5), channel_id=1, source_target_pairs={{0,4},{4,8},{8,12},{12,16},{16,20},{20,24},{24,28},{28,32},{32,36}... | collective-permute-start | bytes 393224 | tf_op jit(solution)/shard_map/ppermute | solution.py:399
  14.6 2.8 %collective-permute-start.1 = (f32[16,16,128]{2,1,0:T(8,128)S(1)}, f32[16,16,128]{2,1,0:T(8,128)S(1)}, u32[]{:S(2)}, u32[]{:S(2)}) collective-permute-start(f32[16,16,128]{2,1,0:T(8,128)S(1)} %get-tuple-element.6), channel_id=1, source_target_pairs={{4,0},{8,4},{12,8},{16,12},{20,16},{24,20},{28,24},{32,28},{36,32}... | collective-permute-start | bytes 393224 | tf_op jit(solution)/shard_map/ppermute | solution.py:400
  17.5 0.0 copy-start.2
  17.5 0.0 copy-start.7
  17.5 0.0 copy-start.12
  17.5 0.0 collective-permute-done.6
  17.5 3.6 %collective-permute-done.5 = f32[1,32,1024]{2,1,0:T(8,128)S(1)} collective-permute-done((f32[1,32,1024]{2,1,0:T(8,128)S(1)}, f32[1,32,1024]{2,1,0:T(8,128)S(1)}, u32[]{:S(2)}, u32[]{:S(2)}) %collective-permute-start.5) | collective-permute-done | bytes 131104 | tf_op jit(solution)/shard_map/ppermute | solution.py:404
  21.1 0.5 %collective-permute-done.4 = f32[1,32,1024]{2,1,0:T(8,128)S(1)} collective-permute-done((f32[1,32,1024]{2,1,0:T(8,128)S(1)}, f32[1,32,1024]{2,1,0:T(8,128)S(1)}, u32[]{:S(2)}, u32[]{:S(2)}) %collective-permute-start.4) | collective-permute-done | bytes 131104 | tf_op jit(solution)/shard_map/ppermute | solution.py:404
  21.6 0.1 collective-permute-start.7
  21.7 0.0 collective-permute-done
  21.7 0.1 fusion.3
  21.8 1.8 %collective-permute-done.1 = f32[16,16,128]{2,1,0:T(8,128)S(1)} collective-permute-done((f32[16,16,128]{2,1,0:T(8,128)S(1)}, f32[16,16,128]{2,1,0:T(8,128)S(1)}, u32[]{:S(2)}, u32[]{:S(2)}) %collective-permute-start.1) | collective-permute-done | bytes 131104 | tf_op jit(solution)/shard_map/ppermute | solution.py:400
  23.6 0.1 fusion.4
  23.7 0.2 maximum_maximum_fusion.own_ref
  24.0 1.9 %collective-permute-start.3 = (f32[16,32,128]{2,1,0:T(8,128)S(1)}, f32[16,32,128]{2,1,0:T(8,128)S(1)}, u32[]{:S(2)}, u32[]{:S(2)}) collective-permute-start(f32[16,32,128]{2,1,0:T(8,128)S(1)} %get-tuple-element.8), channel_id=1, source_target_pairs={{1,0},{2,1},{3,2},{5,4},{6,5},{7,6},{9,8},{10,9},{11,10},{13,12},{... | collective-permute-start | bytes 786440 | tf_op jit(solution)/shard_map/ppermute | solution.py:416
  25.9 2.6 %collective-permute-start.2 = (f32[16,32,128]{2,1,0:T(8,128)S(1)}, f32[16,32,128]{2,1,0:T(8,128)S(1)}, u32[]{:S(2)}, u32[]{:S(2)}) collective-permute-start(f32[16,32,128]{2,1,0:T(8,128)S(1)} %get-tuple-element.9), channel_id=1, source_target_pairs={{0,1},{1,2},{2,3},{4,5},{5,6},{6,7},{8,9},{9,10},{10,11},{12,13},{... | collective-permute-start | bytes 786440 | tf_op jit(solution)/shard_map/ppermute | solution.py:415
  28.5 0.0 copy-done.2
  28.5 0.0 copy-done.7
  28.5 0.0 copy-done.12
  28.5 1.5 %prep.2.kern_a = f32[2,32,64,128]{3,2,1,0:T(8,128)S(1)} custom-call(f32[32,1024]{1,0:T(8,128)S(1)} %get-tuple-element.21.refs_0_, f32[32,1024]{1,0:T(8,128)S(1)} %get-tuple-element.20.refs_1_, f32[32,1024]{1,0:T(8,128)S(1)} %bitcast.18, f32[32,1024]{1,0:T(8,128)S(1)} %bitcast.17, f32[32,1024]{1,0:T(8,128)S(1)} %copy-done.7, bf16[768,512]{1,0:T(8,128)(2,1)S(1)} %copy-done.2, ...), custom_call_target="tpu_custom_call" | custom-call | flops 2000000000 | bytes 4000000 | tf_op jit(solution)/shard_map/prep/pallas_call | solution.py:424
  30.0 0.0 collective-permute-done.7
  30.1 0.0 copy-start
  30.1 0.0 copy-start.1
  30.1 0.0 copy-start.3
  30.1 0.0 copy-start.4
  30.1 0.0 copy-start.5
  30.1 0.0 copy-start.6
  30.1 0.0 copy-start.8
  30.1 0.0 copy-start.9
  30.2 0.0 copy-start.10
  30.2 0.0 copy-start.11
  30.2 1.5 %prep.3.kern_b = f32[2,32,64,128]{3,2,1,0:T(8,128)S(1)} custom-call(f32[32,1024]{1,0:T(8,128)S(1)} %bitcast.16, f32[32,1024]{1,0:T(8,128)S(1)} %get-tuple-element.18.refs_1_, f32[32,1024]{1,0:T(8,128)S(1)} %get-tuple-element.17.refs_2_, f32[32,1024]{1,0:T(8,128)S(1)} %get-tuple-element.16.refs_3_, f32[32,1024]{1,0:T(8,128)S(1)} %copy-done.7, ...), custom_call_target="tpu_custom_call" | custom-call | flops 2000000000 | bytes 4000000 | tf_op jit(solution)/shard_map/prep/pallas_call | solution.py:424
  31.7 0.0 collective-permute-done.3.after_ref
  31.7 1.9 %collective-permute-done.2.before_ref = f32[16,32,128]{2,1,0:T(8,128)S(1)} collective-permute-done((f32[16,32,128]{2,1,0:T(8,128)S(1)}, f32[16,32,128]{2,1,0:T(8,128)S(1)}, u32[]{:S(2)}, u32[]{:S(2)}) %collective-permute-start.2) | collective-permute-done | bytes 262176 | tf_op jit(solution)/shard_map/ppermute | solution.py:415
  33.6 0.0 copy-done
  33.6 0.0 copy-done.1
  33.6 0.0 copy-done.3
  33.6 0.0 copy-done.4
  33.6 0.0 copy-done.5
  33.6 0.0 copy-done.6
  33.7 15.4 %scores.1 = (f32[32,1024]{1,0:T(8,128)}, f32[32,1024]{1,0:T(8,128)}) custom-call(f32[32,32,128]{2,1,0:T(8,128)S(1)} %maximum_maximum_fusion.own_ref, f32[16,32,128]{2,1,0:T(8,128)S(1)} %collective-permute-done.2.before_ref, f32[16,32,128]{2,1,0:T(8,128)S(1)} %collective-permute-done.3.after_ref, f32[2,32,64,128]{3,2,1,0:T(8,128)S(1)} %prep.2.kern_a, ...), custom_call_target="tpu_custom_call" | custom-call | flops 10000000000 | bytes 10000000 | tf_op jit(solution)/shard_map/scores/pallas_call | solution.py:448
  (10 shorter events, 0.2 us)
Async XLA Ops:
  0.6 1.6 %copy-start.13 = (f32[2,32,1024]{2,1,0:T(8,128)S(1)}, f32[2,32,1024]{2,1,0:T(8,128)}, u32[]{:S(2)}) copy-start(f32[2,32,1024]{2,1,0:T(8,128)} %param.16) | copy-start | bytes 786436
  2.3 15.2 %collective-permute-start.6 = (f32[1,32,1024]{2,1,0:T(8,128)S(1)}, f32[1,32,1024]{2,1,0:T(8,128)S(1)}, u32[]{:S(2)}, u32[]{:S(2)}) collective-permute-start(f32[1,32,1024]{2,1,0:T(8,128)S(1)} %get-tuple-element.19), channel_id=1, source_target_pairs={{0,192},{64,0},{128,64},{192,128},{1,193},{65,1},{129,65},{193,129... | collective-permute-start | bytes 393224 | tf_op jit(solution)/shard_map/ppermute | solution.py:404
  7.8 13.3 %collective-permute-start.5 = (f32[1,32,1024]{2,1,0:T(8,128)S(1)}, f32[1,32,1024]{2,1,0:T(8,128)S(1)}, u32[]{:S(2)}, u32[]{:S(2)}) collective-permute-start(f32[1,32,1024]{2,1,0:T(8,128)S(1)} %get-tuple-element.19), channel_id=1, source_target_pairs={{0,128},{64,192},{128,0},{192,64},{1,129},{65,193},{129,1},{193,65... | collective-permute-start | bytes 393224 | tf_op jit(solution)/shard_map/ppermute | solution.py:404
  9.2 12.4 %collective-permute-start.4 = (f32[1,32,1024]{2,1,0:T(8,128)S(1)}, f32[1,32,1024]{2,1,0:T(8,128)S(1)}, u32[]{:S(2)}, u32[]{:S(2)}) collective-permute-start(f32[1,32,1024]{2,1,0:T(8,128)S(1)} %get-tuple-element.19), channel_id=1, source_target_pairs={{0,64},{64,128},{128,192},{192,0},{1,65},{65,129},{129,193},{193,1... | collective-permute-start | bytes 393224 | tf_op jit(solution)/shard_map/ppermute | solution.py:404
  11.6 10.2 %collective-permute-start = (f32[16,16,128]{2,1,0:T(8,128)S(1)}, f32[16,16,128]{2,1,0:T(8,128)S(1)}, u32[]{:S(2)}, u32[]{:S(2)}) collective-permute-start(f32[16,16,128]{2,1,0:T(8,128)S(1)} %get-tuple-element.5), channel_id=1, source_target_pairs={{0,4},{4,8},{8,12},{12,16},{16,20},{20,24},{24,28},{28,32},{32,36}... | collective-permute-start | bytes 393224 | tf_op jit(solution)/shard_map/ppermute | solution.py:399
  14.6 9.0 %collective-permute-start.1 = (f32[16,16,128]{2,1,0:T(8,128)S(1)}, f32[16,16,128]{2,1,0:T(8,128)S(1)}, u32[]{:S(2)}, u32[]{:S(2)}) collective-permute-start(f32[16,16,128]{2,1,0:T(8,128)S(1)} %get-tuple-element.6), channel_id=1, source_target_pairs={{4,0},{8,4},{12,8},{16,12},{20,16},{24,20},{28,24},{32,28},{36,32}... | collective-permute-start | bytes 393224 | tf_op jit(solution)/shard_map/ppermute | solution.py:400
  17.5 11.0 %copy-start.2 = (bf16[768,512]{1,0:T(8,128)(2,1)S(1)}, bf16[768,512]{1,0:T(8,128)(2,1)}, u32[]{:S(2)}) copy-start(bf16[768,512]{1,0:T(8,128)(2,1)} %constant.38.clone.refs_5_) | copy-start | bytes 2359300
  17.5 11.0 %copy-start.7 = (f32[32,1024]{1,0:T(8,128)S(1)}, f32[32,1024]{1,0:T(8,128)}, u32[]{:S(2)}) copy-start(f32[32,1024]{1,0:T(8,128)} %constant.37.clone.refs_4_) | copy-start | bytes 393220
  17.5 11.0 %copy-start.12 = (bf16[128,96]{1,0:T(8,128)(2,1)S(1)}, bf16[128,96]{1,0:T(8,128)(2,1)}, u32[]{:S(2)}) copy-start(bf16[128,96]{1,0:T(8,128)(2,1)} %constant.39.clone.refs_6_) | copy-start | bytes 73732
  21.6 8.4 %collective-permute-start.7 = (f32[3,32,1024]{2,1,0:T(8,128)S(1)}, f32[3,32,1024]{2,1,0:T(8,128)S(1)}, u32[]{:S(2)}, u32[]{:S(2)}) collective-permute-start(f32[3,32,1024]{2,1,0:T(8,128)S(1)} %pad_maximum_fusion), channel_id=1, source_target_pairs={{0,1},{1,0},{2,3},{3,2},{4,5},{5,4},{6,7},{7,6},{8,9},{9,8},{10,11... | collective-permute-start | bytes 1179656 | tf_op jit(solution)/shard_map/ppermute | solution.py:406
  24.0 7.7 %collective-permute-start.3 = (f32[16,32,128]{2,1,0:T(8,128)S(1)}, f32[16,32,128]{2,1,0:T(8,128)S(1)}, u32[]{:S(2)}, u32[]{:S(2)}) collective-permute-start(f32[16,32,128]{2,1,0:T(8,128)S(1)} %get-tuple-element.8), channel_id=1, source_target_pairs={{1,0},{2,1},{3,2},{5,4},{6,5},{7,6},{9,8},{10,9},{11,10},{13,12},{... | collective-permute-start | bytes 786440 | tf_op jit(solution)/shard_map/ppermute | solution.py:416
  25.9 7.7 %collective-permute-start.2 = (f32[16,32,128]{2,1,0:T(8,128)S(1)}, f32[16,32,128]{2,1,0:T(8,128)S(1)}, u32[]{:S(2)}, u32[]{:S(2)}) collective-permute-start(f32[16,32,128]{2,1,0:T(8,128)S(1)} %get-tuple-element.9), channel_id=1, source_target_pairs={{0,1},{1,2},{2,3},{4,5},{5,6},{6,7},{8,9},{9,10},{10,11},{12,13},{... | collective-permute-start | bytes 786440 | tf_op jit(solution)/shard_map/ppermute | solution.py:415
  30.1 3.5 %copy-start = (f32[64,32,128]{2,1,0:T(8,128)S(1)}, f32[64,32,128]{2,1,0:T(8,128)}, u32[]{:S(2)}) copy-start(f32[64,32,128]{2,1,0:T(8,128)} %constant.41.clone.mask_im) | copy-start | bytes 3145732
  30.1 3.5 %copy-start.1 = (f32[64,32,128]{2,1,0:T(8,128)S(1)}, f32[64,32,128]{2,1,0:T(8,128)}, u32[]{:S(2)}) copy-start(f32[64,32,128]{2,1,0:T(8,128)} %constant.40.clone.mask_re) | copy-start | bytes 3145732
  30.1 3.5 %copy-start.3 = (bf16[768,256]{1,0:T(8,128)(2,1)S(1)}, bf16[768,256]{1,0:T(8,128)(2,1)}, u32[]{:S(2)}) copy-start(bf16[768,256]{1,0:T(8,128)(2,1)} %constant.48.clone.bm_ref) | copy-start | bytes 1179652
  30.1 3.5 %copy-start.4 = (bf16[384,256]{1,0:T(8,128)(2,1)S(1)}, bf16[384,256]{1,0:T(8,128)(2,1)}, u32[]{:S(2)}) copy-start(bf16[384,256]{1,0:T(8,128)(2,1)} %constant.42.clone.tz_ref) | copy-start | bytes 589828
  30.1 3.5 %copy-start.5 = (bf16[256,256]{1,0:T(8,128)(2,1)S(1)}, bf16[256,256]{1,0:T(8,128)(2,1)}, u32[]{:S(2)}) copy-start(bf16[256,256]{1,0:T(8,128)(2,1)} %constant.49.clone.copies_ref) | copy-start | bytes 393220
  30.1 3.5 %copy-start.6 = (bf16[256,256]{1,0:T(8,128)(2,1)S(1)}, bf16[256,256]{1,0:T(8,128)(2,1)}, u32[]{:S(2)}) copy-start(bf16[256,256]{1,0:T(8,128)(2,1)} %constant.46.clone.bz_two) | copy-start | bytes 393220
  30.1 3.5 %copy-start.8 = (bf16[256,128]{1,0:T(8,128)(2,1)S(1)}, bf16[256,128]{1,0:T(8,128)(2,1)}, u32[]{:S(2)}) copy-start(bf16[256,128]{1,0:T(8,128)(2,1)} %constant.47.clone.bz_hi) | copy-start | bytes 196612
  30.1 3.5 %copy-start.9 = (bf16[128,96]{1,0:T(8,128)(2,1)S(1)}, bf16[128,96]{1,0:T(8,128)(2,1)}, u32[]{:S(2)}) copy-start(bf16[128,96]{1,0:T(8,128)(2,1)} %constant.45.clone.inv_m_ref) | copy-start | bytes 73732
  30.2 3.5 %copy-start.10 = (bf16[64,192]{1,0:T(8,128)(2,1)S(1)}, bf16[64,192]{1,0:T(8,128)(2,1)}, u32[]{:S(2)}) copy-start(bf16[64,192]{1,0:T(8,128)(2,1)} %constant.44.clone.inv_ref) | copy-start | bytes 73732
  30.2 3.5 %copy-start.11 = (bf16[64,192]{1,0:T(8,128)(2,1)S(1)}, bf16[64,192]{1,0:T(8,128)(2,1)}, u32[]{:S(2)}) copy-start(bf16[64,192]{1,0:T(8,128)(2,1)} %constant.43.clone.fwd_ref) | copy-start | bytes 73732

commit v6 on v5

--- a/solution.py
+++ b/solution.py
@@ -240,7 +240,7 @@
     own_ref, before_ref, after_ref, kern_a, kern_b,
     mask_re, mask_im, tz_ref, fwd_ref, inv_ref, inv_m_ref, bz_two, bz_hi, bm_ref, copies_ref,
     top_ref, next_ref,
-    spec, kspec, fspec, work, slab, back, back_m, plain, u_hi, u_lo,
+    spec, kspec, fspec, work, slab, back, back_m, plain, u_hi, u_lo, scales,
 ):
     filled = float(sphere_np().sum())
     lane = lax.broadcasted_iota(jnp.int32, (1, LANES), 1)
@@ -343,6 +343,13 @@
         u_hi[s, rows, :] = hi
         u_lo[s, rows, :] = lo
 
+    def divisors(step):
+        rows = pl.ds(pl.multiple_of(step * LANES, LANES), LANES)
+        sums = right_dot(u_hi[2, rows, :], u_lo[2, rows, :], bm_ref[...])
+        mean = sums[:, :LANES] / filled
+        var = jnp.maximum(sums[:, LANES:] / filled - mean * mean, 0.0)
+        scales[rows, :] = 1.0 / (np.float32(np.sqrt(filled)) * jnp.sqrt(var + EPSILON))
+
     for g, s in ((0, 2), (1, 0)):
 
         @pl.loop(0, 8, unroll=4)
@@ -352,6 +359,8 @@
                 product_along_y(at, g, k1)
                 if k1 % 2:
                     along_x(4 * step + k1 // 2, s)
+            if g == 1:
+                divisors(step)
             finish(back.at[g], at, g)
 
     for y in range(BOX):
@@ -363,10 +372,7 @@
     quarter = lane // BOX
     for part in range(2):
         rows = pl.ds(512 * part, 512)
-        sums = right_dot(u_hi[2, rows, :], u_lo[2, rows, :], bm_ref[...])
-        mean = sums[:, :LANES] / filled
-        var = jnp.maximum(sums[:, LANES:] / filled - mean * mean, 0.0)
-        scale = 1.0 / (np.float32(np.sqrt(filled)) * jnp.sqrt(var + EPSILON))
+        scale = scales[rows, :]
         corr = []
         for g in range(2):
             both = dot(u_hi[g, rows, :], bz_two[...])
@@ -443,6 +449,7 @@
         pltpu.VMEM((2, GRID, 8, LANES), F32),
         pltpu.VMEM((3, BOX * BOX, 2 * LANES), BF16),
         pltpu.VMEM((3, BOX * BOX, 2 * LANES), BF16),
+        pltpu.VMEM((BOX * BOX, LANES), F32),
     ]
     _, mask_re, mask_im, tz, _, fwd, _, inv, inv_m, *back = tables()
     return pl.pallas_call(

time: 49.3 us -> 49.7 us (level)
  no operation moved by 1% of the time
where the time goes in v6:
time: 49.7 us; the launch traced here: 49.5 us
  starting transfers between devices  19.7 us (40%)
  Pallas kernels  18.8 us (38%)
  waiting for transfers between devices  7.75 us (16%)
  local copies, waits for them, and re-layouts  1.83 us (4%)
  between operations  1.01 us (2%)
    pallas_call x1, Pallas kernels, kernel_call(): pl.pallas_call(body, out_shape=(out, out), scratch_shapes=scratch, compil...  15.8 us
    ppermute x3, starting transfers between devices, local(): lax.ppermute(mine, 'rot', [(i, (i + s) % rots) for i in range(rots)])  9.29 us
    ppermute x3, waiting for transfers between devices, local(): lax.ppermute(mine, 'rot', [(i, (i + s) % rots) for i in range(rots)])  4.09 us
    ppermute x1, starting transfers between devices, local(): before = lax.ppermute(up, 'tx', shifts(tx, 1))  3.05 us
    pallas_call x2, Pallas kernels, prep_call(): pl.pallas_call(prep, out_shape=jax.ShapeDtypeStruct((2, BOX, GRID, LANES)...  2.96 us
    ppermute x1, starting transfers between devices, local(): after = lax.ppermute(down, 'tx', shifts(tx, -1))  2.78 us
    ppermute x1, starting transfers between devices, local(): low = lax.ppermute(grid[HALF:], 'ty', shifts(ty, 1))  2.6 us
    ppermute x1, starting transfers between devices, local(): high = lax.ppermute(grid[:HALF], 'ty', shifts(ty, -1))  1.92 us
  transfers between devices with their start and end apart: 8, of which 4 were waited for; matrix products, arithmetic and copies ran while one was open for 1% of the time, Pallas kernels for 6%

profile of v6, /device:TPU:56, one launch (start us, length us, event | category | flops | bytes accessed | tf_op | source)
XLA Modules:
  0.0 49.5 jit_solution(14193577534799794116)
XLA Ops:
  0.6 0.0 copy-start.13
  0.6 1.4 %copy.19 = f32[32,32,64]{2,0,1:T(8,128)S(1)} copy(f32[32,32,64]{2,1,0:T(8,128)} %param.15) | data formatting | bytes 524288 | tf_op args[0]
  2.1 0.1 pad_maximum_fusion.1
  2.2 0.0 copy-done.13
  2.3 5.5 %collective-permute-start.6 = (f32[1,32,1024]{2,1,0:T(8,128)S(1)}, f32[1,32,1024]{2,1,0:T(8,128)S(1)}, u32[]{:S(2)}, u32[]{:S(2)}) collective-permute-start(f32[1,32,1024]{2,1,0:T(8,128)S(1)} %get-tuple-element.19), channel_id=1, source_target_pairs={{0,192},{64,0},{128,64},{192,128},{1,193},{65,1},{129,65},{193,129... | collective-permute-start | bytes 393224 | tf_op jit(solution)/shard_map/ppermute | solution.py:410
  7.8 1.4 %collective-permute-start.5 = (f32[1,32,1024]{2,1,0:T(8,128)S(1)}, f32[1,32,1024]{2,1,0:T(8,128)S(1)}, u32[]{:S(2)}, u32[]{:S(2)}) collective-permute-start(f32[1,32,1024]{2,1,0:T(8,128)S(1)} %get-tuple-element.19), channel_id=1, source_target_pairs={{0,128},{64,192},{128,0},{192,64},{1,129},{65,193},{129,1},{193,65... | collective-permute-start | bytes 393224 | tf_op jit(solution)/shard_map/ppermute | solution.py:410
  9.2 2.4 %collective-permute-start.4 = (f32[1,32,1024]{2,1,0:T(8,128)S(1)}, f32[1,32,1024]{2,1,0:T(8,128)S(1)}, u32[]{:S(2)}, u32[]{:S(2)}) collective-permute-start(f32[1,32,1024]{2,1,0:T(8,128)S(1)} %get-tuple-element.19), channel_id=1, source_target_pairs={{0,64},{64,128},{128,192},{192,0},{1,65},{65,129},{129,193},{193,1... | collective-permute-start | bytes 393224 | tf_op jit(solution)/shard_map/ppermute | solution.py:410
  11.6 3.0 %collective-permute-start = (f32[16,16,128]{2,1,0:T(8,128)S(1)}, f32[16,16,128]{2,1,0:T(8,128)S(1)}, u32[]{:S(2)}, u32[]{:S(2)}) collective-permute-start(f32[16,16,128]{2,1,0:T(8,128)S(1)} %get-tuple-element.5), channel_id=1, source_target_pairs={{0,4},{4,8},{8,12},{12,16},{16,20},{20,24},{24,28},{28,32},{32,36}... | collective-permute-start | bytes 393224 | tf_op jit(solution)/shard_map/ppermute | solution.py:405
  14.6 2.8 %collective-permute-start.1 = (f32[16,16,128]{2,1,0:T(8,128)S(1)}, f32[16,16,128]{2,1,0:T(8,128)S(1)}, u32[]{:S(2)}, u32[]{:S(2)}) collective-permute-start(f32[16,16,128]{2,1,0:T(8,128)S(1)} %get-tuple-element.6), channel_id=1, source_target_pairs={{4,0},{8,4},{12,8},{16,12},{20,16},{24,20},{28,24},{32,28},{36,32}... | collective-permute-start | bytes 393224 | tf_op jit(solution)/shard_map/ppermute | solution.py:406
  17.5 0.0 copy-start.2
  17.5 0.0 copy-start.7
  17.5 0.0 copy-start.12
  17.5 0.0 collective-permute-done.6
  17.5 3.6 %collective-permute-done.5 = f32[1,32,1024]{2,1,0:T(8,128)S(1)} collective-permute-done((f32[1,32,1024]{2,1,0:T(8,128)S(1)}, f32[1,32,1024]{2,1,0:T(8,128)S(1)}, u32[]{:S(2)}, u32[]{:S(2)}) %collective-permute-start.5) | collective-permute-done | bytes 131104 | tf_op jit(solution)/shard_map/ppermute | solution.py:410
  21.1 0.5 %collective-permute-done.4 = f32[1,32,1024]{2,1,0:T(8,128)S(1)} collective-permute-done((f32[1,32,1024]{2,1,0:T(8,128)S(1)}, f32[1,32,1024]{2,1,0:T(8,128)S(1)}, u32[]{:S(2)}, u32[]{:S(2)}) %collective-permute-start.4) | collective-permute-done | bytes 131104 | tf_op jit(solution)/shard_map/ppermute | solution.py:410
  21.6 0.1 collective-permute-start.7
  21.7 0.0 collective-permute-done
  21.7 0.1 fusion.3
  21.8 1.8 %collective-permute-done.1 = f32[16,16,128]{2,1,0:T(8,128)S(1)} collective-permute-done((f32[16,16,128]{2,1,0:T(8,128)S(1)}, f32[16,16,128]{2,1,0:T(8,128)S(1)}, u32[]{:S(2)}, u32[]{:S(2)}) %collective-permute-start.1) | collective-permute-done | bytes 131104 | tf_op jit(solution)/shard_map/ppermute | solution.py:406
  23.6 0.1 fusion.4
  23.7 0.2 maximum_maximum_fusion.own_ref
  24.0 1.9 %collective-permute-start.3 = (f32[16,32,128]{2,1,0:T(8,128)S(1)}, f32[16,32,128]{2,1,0:T(8,128)S(1)}, u32[]{:S(2)}, u32[]{:S(2)}) collective-permute-start(f32[16,32,128]{2,1,0:T(8,128)S(1)} %get-tuple-element.8), channel_id=1, source_target_pairs={{1,0},{2,1},{3,2},{5,4},{6,5},{7,6},{9,8},{10,9},{11,10},{13,12},{... | collective-permute-start | bytes 786440 | tf_op jit(solution)/shard_map/ppermute | solution.py:422
  25.9 2.6 %collective-permute-start.2 = (f32[16,32,128]{2,1,0:T(8,128)S(1)}, f32[16,32,128]{2,1,0:T(8,128)S(1)}, u32[]{:S(2)}, u32[]{:S(2)}) collective-permute-start(f32[16,32,128]{2,1,0:T(8,128)S(1)} %get-tuple-element.9), channel_id=1, source_target_pairs={{0,1},{1,2},{2,3},{4,5},{5,6},{6,7},{8,9},{9,10},{10,11},{12,13},{... | collective-permute-start | bytes 786440 | tf_op jit(solution)/shard_map/ppermute | solution.py:421
  28.5 0.0 copy-done.2
  28.5 0.0 copy-done.7
  28.5 0.0 copy-done.12
  28.5 1.5 %prep.2.kern_a = f32[2,32,64,128]{3,2,1,0:T(8,128)S(1)} custom-call(f32[32,1024]{1,0:T(8,128)S(1)} %get-tuple-element.21.refs_0_, f32[32,1024]{1,0:T(8,128)S(1)} %get-tuple-element.20.refs_1_, f32[32,1024]{1,0:T(8,128)S(1)} %bitcast.18, f32[32,1024]{1,0:T(8,128)S(1)} %bitcast.17, f32[32,1024]{1,0:T(8,128)S(1)} %copy-done.7, bf16[768,512]{1,0:T(8,128)(2,1)S(1)} %copy-done.2, ...), custom_call_target="tpu_custom_call" | custom-call | flops 2000000000 | bytes 4000000 | tf_op jit(solution)/shard_map/prep/pallas_call | solution.py:430
  30.0 0.0 collective-permute-done.7
  30.1 0.0 copy-start
  30.1 0.0 copy-start.1
  30.1 0.0 copy-start.3
  30.1 0.0 copy-start.4
  30.1 0.0 copy-start.5
  30.1 0.0 copy-start.6
  30.1 0.0 copy-start.8
  30.1 0.0 copy-start.9
  30.2 0.0 copy-start.10
  30.2 0.0 copy-start.11
  30.2 1.5 %prep.3.kern_b = f32[2,32,64,128]{3,2,1,0:T(8,128)S(1)} custom-call(f32[32,1024]{1,0:T(8,128)S(1)} %bitcast.16, f32[32,1024]{1,0:T(8,128)S(1)} %get-tuple-element.18.refs_1_, f32[32,1024]{1,0:T(8,128)S(1)} %get-tuple-element.17.refs_2_, f32[32,1024]{1,0:T(8,128)S(1)} %get-tuple-element.16.refs_3_, f32[32,1024]{1,0:T(8,128)S(1)} %copy-done.7, ...), custom_call_target="tpu_custom_call" | custom-call | flops 2000000000 | bytes 4000000 | tf_op jit(solution)/shard_map/prep/pallas_call | solution.py:430
  31.7 0.0 collective-permute-done.3.after_ref
  31.7 1.9 %collective-permute-done.2.before_ref = f32[16,32,128]{2,1,0:T(8,128)S(1)} collective-permute-done((f32[16,32,128]{2,1,0:T(8,128)S(1)}, f32[16,32,128]{2,1,0:T(8,128)S(1)}, u32[]{:S(2)}, u32[]{:S(2)}) %collective-permute-start.2) | collective-permute-done | bytes 262176 | tf_op jit(solution)/shard_map/ppermute | solution.py:421
  33.6 0.0 copy-done
  33.6 0.0 copy-done.1
  33.6 0.0 copy-done.3
  33.6 0.0 copy-done.4
  33.6 0.0 copy-done.5
  33.6 0.0 copy-done.6
  33.7 15.8 %scores.1 = (f32[32,1024]{1,0:T(8,128)}, f32[32,1024]{1,0:T(8,128)}) custom-call(f32[32,32,128]{2,1,0:T(8,128)S(1)} %maximum_maximum_fusion.own_ref, f32[16,32,128]{2,1,0:T(8,128)S(1)} %collective-permute-done.2.before_ref, f32[16,32,128]{2,1,0:T(8,128)S(1)} %collective-permute-done.3.after_ref, f32[2,32,64,128]{3,2,1,0:T(8,128)S(1)} %prep.2.kern_a, ...), custom_call_target="tpu_custom_call" | custom-call | flops 10000000000 | bytes 10000000 | tf_op jit(solution)/shard_map/scores/pallas_call | solution.py:455
  (10 shorter events, 0.2 us)
Async XLA Ops:
  0.6 1.6 %copy-start.13 = (f32[2,32,1024]{2,1,0:T(8,128)S(1)}, f32[2,32,1024]{2,1,0:T(8,128)}, u32[]{:S(2)}) copy-start(f32[2,32,1024]{2,1,0:T(8,128)} %param.16) | copy-start | bytes 786436
  2.3 15.2 %collective-permute-start.6 = (f32[1,32,1024]{2,1,0:T(8,128)S(1)}, f32[1,32,1024]{2,1,0:T(8,128)S(1)}, u32[]{:S(2)}, u32[]{:S(2)}) collective-permute-start(f32[1,32,1024]{2,1,0:T(8,128)S(1)} %get-tuple-element.19), channel_id=1, source_target_pairs={{0,192},{64,0},{128,64},{192,128},{1,193},{65,1},{129,65},{193,129... | collective-permute-start | bytes 393224 | tf_op jit(solution)/shard_map/ppermute | solution.py:410
  7.8 13.3 %collective-permute-start.5 = (f32[1,32,1024]{2,1,0:T(8,128)S(1)}, f32[1,32,1024]{2,1,0:T(8,128)S(1)}, u32[]{:S(2)}, u32[]{:S(2)}) collective-permute-start(f32[1,32,1024]{2,1,0:T(8,128)S(1)} %get-tuple-element.19), channel_id=1, source_target_pairs={{0,128},{64,192},{128,0},{192,64},{1,129},{65,193},{129,1},{193,65... | collective-permute-start | bytes 393224 | tf_op jit(solution)/shard_map/ppermute | solution.py:410
  9.2 12.4 %collective-permute-start.4 = (f32[1,32,1024]{2,1,0:T(8,128)S(1)}, f32[1,32,1024]{2,1,0:T(8,128)S(1)}, u32[]{:S(2)}, u32[]{:S(2)}) collective-permute-start(f32[1,32,1024]{2,1,0:T(8,128)S(1)} %get-tuple-element.19), channel_id=1, source_target_pairs={{0,64},{64,128},{128,192},{192,0},{1,65},{65,129},{129,193},{193,1... | collective-permute-start | bytes 393224 | tf_op jit(solution)/shard_map/ppermute | solution.py:410
  11.6 10.2 %collective-permute-start = (f32[16,16,128]{2,1,0:T(8,128)S(1)}, f32[16,16,128]{2,1,0:T(8,128)S(1)}, u32[]{:S(2)}, u32[]{:S(2)}) collective-permute-start(f32[16,16,128]{2,1,0:T(8,128)S(1)} %get-tuple-element.5), channel_id=1, source_target_pairs={{0,4},{4,8},{8,12},{12,16},{16,20},{20,24},{24,28},{28,32},{32,36}... | collective-permute-start | bytes 393224 | tf_op jit(solution)/shard_map/ppermute | solution.py:405
  14.6 9.0 %collective-permute-start.1 = (f32[16,16,128]{2,1,0:T(8,128)S(1)}, f32[16,16,128]{2,1,0:T(8,128)S(1)}, u32[]{:S(2)}, u32[]{:S(2)}) collective-permute-start(f32[16,16,128]{2,1,0:T(8,128)S(1)} %get-tuple-element.6), channel_id=1, source_target_pairs={{4,0},{8,4},{12,8},{16,12},{20,16},{24,20},{28,24},{32,28},{36,32}... | collective-permute-start | bytes 393224 | tf_op jit(solution)/shard_map/ppermute | solution.py:406
  17.5 11.0 %copy-start.2 = (bf16[768,512]{1,0:T(8,128)(2,1)S(1)}, bf16[768,512]{1,0:T(8,128)(2,1)}, u32[]{:S(2)}) copy-start(bf16[768,512]{1,0:T(8,128)(2,1)} %constant.38.clone.refs_5_) | copy-start | bytes 2359300
  17.5 11.0 %copy-start.7 = (f32[32,1024]{1,0:T(8,128)S(1)}, f32[32,1024]{1,0:T(8,128)}, u32[]{:S(2)}) copy-start(f32[32,1024]{1,0:T(8,128)} %constant.37.clone.refs_4_) | copy-start | bytes 393220
  17.5 11.0 %copy-start.12 = (bf16[128,96]{1,0:T(8,128)(2,1)S(1)}, bf16[128,96]{1,0:T(8,128)(2,1)}, u32[]{:S(2)}) copy-start(bf16[128,96]{1,0:T(8,128)(2,1)} %constant.39.clone.refs_6_) | copy-start | bytes 73732
  21.6 8.4 %collective-permute-start.7 = (f32[3,32,1024]{2,1,0:T(8,128)S(1)}, f32[3,32,1024]{2,1,0:T(8,128)S(1)}, u32[]{:S(2)}, u32[]{:S(2)}) collective-permute-start(f32[3,32,1024]{2,1,0:T(8,128)S(1)} %pad_maximum_fusion), channel_id=1, source_target_pairs={{0,1},{1,0},{2,3},{3,2},{4,5},{5,4},{6,7},{7,6},{8,9},{9,8},{10,11... | collective-permute-start | bytes 1179656 | tf_op jit(solution)/shard_map/ppermute | solution.py:412
  24.0 7.7 %collective-permute-start.3 = (f32[16,32,128]{2,1,0:T(8,128)S(1)}, f32[16,32,128]{2,1,0:T(8,128)S(1)}, u32[]{:S(2)}, u32[]{:S(2)}) collective-permute-start(f32[16,32,128]{2,1,0:T(8,128)S(1)} %get-tuple-element.8), channel_id=1, source_target_pairs={{1,0},{2,1},{3,2},{5,4},{6,5},{7,6},{9,8},{10,9},{11,10},{13,12},{... | collective-permute-start | bytes 786440 | tf_op jit(solution)/shard_map/ppermute | solution.py:422
  25.9 7.7 %collective-permute-start.2 = (f32[16,32,128]{2,1,0:T(8,128)S(1)}, f32[16,32,128]{2,1,0:T(8,128)S(1)}, u32[]{:S(2)}, u32[]{:S(2)}) collective-permute-start(f32[16,32,128]{2,1,0:T(8,128)S(1)} %get-tuple-element.9), channel_id=1, source_target_pairs={{0,1},{1,2},{2,3},{4,5},{5,6},{6,7},{8,9},{9,10},{10,11},{12,13},{... | collective-permute-start | bytes 786440 | tf_op jit(solution)/shard_map/ppermute | solution.py:421
  30.1 3.5 %copy-start = (f32[64,32,128]{2,1,0:T(8,128)S(1)}, f32[64,32,128]{2,1,0:T(8,128)}, u32[]{:S(2)}) copy-start(f32[64,32,128]{2,1,0:T(8,128)} %constant.41.clone.mask_im) | copy-start | bytes 3145732
  30.1 3.5 %copy-start.1 = (f32[64,32,128]{2,1,0:T(8,128)S(1)}, f32[64,32,128]{2,1,0:T(8,128)}, u32[]{:S(2)}) copy-start(f32[64,32,128]{2,1,0:T(8,128)} %constant.40.clone.mask_re) | copy-start | bytes 3145732
  30.1 3.5 %copy-start.3 = (bf16[768,256]{1,0:T(8,128)(2,1)S(1)}, bf16[768,256]{1,0:T(8,128)(2,1)}, u32[]{:S(2)}) copy-start(bf16[768,256]{1,0:T(8,128)(2,1)} %constant.48.clone.bm_ref) | copy-start | bytes 1179652
  30.1 3.5 %copy-start.4 = (bf16[384,256]{1,0:T(8,128)(2,1)S(1)}, bf16[384,256]{1,0:T(8,128)(2,1)}, u32[]{:S(2)}) copy-start(bf16[384,256]{1,0:T(8,128)(2,1)} %constant.42.clone.tz_ref) | copy-start | bytes 589828
  30.1 3.5 %copy-start.5 = (bf16[256,256]{1,0:T(8,128)(2,1)S(1)}, bf16[256,256]{1,0:T(8,128)(2,1)}, u32[]{:S(2)}) copy-start(bf16[256,256]{1,0:T(8,128)(2,1)} %constant.49.clone.copies_ref) | copy-start | bytes 393220
  30.1 3.5 %copy-start.6 = (bf16[256,256]{1,0:T(8,128)(2,1)S(1)}, bf16[256,256]{1,0:T(8,128)(2,1)}, u32[]{:S(2)}) copy-start(bf16[256,256]{1,0:T(8,128)(2,1)} %constant.46.clone.bz_two) | copy-start | bytes 393220
  30.1 3.5 %copy-start.8 = (bf16[256,128]{1,0:T(8,128)(2,1)S(1)}, bf16[256,128]{1,0:T(8,128)(2,1)}, u32[]{:S(2)}) copy-start(bf16[256,128]{1,0:T(8,128)(2,1)} %constant.47.clone.bz_hi) | copy-start | bytes 196612
  30.1 3.5 %copy-start.9 = (bf16[128,96]{1,0:T(8,128)(2,1)S(1)}, bf16[128,96]{1,0:T(8,128)(2,1)}, u32[]{:S(2)}) copy-start(bf16[128,96]{1,0:T(8,128)(2,1)} %constant.45.clone.inv_m_ref) | copy-start | bytes 73732
  30.2 3.5 %copy-start.10 = (bf16[64,192]{1,0:T(8,128)(2,1)S(1)}, bf16[64,192]{1,0:T(8,128)(2,1)}, u32[]{:S(2)}) copy-start(bf16[64,192]{1,0:T(8,128)(2,1)} %constant.44.clone.inv_ref) | copy-start | bytes 73732
  30.2 3.5 %copy-start.11 = (bf16[64,192]{1,0:T(8,128)(2,1)S(1)}, bf16[64,192]{1,0:T(8,128)(2,1)}, u32[]{:S(2)}) copy-start(bf16[64,192]{1,0:T(8,128)(2,1)} %constant.43.clone.fwd_ref) | copy-start | bytes 73732
